TPU v7x, 512 devices: a whole 4x8x8 slice. The times are simulated.
512 devices in a mesh: dp: 8 (over y), expert: 64 (over z, x, core).
Axes of the slice: x: 4, y: 8, z: 8, core: 2. Of those that a mesh axis runs over, the one named last changes fastest.
Arguments:
- tokens: bfloat16 [65536, 4096], P(('dp', 'expert')), may hold values from -6 to 6
- routes: int32 [65536, 8], P(('dp', 'expert')), may hold values from 0 to 63, all different within a row; in each aligned block of 128 rows (0 to 127, 128 to 255, ...) at most 20 rows name the same one
- mix_weights: float32 [65536, 8], P(('dp', 'expert')), may hold values from 0.05 to 0.45
- gate_up: bfloat16 [64, 512, 1024], P('expert'), may hold values from -0.25 to 0.25
- down: bfloat16 [64, 512, 512], P('expert'), may hold values from -0.25 to 0.25
- w_in: bfloat16 [4096, 512], P(('dp', 'expert')), may hold values from -0.09375 to 0.09375
- grad_combined: bfloat16 [65536, 512], P(('dp', 'expert')), may hold values from -6 to 6
Outputs:
- combined: bfloat16 [65536, 512], P(('dp', 'expert'))
- grad_tokens: bfloat16 [65536, 4096], P(('dp', 'expert'))
- grad_w_in: float32 [4096, 512], P(('dp', 'expert'))
Inputs may be any that keep to these rules, and one draw needn't show every extreme that they name: `routes`: each row names 8 different experts. Among the rows of one device no expert is named more than 20 times, and in every draw some expert is named exactly 20 times by some device's rows.
All inputs are finite; a program needn't handle non-finite values.
Results may differ from a plain program's by a relative error of at most 0.0085.
Values may be sent and summed in bfloat16 or wider, within the bound.
No kernel may reach another device: no remote copies, remote signals or barrier semaphores. Data moves between devices by JAX's collectives and lax.ppermute only.
A program may use at most 64 MiB of HBM per device.

v0:
```python
import jax
import jax.numpy as jnp
from jax import lax
from jax.sharding import PartitionSpec as P


def shards(tokens, routes, mix_weights, gate_up, down, w_in, grad_combined):
    rows = tokens.shape[0]
    top = routes.shape[1]
    n_devices = lax.axis_size("expert")
    local = gate_up.shape[0]
    experts = n_devices * local
    latent_w = w_in.shape[1]
    hidden = down.shape[1]
    capacity = rows * top // experts + rows * top // (4 * experts)
    whole = lax.all_gather(w_in, ("dp", "expert"), axis=0, tiled=True)
    latent32 = jnp.dot(tokens, whole, preferred_element_type=jnp.float32)
    latent = latent32.astype(jnp.bfloat16)
    flat = routes.reshape(-1)
    onehot = (flat[:, None] == jnp.arange(experts, dtype=jnp.int32)[None, :]).astype(jnp.int32)
    rank = jnp.sum((jnp.cumsum(onehot, axis=0) - onehot) * onehot, axis=1)
    slots = flat * capacity + rank
    repeated = jnp.repeat(latent, top, axis=0)
    outgoing = jnp.zeros((experts * capacity, latent_w), jnp.bfloat16).at[slots].set(repeated)
    outgoing = outgoing.reshape(n_devices, local, capacity, latent_w)
    pre = jnp.einsum(
        "necl,elf->necf",
        lax.all_to_all(outgoing, "expert", split_axis=0, concat_axis=0, tiled=True),
        gate_up,
        preferred_element_type=jnp.float32,
    )
    gate = pre[..., :hidden]
    upper = pre[..., hidden:]
    act = (jax.nn.silu(gate) * upper).astype(jnp.bfloat16)
    outputs = jnp.einsum("necf,efl->necl", act, down, preferred_element_type=jnp.float32).astype(
        jnp.bfloat16
    )
    returned = lax.all_to_all(outputs, "expert", split_axis=0, concat_axis=0, tiled=True)
    returned, gate, upper = (returned, gate, upper)
    picked = returned.reshape(experts * capacity, latent_w)[slots].reshape(rows, top, latent_w)
    combined = jnp.sum(mix_weights[..., None] * picked.astype(jnp.float32), axis=1).astype(
        jnp.bfloat16
    )
    grad_slots = (mix_weights[..., None] * grad_combined[:, None, :].astype(jnp.float32)).astype(
        jnp.bfloat16
    )
    grad_send = (
        jnp.zeros((experts * capacity, latent_w), jnp.bfloat16)
        .at[slots]
        .set(grad_slots.reshape(rows * top, latent_w))
    )
    grad_send = grad_send.reshape(n_devices, local, capacity, latent_w)
    grad_recv = lax.all_to_all(grad_send, "expert", split_axis=0, concat_axis=0, tiled=True)
    grad_act = jnp.einsum("necl,efl->necf", grad_recv, down, preferred_element_type=jnp.float32)
    sigma = jax.nn.sigmoid(gate)
    grad_gate = grad_act * upper * sigma * (1.0 + gate * (1.0 - sigma))
    grad_up = grad_act * (gate * sigma)
    grad_pre = jnp.concatenate([grad_gate, grad_up], axis=-1).astype(jnp.bfloat16)
    grad_rows = jnp.einsum(
        "necf,elf->necl", grad_pre, gate_up, preferred_element_type=jnp.float32
    ).astype(jnp.bfloat16)
    grad_back = lax.all_to_all(grad_rows, "expert", split_axis=0, concat_axis=0, tiled=True)
    grad_picked = grad_back.reshape(experts * capacity, latent_w)[slots].reshape(
        rows, top, latent_w
    )
    grad_latent = jnp.sum(grad_picked.astype(jnp.float32), axis=1).astype(jnp.bfloat16)
    grad_tokens32 = lax.dot_general(
        grad_latent, whole, (((1,), (1,)), ((), ())), preferred_element_type=jnp.float32
    )
    grad_tokens = grad_tokens32.astype(jnp.bfloat16)
    feature_block = lax.all_to_all(tokens, "dp", split_axis=1, concat_axis=0, tiled=True)
    group_grads = lax.all_gather(grad_latent, "dp", axis=0, tiled=True)
    grad_w_in = (
        lax.psum_scatter(
            lax.dot_general(
                feature_block,
                group_grads,
                (((0,), (0,)), ((), ())),
                preferred_element_type=jnp.float32,
            ),
            "expert",
            scatter_dimension=0,
            tiled=True,
        )
        / rows
    )
    return (combined, grad_tokens, grad_w_in)


def solution(mesh):
    in_specs = (
        P(("dp", "expert"), None),
        P(("dp", "expert"), None),
        P(("dp", "expert"), None),
        P("expert", None, None),
        P("expert", None, None),
        P(("dp", "expert"), None),
        P(("dp", "expert"), None),
    )
    out_specs = (P(("dp", "expert"), None), P(("dp", "expert"), None), P(("dp", "expert"), None))
    return jax.shard_map(shards, mesh=mesh, in_specs=in_specs, out_specs=out_specs, check_vma=False)
```

profile of v0, /device:TPU:1, one launch (start us, length us, event | category | flops | bytes accessed | tf_op | source)
XLA Modules:
  0.0 533.5 jit_solution(5990607224384122413)
XLA Ops:
  7.2 0.7 all-gather.3.cloned.1.call-update
  7.9 0.8 copy.40
  8.7 0.1 eq.29
  8.9 18.0 %reduce-window.6 = s32[64,8,128]{2,1,0:T(8,128)S(1)} reduce-window(s32[64,8,128]{2,1,0:T(8,128)S(1)} %fusion.44, s32[]{:T(128)} %constant.6.clone.1), window={size=1x1x128 pad=0_0x0_0x127_0}, to_apply=%region_0.0 | reduce-window | flops 8323072 | bytes 524292 | tf_op jit(solution)/shard_map/reduce-window
  26.9 0.1 slice.20
  27.1 0.1 copy.42
  27.3 0.7 broadcast_multiply_fusion
  28.0 0.1 copy.39
  28.1 0.1 mul.71
  28.2 0.8 copy.38
  29.0 0.1 mul.76
  29.2 0.1 broadcast_add_fusion
  29.4 5.9 %scatter_custom_fusion.1 = bf16[1280,512]{1,0:T(8,128)(2,1)S(1)} fusion(s32[1024]{0:T(1024)S(1)} %bitcast.120, f32[128,512]{1,0:T(8,128)S(1)} %convert_element_type.74, f32[1024]{0:T(1024)S(1)} %mul.76, bf16[]{:T(256)} %constant.7.clone.1), kind=kCustom, calls=%fused_computation.37 | custom fusion | flops 1048576 | bytes 1576962 | tf_op jit(solution)/shard_map/scatter | solution.py:50
  35.3 1.3 reshape.127
  36.6 15.1 %all-to-all-start.2 = ((bf16[64,1,20,512]{3,2,1,0:T(8,128)(2,1)}), bf16[64,1,20,512]{3,2,1,0:T(8,128)(2,1)}, u32[]{:S(2)}, u32[]{:S(2)}) async-start(bf16[64,1,20,512]{3,2,1,0:T(8,128)(2,1)} %bitcast.22), calls=%async_computation.2 | async-start | bytes 3145728 | tf_op jit(solution)/shard_map/all_to_all | solution.py:53
  51.7 88.8 %all-gather.3.cloned.1.call-done = bf16[4096,512]{1,0:T(8,128)(2,1)} async-done(((bf16[8,512]{1,0:T(8,128)(2,1)}), bf16[4096,512]{1,0:T(8,128)(2,1)}) %all-gather.3.cloned.1.call-update) | async-done | bytes 4194320 | tf_op jit(solution)/shard_map/all_gather | solution.py:16
  140.5 2.9 convolution_convert_fusion.2
  143.4 5.5 %scatter_custom_fusion = bf16[1280,512]{1,0:T(8,128)(2,1)S(1)} fusion(s32[1024]{0:T(1024)S(1)} %bitcast.121, bf16[]{:T(256)} %constant.7.clone.1, bf16[128,512]{1,0:T(8,128)(2,1)S(1)} %convolution_convert_fusion.2), kind=kCustom, calls=%fused_computation.41 | custom fusion | bytes 1441794 | tf_op jit(solution)/shard_map/scatter | solution.py:24
  148.9 1.3 reshape.121
  150.2 7.5 %all-to-all-start = ((bf16[64,1,20,512]{3,2,1,0:T(8,128)(2,1)}), bf16[64,1,20,512]{3,2,1,0:T(8,128)(2,1)S(1)}, u32[]{:S(2)}, u32[]{:S(2)}) async-start(bf16[64,1,20,512]{3,2,1,0:T(8,128)(2,1)} %bitcast.5), calls=%async_computation | async-start | bytes 3145728 | tf_op jit(solution)/shard_map/all_to_all | solution.py:28
  157.7 2.3 copy.51
  160.0 36.7 %all-to-all-done = bf16[64,1,20,512]{3,2,1,0:T(8,128)(2,1)S(1)} async-done(((bf16[64,1,20,512]{3,2,1,0:T(8,128)(2,1)}), bf16[64,1,20,512]{3,2,1,0:T(8,128)(2,1)S(1)}, u32[]{:S(2)}, u32[]{:S(2)}) %all-to-all-start) | async-done | bytes 1310752 | tf_op jit(solution)/shard_map/all_to_all | solution.py:28
  196.7 4.5 all-to-all-start.4
  201.2 1.6 convolution_bitcast_fusion
  202.8 4.6 fusion.26
  207.4 1.6 fusion.15
  208.9 1.9 copy.50
  210.8 19.7 %all-to-all-done.4 = bf16[128,8,512]{0,2,1:T(8,128)(2,1)} async-done(((bf16[128,8,512]{0,2,1:T(8,128)(2,1)}), bf16[128,8,512]{0,2,1:T(8,128)(2,1)}, u32[]{:S(2)}, u32[]{:S(2)}) %all-to-all-start.4) | async-done | bytes 1048608 | tf_op jit(solution)/shard_map/all_to_all | solution.py:71
  230.5 6.2 %all-to-all-start.3 = ((bf16[64,1,20,512]{3,2,1,0:T(8,128)(2,1)}), bf16[64,1,20,512]{3,2,1,0:T(8,128)(2,1)S(1)}, u32[]{:S(2)}, u32[]{:S(2)}) async-start(bf16[64,1,20,512]{3,2,1,0:T(8,128)(2,1)} %copy.50), calls=%async_computation.3 | async-start | bytes 3145728 | tf_op jit(solution)/shard_map/all_to_all | solution.py:62
  236.7 3.4 fusion.14
  240.1 1.9 copy.46
  242.0 33.7 %all-to-all-done.3 = bf16[64,1,20,512]{3,2,1,0:T(8,128)(2,1)S(1)} async-done(((bf16[64,1,20,512]{3,2,1,0:T(8,128)(2,1)}), bf16[64,1,20,512]{3,2,1,0:T(8,128)(2,1)S(1)}, u32[]{:S(2)}, u32[]{:S(2)}) %all-to-all-start.3) | async-done | bytes 1310752 | tf_op jit(solution)/shard_map/all_to_all | solution.py:62
  275.7 6.6 %all-to-all-start.1 = ((bf16[64,1,20,512]{3,2,1,0:T(8,128)(2,1)}), bf16[64,1,20,512]{3,2,1,0:T(8,128)(2,1)}, u32[]{:S(2)}, u32[]{:S(2)}) async-start(bf16[64,1,20,512]{3,2,1,0:T(8,128)(2,1)} %copy.46), calls=%async_computation.1 | async-start | bytes 3145728 | tf_op jit(solution)/shard_map/all_to_all | solution.py:38
  282.4 2.3 reshape.129
  284.7 4.0 gather_fusion.1
  288.7 1.3 bitcast_reduce_fusion
  290.0 0.3 all-reduce.3.cloned.1.call-start
  290.3 1.3 dynamic-slice
  292.2 2.3 copy.52
  294.5 26.8 %all-to-all-done.1 = bf16[64,1,20,512]{3,2,1,0:T(8,128)(2,1)} async-done(((bf16[64,1,20,512]{3,2,1,0:T(8,128)(2,1)}), bf16[64,1,20,512]{3,2,1,0:T(8,128)(2,1)}, u32[]{:S(2)}, u32[]{:S(2)}) %all-to-all-start.1) | async-done | bytes 1310752 | tf_op jit(solution)/shard_map/all_to_all | solution.py:38
  321.3 2.3 reshape.126
  323.6 4.0 gather_fusion
  327.6 3.2 convolution_bitcast_fusion.1
  330.8 1.3 fusion.9
  332.2 4.6 convolution_convert_fusion
  336.8 188.4 %all-reduce.3.cloned.1.call-done = f32[512,512]{0,1:T(8,128)} async-done(((f32[512,512]{0,1:T(8,128)}), f32[512,512]{0,1:T(8,128)}) %all-reduce.3.cloned.1.call-update) | async-done | bytes 1048592
  525.2 1.1 dynamic-slice_multiply_fusion
  526.3 0.7 copy.53
  (29 shorter events, 0.5 us)
Async XLA Ops:
  7.2 194.0 %copy-start = (bf16[1,512,1024]{2,1,0:T(8,128)(2,1)S(1)}, bf16[1,512,1024]{2,1,0:T(8,128)(2,1)}, u32[]{:S(2)}) copy-start(bf16[1,512,1024]{2,1,0:T(8,128)(2,1)} %param.10) | copy-start | bytes 3145732
  7.2 21.9 %copy-start.5 = (bf16[128,512]{1,0:T(8,128)(2,1)S(1)}, bf16[128,512]{1,0:T(8,128)(2,1)}, u32[]{:S(2)}) copy-start(bf16[128,512]{1,0:T(8,128)(2,1)} %param.13) | copy-start | bytes 393220
  7.2 133.3 %all-gather.3.cloned.1.call-start = ((), (), s32[]{:S(2)}) async-start(), calls=%async_computation.5 | async-start | bytes 4202496 | tf_op jit(solution)/shard_map/all_gather | solution.py:16
  36.6 103.9 %copy-start.3 = (bf16[128,4096]{1,0:T(8,128)(2,1)S(1)}, bf16[128,4096]{1,0:T(8,128)(2,1)}, u32[]{:S(2)}) copy-start(bf16[128,4096]{1,0:T(8,128)(2,1)} %param.7) | copy-start | bytes 3145732
  36.6 113.6 %all-to-all-start.2 = ((bf16[64,1,20,512]{3,2,1,0:T(8,128)(2,1)}), bf16[64,1,20,512]{3,2,1,0:T(8,128)(2,1)}, u32[]{:S(2)}, u32[]{:S(2)}) async-start(bf16[64,1,20,512]{3,2,1,0:T(8,128)(2,1)} %bitcast.22), calls=%async_computation.2 | async-start | bytes 3145728 | tf_op jit(solution)/shard_map/all_to_all | solution.py:53
  150.2 46.5 %all-to-all-start = ((bf16[64,1,20,512]{3,2,1,0:T(8,128)(2,1)}), bf16[64,1,20,512]{3,2,1,0:T(8,128)(2,1)S(1)}, u32[]{:S(2)}, u32[]{:S(2)}) async-start(bf16[64,1,20,512]{3,2,1,0:T(8,128)(2,1)} %bitcast.5), calls=%async_computation | async-start | bytes 3145728 | tf_op jit(solution)/shard_map/all_to_all | solution.py:28
  196.7 33.8 %all-to-all-start.4 = ((bf16[128,8,512]{0,2,1:T(8,128)(2,1)}), bf16[128,8,512]{0,2,1:T(8,128)(2,1)}, u32[]{:S(2)}, u32[]{:S(2)}) async-start(bf16[128,8,512]{0,2,1:T(8,128)(2,1)} %bitcast.115), calls=%async_computation.4 | async-start | bytes 2097152 | tf_op jit(solution)/shard_map/all_to_all | solution.py:71
  201.2 1.6 copy-start.6
  202.8 4.6 copy-start.2
  230.5 45.2 %all-to-all-start.3 = ((bf16[64,1,20,512]{3,2,1,0:T(8,128)(2,1)}), bf16[64,1,20,512]{3,2,1,0:T(8,128)(2,1)S(1)}, u32[]{:S(2)}, u32[]{:S(2)}) async-start(bf16[64,1,20,512]{3,2,1,0:T(8,128)(2,1)} %copy.50), calls=%async_computation.3 | async-start | bytes 3145728 | tf_op jit(solution)/shard_map/all_to_all | solution.py:62
  275.7 6.7 %copy-start.1 = (bf16[64,1,20,512]{3,2,1,0:T(8,128)(2,1)}, bf16[64,1,20,512]{3,2,1,0:T(8,128)(2,1)S(1)}, u32[]{:S(2)}) copy-start(bf16[64,1,20,512]{3,2,1,0:T(8,128)(2,1)S(1)} %all-to-all-done.3) | copy-start | bytes 3932164
  275.7 45.6 %all-to-all-start.1 = ((bf16[64,1,20,512]{3,2,1,0:T(8,128)(2,1)}), bf16[64,1,20,512]{3,2,1,0:T(8,128)(2,1)}, u32[]{:S(2)}, u32[]{:S(2)}) async-start(bf16[64,1,20,512]{3,2,1,0:T(8,128)(2,1)} %copy.46), calls=%async_computation.1 | async-start | bytes 3145728 | tf_op jit(solution)/shard_map/all_to_all | solution.py:38
  282.3 45.2 %all-gather.5.cloned.1.call-start = ((), (), s32[]{:S(2)}) async-start(), calls=%async_computation.6 | async-start | bytes 1179648 | tf_op jit(solution)/shard_map/all_gather | solution.py:72
  290.0 235.1 %all-reduce.3.cloned.1.call-start = ((), (), s32[]{:S(2)}) async-start(), calls=%async_computation.7 | async-start | bytes 2097152
  330.8 1.4 copy-start.4
Sparse Core Ops, SparseCore 0:
  12.2 128.2 all-gather.2
  290.2 32.7 all-gather.4
  331.0 194.1 all-reduce.2
where the time goes:
time: 536 us; the launch traced here: 534 us
  waiting for transfers between devices  395 us (74%)
  starting transfers between devices  40.3 us (8%)
  local copies, waits for them, and re-layouts  33.3 us (6%)
  other arithmetic  28.6 us (5%)
  matrix products  21.9 us (4%)
  between operations  14.7 us (3%)
    unnamed x4, waiting for transfers between devices  189 us
    all_gather x1, waiting for transfers between devices, shards(): whole = lax.all_gather(w_in, ('dp', 'expert'), axis=0, tiled=True)  88.8 us
    all_to_all x1, waiting for transfers between devices, shards(): lax.all_to_all(outgoing, 'expert', split_axis=0, concat_axis=0, tiled=True)  36.7 us
    all_to_all x1, waiting for transfers between devices, shards(): lax.all_to_all(grad_rows, 'expert', split_axis=0, concat_axis=0, tiled=True)  33.7 us
    all_to_all x1, waiting for transfers between devices, shards(): lax.all_to_all(outputs, 'expert', split_axis=0, concat_axis=0, tiled=True)  26.8 us
    all_to_all x1, waiting for transfers between devices, shards(): lax.all_to_all(tokens, 'dp', split_axis=1, concat_axis=0, tiled=True)  19.7 us
    another operation x3, other arithmetic  18.2 us
    all_to_all x1, starting transfers between devices, shards(): lax.all_to_all(grad_send, 'expert', split_axis=0, concat_axis=0, tiled=True)  15.1 us
  transfers between devices with their start and end apart: 8, of which 6 were waited for; matrix products, arithmetic and copies ran while one was open for 15% of the time, Pallas kernels for 0%

commit v1 on v0

v1 whole, which is shorter than its diff:
```python
import jax
import jax.numpy as jnp
from jax import lax
from jax.sharding import Mesh, PartitionSpec as P

BF = jnp.bfloat16
F32 = jnp.float32
XC = ("x", "c")
YZ = ("dp", "z")
ZX = ("z", "x")
CAP = 20
MAIN = 16
PAIR = 2 * CAP


def mm(a, b, dims=((1,), (0,))):
    return lax.dot_general(a, b, (dims, ((), ())), preferred_element_type=F32)


def after(x, *deps):
    return lax.optimization_barrier((x,) + deps)[0]


def swap_core(x):
    return lax.ppermute(x, "c", [(0, 1), (1, 0)])


def column_order(tokens):
    rows = tokens.shape[0]
    a = lax.broadcasted_iota(jnp.int32, (1024, 1024), 0)
    b = lax.broadcasted_iota(jnp.int32, (1024, 1024), 1)
    y, z, xc, i = a // 512, (a // 64) % 8, (a // 8) % 8, a % 8
    pick = (xc * 128 + y * 64 + z * 8 + i == b).astype(BF)
    parts = [mm(tokens[:, p * 1024 : (p + 1) * 1024], pick).astype(BF) for p in range(4)]
    return jnp.concatenate(
        [parts[p][:, xc * 128 : (xc + 1) * 128] for xc in range(8) for p in range(4)], axis=1
    )


def shards(tokens, routes, mix_weights, gate_up, down, w_in, grad_combined):
    rows = tokens.shape[0]
    gate_up, down = gate_up[0], down[0]
    hidden = down.shape[0]
    experts = 64
    slots = experts * CAP

    w_part = lax.all_to_all(
        jnp.broadcast_to(w_in[None], (64,) + w_in.shape), YZ, split_axis=0, concat_axis=0, tiled=True
    ).reshape(512, 512)
    w_all = lax.all_gather(w_part, XC, axis=0, tiled=True)

    gate_up2, down2 = swap_core(gate_up), swap_core(down)

    core = lax.axis_index("c")
    r = lax.broadcasted_iota(jnp.int32, (experts, slots), 1)
    q = r % PAIR
    other = jnp.where(q < 2 * MAIN, q // MAIN, (q - 2 * MAIN) // (CAP - MAIN))
    spread = (
        lax.broadcasted_iota(jnp.int32, (experts, slots), 0) == (r // PAIR) * 2 + (core + other) % 2
    )
    q1 = lax.broadcasted_iota(jnp.int32, (rows, slots), 1) % PAIR
    place = jnp.where(q1 < 2 * MAIN, q1 % MAIN, MAIN + (q1 - 2 * MAIN) % (CAP - MAIN))
    hit = routes[:, :, None] == lax.broadcasted_iota(jnp.int32, (1, 1, experts), 2)
    named = jnp.any(hit, axis=1)
    weight = jnp.sum(jnp.where(hit, mix_weights[:, :, None], 0.0), axis=1)
    below = (
        lax.broadcasted_iota(jnp.int32, (rows, rows), 0)
        > lax.broadcasted_iota(jnp.int32, (rows, rows), 1)
    ).astype(BF)
    rank = mm(below, named.astype(BF))
    code = jnp.where(named, rank, -1.0).astype(BF)
    send = mm(code, spread.astype(BF)) == place.astype(F32)
    onehot = send.astype(BF)
    weight_hi = weight.astype(BF)
    weight_mid = (weight - weight_hi.astype(F32)).astype(BF)
    weight_lo = (weight - weight_hi.astype(F32) - weight_mid.astype(F32)).astype(BF)
    spread = spread.astype(BF)
    at_slot = mm(weight_hi, spread) + mm(weight_mid, spread) + mm(weight_lo, spread)
    weight_slot = jnp.where(send, at_slot, 0.0)
    slot_weight = jnp.sum(weight_slot, axis=0)
    mix_hi = weight_slot.astype(BF)
    mix_lo = (weight_slot - mix_hi.astype(F32)).astype(BF)

    picked = mm(onehot, grad_combined, ((0,), (0,)))
    grad_send = (slot_weight[:, None] * picked).astype(BF).reshape(32, PAIR, 512)
    grad_send = after(grad_send, w_part)
    grad_recv = lax.all_to_all(grad_send, ZX, split_axis=0, concat_axis=0, tiled=True)

    ordered = column_order(tokens)
    latent = mm(ordered, w_all).astype(BF)
    out_send = mm(onehot, latent, ((0,), (0,))).astype(BF).reshape(32, PAIR, 512)
    out_send = after(out_send, grad_recv)
    recv = lax.all_to_all(out_send, ZX, split_axis=0, concat_axis=0, tiled=True)

    feats = ordered.reshape(rows, 8, 512).transpose(1, 0, 2)
    feats = after(feats, recv)
    feature_block = lax.all_to_all(feats, XC, split_axis=0, concat_axis=0, tiled=True).reshape(
        8 * rows, 512
    )

    def split(x):
        tail = x[:, 2 * MAIN :].reshape(256, 512)
        return (
            jnp.concatenate([x[:, :MAIN].reshape(512, 512), tail]),
            jnp.concatenate([x[:, MAIN : 2 * MAIN].reshape(512, 512), tail]),
        )

    def join(a, b):
        own = (lax.broadcasted_iota(jnp.int32, (256, 1), 0) % 8) < 4
        tail = jnp.where(own, a[512:], b[512:])
        return jnp.concatenate(
            [a[:512].reshape(32, MAIN, 512), b[:512].reshape(32, MAIN, 512), tail.reshape(32, 8, 512)],
            axis=1,
        )

    def expert(x, g, w_up, w_down):
        pre = mm(x, w_up)
        gate, upper = pre[:, :hidden], pre[:, hidden:]
        sigma = jax.nn.sigmoid(gate)
        act = (gate * sigma * upper).astype(BF)
        grad_act = mm(g, w_down, ((1,), (1,)))
        grad_gate = grad_act * upper * sigma * (1.0 + gate * (1.0 - sigma))
        grad_up = grad_act * (gate * sigma)
        grad_pre = jnp.concatenate([grad_gate, grad_up], axis=-1).astype(BF)
        grad_rows = mm(grad_pre, w_up, ((1,), (1,))).astype(BF)
        out = mm(act, w_down).astype(BF)
        return out, grad_rows

    x1, x2 = split(recv)
    g1, g2 = split(grad_recv)
    o1, b1 = expert(x1, g1, gate_up, down)
    o2, b2 = expert(x2, g2, gate_up2, down2)
    grad_rows = after(join(b1, b2), feature_block)
    grad_back = lax.all_to_all(grad_rows, ZX, split_axis=0, concat_axis=0, tiled=True)
    outputs = after(join(o1, o2), grad_back)
    returned = lax.all_to_all(outputs, ZX, split_axis=0, concat_axis=0, tiled=True)

    grad_latent = mm(onehot, grad_back.reshape(slots, 512)).astype(BF)
    group_grads = lax.all_gather(grad_latent, XC, axis=0, tiled=True)
    part = mm(feature_block, group_grads, ((0,), (0,))).astype(BF).reshape(64, 8, 512)
    part = after(part, returned)
    parts = lax.all_to_all(part, YZ, split_axis=0, concat_axis=0, tiled=True)
    grad_w_in = jnp.sum(parts.astype(F32), axis=0) / rows

    w_natural = w_all.reshape(8, 64, 8, 512).transpose(1, 0, 2, 3).reshape(4096, 512)
    grad_tokens = mm(grad_latent, w_natural, ((1,), (1,))).astype(BF)
    flat = returned.reshape(slots, 512)
    combined = (mm(mix_hi, flat) + mm(mix_lo, flat)).astype(BF)
    return combined, grad_tokens, grad_w_in


def solution(mesh):
    split = Mesh(mesh.devices.reshape(8, 8, 4, 2), ("dp", "z", "x", "c"))
    every = P(("dp", "z", "x", "c"), None)
    each = P(("z", "x", "c"), None, None)
    return jax.shard_map(
        shards,
        mesh=split,
        in_specs=(every, every, every, each, each, every, every),
        out_specs=(every, every, every),
        check_vma=False,
    )
```

time: 536 us -> 280 us (0.52)
  waiting for transfers between devices: 395 us -> 134 us
  starting transfers between devices: 40.3 us -> 67.4 us
  other arithmetic: 28.6 us -> 5.8 us
  local copies, waits for them, and re-layouts: 33.3 us -> 22.3 us
  matrix products: 21.9 us -> 32.2 us
    unnamed x4 -> x2, waiting for transfers between devices: 189 us -> 0.03 us
    all_to_all x5 -> x7, waiting for transfers between devices: 117 us -> 72.7 us  [the longest x1 29 us: shards(): lax.all_to_all(grad_rows, ZX, split_axis=0, concat_axis=0, tiled=True)]
    all_gather x2, waiting for transfers between devices: 88.8 us -> 61.1 us  [the longest x1 32.1 us: shards(): group_grads = lax.all_gather(grad_latent, XC, axis=0, tiled=True)]
    all_to_all x5 -> x7, starting transfers between devices: 40 us -> 62.9 us  [the longest x1 17.3 us: shards(): lax.all_to_all(jnp.broadcast_to(w_in[None], (64,) + w_in.shape), YZ, spli...]
    another operation x3 -> x0, other arithmetic: 18.2 us -> none
    dot_general x7 -> x23, matrix products: 21.9 us -> 32.2 us  [mm(): return lax.dot_general(a, b, (dims, ((), ())), preferred_element_type=F32)]
    gather x2 -> x0, local copies, waits for them, and re-layouts: 7.93 us -> none  [the longest x1 3.97 us: shards(): grad_back.reshape(experts * capacity, latent_w)[slots]]
    scatter x1 -> x0, other arithmetic: 5.86 us -> none  [shards(): grad_send = jnp.zeros((experts * capacity, latent_w), jnp.bfloat16).at[sl...]
  transfers between devices with their start and end apart: 8 -> 11, of which waited for: 6 -> 6; matrix products, arithmetic and copies ran while one was open for 15% -> 20% of each run, Pallas kernels for 0% -> 0%
where the time goes in v1:
time: 280 us; the launch traced here: 276 us
  waiting for transfers between devices  134 us (48%)
  starting transfers between devices  67.4 us (24%)
  matrix products  32.2 us (12%)
  local copies, waits for them, and re-layouts  22.3 us (8%)
  between operations  14.7 us (5%)
  other arithmetic  5.8 us (2%)
    dot_general x23, matrix products, mm(): return lax.dot_general(a, b, (dims, ((), ())), preferred_element_type=F32)  32.2 us
    all_gather x1, waiting for transfers between devices, shards(): group_grads = lax.all_gather(grad_latent, XC, axis=0, tiled=True)  32.1 us
    all_gather x1, waiting for transfers between devices, shards(): w_all = lax.all_gather(w_part, XC, axis=0, tiled=True)  29 us
    all_to_all x1, waiting for transfers between devices, shards(): lax.all_to_all(grad_rows, ZX, split_axis=0, concat_axis=0, tiled=True)  29 us
    all_to_all x1, waiting for transfers between devices, shards(): recv = lax.all_to_all(out_send, ZX, split_axis=0, concat_axis=0, tiled=True)  23.9 us
    all_to_all x1, starting transfers between devices, shards(): lax.all_to_all(jnp.broadcast_to(w_in[None], (64,) + w_in.shape), YZ, spli...  17.3 us
    all_to_all x1, starting transfers between devices, shards(): parts = lax.all_to_all(part, YZ, split_axis=0, concat_axis=0, tiled=True)  12 us
    unnamed x71, local copies, waits for them, and re-layouts  10.6 us
  transfers between devices with their start and end apart: 11, of which 6 were waited for; matrix products, arithmetic and copies ran while one was open for 20% of the time, Pallas kernels for 0%

profile of v1, /device:TPU:1, one launch (start us, length us, event | category | flops | bytes accessed | tf_op | source)
XLA Modules:
  0.0 276.2 jit_solution(17235346221900609043)
XLA Ops:
  7.2 1.6 broadcast_in_dim.46
  8.7 17.3 %all-to-all-start = ((bf16[64,8,512]{2,1,0:T(8,128)(2,1)}), bf16[64,8,512]{2,1,0:T(8,128)(2,1)S(1)}, u32[]{:S(2)}, u32[]{:S(2)}) async-start(bf16[64,8,512]{2,1,0:T(8,128)(2,1)} %broadcast_in_dim.46), calls=%async_computation | async-start | bytes 1048576 | tf_op jit(solution)/shard_map/all_to_all | solution.py:47
  26.1 2.5 fusion.8
  31.1 1.7 fusion.31
  32.9 9.5 %all-to-all-done = bf16[64,8,512]{2,1,0:T(8,128)(2,1)S(1)} async-done(((bf16[64,8,512]{2,1,0:T(8,128)(2,1)}), bf16[64,8,512]{2,1,0:T(8,128)(2,1)S(1)}, u32[]{:S(2)}, u32[]{:S(2)}) %all-to-all-start) | async-done | bytes 524320 | tf_op jit(solution)/shard_map/all_to_all | solution.py:47
  42.4 0.8 copy-done.2
  44.9 1.6 fusion.9
  46.6 8.1 %all-to-all-start.1 = ((bf16[32,40,512]{2,1,0:T(8,128)(2,1)}), bf16[32,40,512]{2,1,0:T(8,128)(2,1)S(1)}, u32[]{:S(2)}, u32[]{:S(2)}) async-start(bf16[32,40,512]{2,1,0:T(8,128)(2,1)} %bitcast.6), calls=%async_computation.1 | async-start | bytes 2621440 | tf_op jit(solution)/shard_map/all_to_all | solution.py:87
  54.7 0.8 constant_dynamic-update-slice_fusion.9
  55.5 0.8 constant_dynamic-update-slice_fusion.8
  56.3 0.8 constant_dynamic-update-slice_fusion.7
  57.0 0.8 constant_dynamic-update-slice_fusion.6
  57.8 0.8 constant_dynamic-update-slice_fusion.5
  58.6 0.8 constant_dynamic-update-slice_fusion.4
  61.6 0.8 constant_dynamic-update-slice_fusion
  62.4 29.0 %all-gather.3.cloned.1.call-done = bf16[4096,512]{1,0:T(8,128)(2,1)} async-done(((bf16[512,512]{1,0:T(8,128)(2,1)}), bf16[4096,512]{1,0:T(8,128)(2,1)}) %all-gather.3.cloned.1.call-update) | async-done | bytes 4194320 | tf_op jit(solution)/shard_map/all_gather | solution.py:50
  91.4 4.5 %convolution_convert_fusion.1 = bf16[1280,512]{1,0:T(8,128)(2,1)} fusion(pred[128,1280]{1,0:T(32,128)(4,1)S(1)} %convolution_compare_fusion, bf16[128,4096]{0,1:T(8,128)(2,1)S(1)} %constant_dynamic-update-slice_fusion, bf16[4096,512]{1,0:T(8,128)(2,1)} %all-gather.3.cloned.1.call-done), kind=kOutput, calls=%fused_computation.22 | convolution fusion | flops 705363968 | bytes 6717440 | tf_op jit(solution)/shard_map/dot_general | solution.py:17
  95.9 7.4 %all-to-all-start.2 = ((bf16[32,40,512]{2,1,0:T(8,128)(2,1)}), bf16[32,40,512]{2,1,0:T(8,128)(2,1)S(1)}, u32[]{:S(2)}, u32[]{:S(2)}) async-start(bf16[32,40,512]{2,1,0:T(8,128)(2,1)} %bitcast.5), calls=%async_computation.2 | async-start | bytes 2621440 | tf_op jit(solution)/shard_map/all_to_all | solution.py:93
  103.3 2.5 collective-permute-start
  105.8 1.9 collective-permute-start.1
  107.7 2.3 copy.35
  110.7 1.2 fusion.120
  111.9 23.9 %all-to-all-done.2 = bf16[32,40,512]{2,1,0:T(8,128)(2,1)S(1)} async-done(((bf16[32,40,512]{2,1,0:T(8,128)(2,1)}), bf16[32,40,512]{2,1,0:T(8,128)(2,1)S(1)}, u32[]{:S(2)}, u32[]{:S(2)}) %all-to-all-start.2) | async-done | bytes 1310752 | tf_op jit(solution)/shard_map/all_to_all | solution.py:93
  135.8 6.7 %all-to-all-start.3 = ((bf16[8,128,512]{2,1,0:T(8,128)(2,1)}), bf16[8,128,512]{2,1,0:T(8,128)(2,1)S(1)}, u32[]{:S(2)}, u32[]{:S(2)}) async-start(bf16[8,128,512]{2,1,0:T(8,128)(2,1)} %bitcast.78), calls=%async_computation.3 | async-start | bytes 2097152 | tf_op jit(solution)/shard_map/all_to_all | solution.py:97
  142.6 1.1 copy-done.5
  143.7 1.0 fusion.39
  145.0 1.1 multiply_convert_fusion.3
  146.1 2.2 fusion.40
  148.4 1.0 fusion.24
  150.4 2.2 multiply_convert_fusion.1
  152.6 2.2 fusion.21
  154.9 1.6 convolution_convert_fusion.2
  156.7 0.8 copy-done.8
  157.5 1.2 pad_maximum_fusion.1
  158.7 5.5 %all-to-all-start.4 = ((bf16[32,40,512]{2,1,0:T(8,128)(2,1)}), bf16[32,40,512]{2,1,0:T(8,128)(2,1)S(1)}, u32[]{:S(2)}, u32[]{:S(2)}) async-start(bf16[32,40,512]{2,1,0:T(8,128)(2,1)} %pad_maximum_fusion.1), calls=%async_computation.4 | async-start | bytes 2621440 | tf_op jit(solution)/shard_map/all_to_all | solution.py:134
  164.2 1.1 slice.252
  165.3 1.1 slice.256
  166.4 1.2 pad_maximum_fusion
  167.6 29.0 %all-to-all-done.4 = bf16[32,40,512]{2,1,0:T(8,128)(2,1)S(1)} async-done(((bf16[32,40,512]{2,1,0:T(8,128)(2,1)}), bf16[32,40,512]{2,1,0:T(8,128)(2,1)S(1)}, u32[]{:S(2)}, u32[]{:S(2)}) %all-to-all-start.4) | async-done | bytes 1310752 | tf_op jit(solution)/shard_map/all_to_all | solution.py:134
  196.6 5.8 %all-to-all-start.5 = ((bf16[32,40,512]{2,1,0:T(8,128)(2,1)}), bf16[32,40,512]{2,1,0:T(8,128)(2,1)S(1)}, u32[]{:S(2)}, u32[]{:S(2)}) async-start(bf16[32,40,512]{2,1,0:T(8,128)(2,1)} %pad_maximum_fusion), calls=%async_computation.5 | async-start | bytes 2621440 | tf_op jit(solution)/shard_map/all_to_all | solution.py:136
  202.5 1.9 convolution_convert_fusion.10
  204.4 32.1 %all-gather.5.cloned.1.call-done = bf16[1024,512]{1,0:T(8,128)(2,1)} async-done(((bf16[128,512]{1,0:T(8,128)(2,1)}), bf16[1024,512]{1,0:T(8,128)(2,1)}) %all-gather.5.cloned.1.call-update) | async-done | bytes 1048592 | tf_op jit(solution)/shard_map/all_gather | solution.py:139
  236.5 3.1 %fusion.27 = bf16[64,8,512]{2,1,0:T(8,128)(2,1)} fusion(bf16[1024,512]{1,0:T(8,128)(2,1)} %bitcast.87, bf16[1024,512]{1,0:T(8,128)(2,1)} %all-gather.5.cloned.1.call-done), kind=kOutput, calls=%fused_computation.57 | convolution fusion | flops 537133056 | bytes 2621440 | tf_op jit(solution)/shard_map/dot_general | solution.py:17
  239.6 12.0 %all-to-all-start.6 = ((bf16[64,8,512]{2,1,0:T(8,128)(2,1)}), bf16[64,8,512]{2,1,0:T(8,128)(2,1)S(1)}, u32[]{:S(2)}, u32[]{:S(2)}) async-start(bf16[64,8,512]{2,1,0:T(8,128)(2,1)} %fusion.27), calls=%async_computation.6 | async-start | bytes 1048576 | tf_op jit(solution)/shard_map/all_to_all | solution.py:142
  251.7 2.8 %copy.36 = bf16[64,8,8,512]{3,2,1,0:T(8,128)(2,1)S(1)} copy(bf16[64,8,8,512]{3,2,0,1:T(8,128)(2,1)} %bitcast.72) | data formatting | bytes 8388608 | tf_op jit(solution)/shard_map/transpose | solution.py:145
  254.5 2.4 convolution_convert_fusion
  257.3 1.0 fusion.35
  258.3 10.4 %all-to-all-done.6 = bf16[64,8,512]{2,1,0:T(8,128)(2,1)S(1)} async-done(((bf16[64,8,512]{2,1,0:T(8,128)(2,1)}), bf16[64,8,512]{2,1,0:T(8,128)(2,1)S(1)}, u32[]{:S(2)}, u32[]{:S(2)}) %all-to-all-start.6) | async-done | bytes 524320 | tf_op jit(solution)/shard_map/all_to_all | solution.py:142
  (100 shorter events, 9.9 us)
Async XLA Ops:
  7.2 37.8 %copy-start = (bf16[128,512]{1,0:T(8,128)(2,1)S(1)}, bf16[128,512]{1,0:T(8,128)(2,1)}, u32[]{:S(2)}) copy-start(bf16[128,512]{1,0:T(8,128)(2,1)} %param.13) | copy-start | bytes 393220
  8.7 19.9 %copy-start.18 = (bf16[128,4096]{1,0:T(8,128)(2,1)S(1)}, bf16[128,4096]{1,0:T(8,128)(2,1)}, u32[]{:S(2)}) copy-start(bf16[128,4096]{1,0:T(8,128)(2,1)} %param.7) | copy-start | bytes 3145732
  8.7 33.6 %all-to-all-start = ((bf16[64,8,512]{2,1,0:T(8,128)(2,1)}), bf16[64,8,512]{2,1,0:T(8,128)(2,1)S(1)}, u32[]{:S(2)}, u32[]{:S(2)}) async-start(bf16[64,8,512]{2,1,0:T(8,128)(2,1)} %broadcast_in_dim.46), calls=%async_computation | async-start | bytes 1048576 | tf_op jit(solution)/shard_map/all_to_all | solution.py:47
  26.0 65.4 %all-gather.3.cloned.1.call-start = ((), (), s32[]{:S(2)}) async-start(), calls=%async_computation.7 | async-start | bytes 4718592 | tf_op jit(solution)/shard_map/all_gather | solution.py:50
  29.4 14.0 %copy-start.13 = (bf16[128,1024]{0,1:T(8,128)(2,1)}, bf16[128,1024]{0,1:T(8,128)(2,1)S(1)}, u32[]{:S(2)}) copy-start(bf16[128,1024]{0,1:T(8,128)(2,1)S(1)} %fusion.28) | copy-start | bytes 786436
  30.2 13.3 %copy-start.12 = (bf16[128,1024]{0,1:T(8,128)(2,1)}, bf16[128,1024]{0,1:T(8,128)(2,1)S(1)}, u32[]{:S(2)}) copy-start(bf16[128,1024]{0,1:T(8,128)(2,1)S(1)} %fusion.29) | copy-start | bytes 786436
  30.2 0.8 copy-start.16
  30.2 0.9 copy-start.17
  31.0 12.4 %copy-start.11 = (bf16[128,1024]{0,1:T(8,128)(2,1)}, bf16[128,1024]{0,1:T(8,128)(2,1)S(1)}, u32[]{:S(2)}) copy-start(bf16[128,1024]{0,1:T(8,128)(2,1)S(1)} %fusion.30) | copy-start | bytes 786436
  32.9 11.0 %copy-start.14 = (bf16[128,1024]{0,1:T(8,128)(2,1)}, bf16[128,1024]{0,1:T(8,128)(2,1)S(1)}, u32[]{:S(2)}) copy-start(bf16[128,1024]{0,1:T(8,128)(2,1)S(1)} %fusion.31) | copy-start | bytes 786436
  42.4 0.8 copy-start.2
  44.6 46.8 %copy-start.3 = (pred[128,1280]{1,0:T(32,128)(4,1)}, pred[128,1280]{1,0:T(32,128)(4,1)S(1)}, u32[]{:S(2)}) copy-start(pred[128,1280]{1,0:T(32,128)(4,1)S(1)} %convolution_compare_fusion) | copy-start | bytes 491524
  46.6 49.3 %all-to-all-start.1 = ((bf16[32,40,512]{2,1,0:T(8,128)(2,1)}), bf16[32,40,512]{2,1,0:T(8,128)(2,1)S(1)}, u32[]{:S(2)}, u32[]{:S(2)}) async-start(bf16[32,40,512]{2,1,0:T(8,128)(2,1)} %bitcast.6), calls=%async_computation.1 | async-start | bytes 2621440 | tf_op jit(solution)/shard_map/all_to_all | solution.py:87
  62.4 33.5 %copy-start.1 = (bf16[128,4096]{0,1:T(8,128)(2,1)}, bf16[128,4096]{0,1:T(8,128)(2,1)S(1)}, u32[]{:S(2)}) copy-start(bf16[128,4096]{0,1:T(8,128)(2,1)S(1)} %constant_dynamic-update-slice_fusion) | copy-start | bytes 3145732
  95.9 39.8 %all-to-all-start.2 = ((bf16[32,40,512]{2,1,0:T(8,128)(2,1)}), bf16[32,40,512]{2,1,0:T(8,128)(2,1)S(1)}, u32[]{:S(2)}, u32[]{:S(2)}) async-start(bf16[32,40,512]{2,1,0:T(8,128)(2,1)} %bitcast.5), calls=%async_computation.2 | async-start | bytes 2621440 | tf_op jit(solution)/shard_map/all_to_all | solution.py:93
  103.3 42.8 %collective-permute-start = (bf16[512,1024]{1,0:T(8,128)(2,1)}, bf16[512,1024]{1,0:T(8,128)(2,1)}, u32[]{:S(2)}, u32[]{:S(2)}) collective-permute-start(bf16[512,1024]{1,0:T(8,128)(2,1)} %bitcast.86), channel_id=1, source_target_pairs={{0,1},{1,0},{2,3},{3,2},{4,5},{5,4},{6,7},{7,6},{8,9},{9,8},{10,11... | collective-permute-start | bytes 3145736 | tf_op jit(solution)/shard_map/ppermute | solution.py:25
  105.8 44.2 %collective-permute-start.1 = (bf16[512,512]{1,0:T(8,128)(2,1)}, bf16[512,512]{1,0:T(8,128)(2,1)}, u32[]{:S(2)}, u32[]{:S(2)}) collective-permute-start(bf16[512,512]{1,0:T(8,128)(2,1)} %bitcast.90), channel_id=1, source_target_pairs={{0,1},{1,0},{2,3},{3,2},{4,5},{5,4},{6,7},{7,6},{8,9},{9,8},{10,11... | collective-permute-start | bytes 1572872 | tf_op jit(solution)/shard_map/ppermute | solution.py:25
  135.8 22.9 %all-to-all-start.3 = ((bf16[8,128,512]{2,1,0:T(8,128)(2,1)}), bf16[8,128,512]{2,1,0:T(8,128)(2,1)S(1)}, u32[]{:S(2)}, u32[]{:S(2)}) async-start(bf16[8,128,512]{2,1,0:T(8,128)(2,1)} %bitcast.78), calls=%async_computation.3 | async-start | bytes 2097152 | tf_op jit(solution)/shard_map/all_to_all | solution.py:97
  142.5 1.2 copy-start.5
  143.7 1.0 copy-start.10
  143.7 1.1 copy-start.15
  143.7 1.3 copy-start.19
  149.4 1.0 copy-start.9
  150.0 6.6 %copy-start.7 = (bf16[768,512]{1,0:T(8,128)(2,1)}, bf16[768,512]{1,0:T(8,128)(2,1)S(1)}, u32[]{:S(2)}) copy-start(bf16[768,512]{1,0:T(8,128)(2,1)S(1)} %convolution_convert_fusion.3) | copy-start | bytes 2359300
  156.6 1.0 copy-start.8
  158.7 6.6 %copy-start.6 = (bf16[8,128,512]{2,1,0:T(8,128)(2,1)}, bf16[8,128,512]{2,1,0:T(8,128)(2,1)S(1)}, u32[]{:S(2)}) copy-start(bf16[8,128,512]{2,1,0:T(8,128)(2,1)S(1)} %all-to-all-done.3) | copy-start | bytes 3145732
  158.7 37.9 %all-to-all-start.4 = ((bf16[32,40,512]{2,1,0:T(8,128)(2,1)}), bf16[32,40,512]{2,1,0:T(8,128)(2,1)S(1)}, u32[]{:S(2)}, u32[]{:S(2)}) async-start(bf16[32,40,512]{2,1,0:T(8,128)(2,1)} %pad_maximum_fusion.1), calls=%async_computation.4 | async-start | bytes 2621440 | tf_op jit(solution)/shard_map/all_to_all | solution.py:134
  196.6 43.0 %all-to-all-start.5 = ((bf16[32,40,512]{2,1,0:T(8,128)(2,1)}), bf16[32,40,512]{2,1,0:T(8,128)(2,1)S(1)}, u32[]{:S(2)}, u32[]{:S(2)}) async-start(bf16[32,40,512]{2,1,0:T(8,128)(2,1)} %pad_maximum_fusion), calls=%async_computation.5 | async-start | bytes 2621440 | tf_op jit(solution)/shard_map/all_to_all | solution.py:136
  202.4 34.1 %all-gather.5.cloned.1.call-start = ((), (), s32[]{:S(2)}) async-start(), calls=%async_computation.8 | async-start | bytes 1179648 | tf_op jit(solution)/shard_map/all_gather | solution.py:139
  239.6 29.1 %all-to-all-start.6 = ((bf16[64,8,512]{2,1,0:T(8,128)(2,1)}), bf16[64,8,512]{2,1,0:T(8,128)(2,1)S(1)}, u32[]{:S(2)}, u32[]{:S(2)}) async-start(bf16[64,8,512]{2,1,0:T(8,128)(2,1)} %fusion.27), calls=%async_computation.6 | async-start | bytes 1048576 | tf_op jit(solution)/shard_map/all_to_all | solution.py:142
  251.7 2.8 %copy-start.4 = (bf16[128,512]{1,0:T(8,128)(2,1)S(1)}, bf16[128,512]{1,0:T(8,128)(2,1)}, u32[]{:S(2)}) copy-start(bf16[128,512]{1,0:T(8,128)(2,1)} %convolution_convert_fusion.10) | copy-start | bytes 393220
Sparse Core Ops, SparseCore 0:
  43.3 48.0 all-gather.2
  206.0 30.5 all-gather.4

commit v2 on v1

--- a/solution.py
+++ b/solution.py
@@ -1,6 +1,8 @@
 import jax
 import jax.numpy as jnp
 from jax import lax
+from jax.experimental import pallas as pl
+from jax.experimental.pallas import tpu as pltpu
 from jax.sharding import Mesh, PartitionSpec as P
 
 BF = jnp.bfloat16
@@ -37,10 +39,62 @@
     )
 
 
+def expert_kernel(x_ref, g_ref, up_ref, down_ref, back_ref, out_ref):
+    w_up, w_down = up_ref[0], down_ref[0]
+    x = x_ref[...].reshape(256, 512)
+    g = g_ref[...].reshape(256, 512)
+    pre = mm(x, w_up)
+    grad_act = mm(g, w_down, ((1,), (1,)))
+    gate, upper = pre[:, :512], pre[:, 512:]
+    sigma = jax.nn.sigmoid(gate)
+    soft = gate * sigma
+    act = (soft * upper).astype(BF)
+    grad_gate = (grad_act * upper * sigma * (1.0 + gate * (1.0 - sigma))).astype(BF)
+    grad_up = (grad_act * soft).astype(BF)
+    last = ((1,), (1,))
+    back = mm(grad_gate, w_up[:, :512], last) + mm(grad_up, w_up[:, 512:], last)
+    back = back.astype(BF).reshape(16, 16, 512)
+    out = mm(act, w_down).astype(BF).reshape(16, 16, 512)
+    step = pl.program_id(0)
+
+    @pl.when(step != 3)
+    def _():
+        back_ref[...] = back
+        out_ref[...] = out
+
+    @pl.when(step == 3)
+    def _():
+        keep = (lax.broadcasted_iota(jnp.int32, (16, 16, 512), 1) % 8) < 4
+        back_ref[...] = jnp.where(keep, back_ref[...].astype(F32), back.astype(F32)).astype(BF)
+        out_ref[...] = jnp.where(keep, out_ref[...].astype(F32), out.astype(F32)).astype(BF)
+
+
+def expert_rows(x, g, ups, downs):
+    def block(i):
+        return (0, jnp.where(i == 0, 0, jnp.where(i == 1, 3, jnp.where(i < 4, 2, jnp.where(i == 4, 1, 4)))), 0)
+
+    rows = pl.BlockSpec((16, 16, 512), block)
+    shape = jax.ShapeDtypeStruct((16, 80, 512), BF)
+    back, out = pl.pallas_call(
+        expert_kernel,
+        grid=(6,),
+        in_specs=[
+            rows,
+            rows,
+            pl.BlockSpec((1, 512, 1024), lambda i: (i // 3, 0, 0)),
+            pl.BlockSpec((1, 512, 512), lambda i: (i // 3, 0, 0)),
+        ],
+        out_specs=[rows, rows],
+        out_shape=[shape, shape],
+        compiler_params=pltpu.CompilerParams(vmem_limit_bytes=40 * 1024 * 1024),
+        cost_estimate=pl.CostEstimate(flops=4_800_000_000, bytes_accessed=8_500_000, transcendentals=800_000),
+    )(x.reshape(16, 80, 512), g.reshape(16, 80, 512), ups, downs)
+    return back.reshape(32, PAIR, 512), out.reshape(32, PAIR, 512)
+
+
 def shards(tokens, routes, mix_weights, gate_up, down, w_in, grad_combined):
     rows = tokens.shape[0]
     gate_up, down = gate_up[0], down[0]
-    hidden = down.shape[0]
     experts = 64
     slots = experts * CAP
 
@@ -52,13 +106,14 @@
     gate_up2, down2 = swap_core(gate_up), swap_core(down)
 
     core = lax.axis_index("c")
+    shift = 32 * (lax.axis_index("x") % 2)
     r = lax.broadcasted_iota(jnp.int32, (experts, slots), 1)
-    q = r % PAIR
+    q = (r % PAIR + shift) % PAIR
     other = jnp.where(q < 2 * MAIN, q // MAIN, (q - 2 * MAIN) // (CAP - MAIN))
     spread = (
         lax.broadcasted_iota(jnp.int32, (experts, slots), 0) == (r // PAIR) * 2 + (core + other) % 2
     )
-    q1 = lax.broadcasted_iota(jnp.int32, (rows, slots), 1) % PAIR
+    q1 = (lax.broadcasted_iota(jnp.int32, (rows, slots), 1) % PAIR + shift) % PAIR
     place = jnp.where(q1 < 2 * MAIN, q1 % MAIN, MAIN + (q1 - 2 * MAIN) % (CAP - MAIN))
     hit = routes[:, :, None] == lax.broadcasted_iota(jnp.int32, (1, 1, experts), 2)
     named = jnp.any(hit, axis=1)
@@ -92,52 +147,34 @@
     out_send = after(out_send, grad_recv)
     recv = lax.all_to_all(out_send, ZX, split_axis=0, concat_axis=0, tiled=True)
 
-    feats = ordered.reshape(rows, 8, 512).transpose(1, 0, 2)
-    feats = after(feats, recv)
-    feature_block = lax.all_to_all(feats, XC, split_axis=0, concat_axis=0, tiled=True).reshape(
-        8 * rows, 512
-    )
+    me, other_core = core, 1 - core
+    feats = ordered.reshape(rows, 4, 2, 512).transpose(2, 1, 0, 3)
+    mine = lax.dynamic_index_in_dim(feats, me, 0, keepdims=False)
+    theirs = swap_core(lax.dynamic_index_in_dim(feats, other_core, 0, keepdims=False))
+    both = jnp.stack([mine, theirs], axis=1)
+    at = lax.axis_index("x")
+    blocks = [lax.dynamic_index_in_dim(both, at, 0, keepdims=False)]
+    for d in (1, 2, 3):
+        block = lax.dynamic_index_in_dim(both, (at + d) % 4, 0, keepdims=False)
+        blocks.append(lax.ppermute(block, "x", [(i, (i + d) % 4) for i in range(4)]))
+    blocks = jnp.stack(blocks)
+    feature_block = jnp.stack(
+        [lax.dynamic_index_in_dim(blocks, (at - j) % 4, 0, keepdims=False) for j in range(4)], axis=1
+    ).reshape(2, 4 * rows, 512)
 
-    def split(x):
-        tail = x[:, 2 * MAIN :].reshape(256, 512)
-        return (
-            jnp.concatenate([x[:, :MAIN].reshape(512, 512), tail]),
-            jnp.concatenate([x[:, MAIN : 2 * MAIN].reshape(512, 512), tail]),
-        )
-
-    def join(a, b):
-        own = (lax.broadcasted_iota(jnp.int32, (256, 1), 0) % 8) < 4
-        tail = jnp.where(own, a[512:], b[512:])
-        return jnp.concatenate(
-            [a[:512].reshape(32, MAIN, 512), b[:512].reshape(32, MAIN, 512), tail.reshape(32, 8, 512)],
-            axis=1,
-        )
-
-    def expert(x, g, w_up, w_down):
-        pre = mm(x, w_up)
-        gate, upper = pre[:, :hidden], pre[:, hidden:]
-        sigma = jax.nn.sigmoid(gate)
-        act = (gate * sigma * upper).astype(BF)
-        grad_act = mm(g, w_down, ((1,), (1,)))
-        grad_gate = grad_act * upper * sigma * (1.0 + gate * (1.0 - sigma))
-        grad_up = grad_act * (gate * sigma)
-        grad_pre = jnp.concatenate([grad_gate, grad_up], axis=-1).astype(BF)
-        grad_rows = mm(grad_pre, w_up, ((1,), (1,))).astype(BF)
-        out = mm(act, w_down).astype(BF)
-        return out, grad_rows
-
-    x1, x2 = split(recv)
-    g1, g2 = split(grad_recv)
-    o1, b1 = expert(x1, g1, gate_up, down)
-    o2, b2 = expert(x2, g2, gate_up2, down2)
-    grad_rows = after(join(b1, b2), feature_block)
+    ups = jnp.stack([gate_up, gate_up2])
+    downs = jnp.stack([down, down2])
+    grad_rows, outputs = expert_rows(recv, grad_recv, ups, downs)
     grad_back = lax.all_to_all(grad_rows, ZX, split_axis=0, concat_axis=0, tiled=True)
-    outputs = after(join(o1, o2), grad_back)
+    outputs = after(outputs, grad_back)
     returned = lax.all_to_all(outputs, ZX, split_axis=0, concat_axis=0, tiled=True)
 
     grad_latent = mm(onehot, grad_back.reshape(slots, 512)).astype(BF)
-    group_grads = lax.all_gather(grad_latent, XC, axis=0, tiled=True)
-    part = mm(feature_block, group_grads, ((0,), (0,))).astype(BF).reshape(64, 8, 512)
+    line_grads = lax.all_gather(grad_latent, "x", axis=0, tiled=True)
+    other_grads = swap_core(line_grads)
+    first = ((0,), (0,))
+    part = mm(feature_block[0], line_grads, first) + mm(feature_block[1], other_grads, first)
+    part = part.astype(BF).reshape(64, 8, 512)
     part = after(part, returned)
     parts = lax.all_to_all(part, YZ, split_axis=0, concat_axis=0, tiled=True)
     grad_w_in = jnp.sum(parts.astype(F32), axis=0) / rows

time: 280 us -> 291 us (1.039)
  starting transfers between devices: 67.4 us -> 80.3 us
  matrix products: 32.2 us -> 20.1 us
  waiting for transfers between devices: 134 us -> 123 us
  blocking collectives: 0 us -> 10.2 us
  Pallas kernels: 0 us -> 9.39 us
  other arithmetic: 5.8 us -> 10.2 us
  local copies, waits for them, and re-layouts: 22.3 us -> 19.3 us
    all_gather x1 -> x0, waiting for transfers between devices: 32.1 us -> none  [shards(): group_grads = lax.all_gather(grad_latent, XC, axis=0, tiled=True)]
    ppermute x0 -> x3, waiting for transfers between devices: none -> 14.6 us  [shards(): lax.ppermute(block, 'x', [(i, (i + d) % 4) for i in range(4)])]
    dot_general x23 -> x16, matrix products: 32.2 us -> 20.1 us  [mm(): return lax.dot_general(a, b, (dims, ((), ())), preferred_element_type=F32)]
    ppermute x0 -> x3, starting transfers between devices: none -> 11 us  [shards(): lax.ppermute(block, 'x', [(i, (i + d) % 4) for i in range(4)])]
    all_gather x0 -> x1, blocking collectives: none -> 10.2 us  [shards(): line_grads = lax.all_gather(grad_latent, 'x', axis=0, tiled=True)]
    ppermute x2 -> x4, starting transfers between devices: 4.39 us -> 14.5 us  [swap_core(): return lax.ppermute(x, 'c', [(0, 1), (1, 0)])]
    pallas_call x0 -> x1, Pallas kernels: none -> 9.39 us  [expert_rows(): pl.pallas_call(expert_kernel, grid=(6,), in_specs=[rows, rows, pl.BlockSp...]
    another operation x0 -> x5, other arithmetic: none -> 6.92 us  [the longest x1 2 us: shards(): both = jnp.stack([mine, theirs], axis=1)]
  transfers between devices with their start and end apart: 11 -> 14, of which waited for: 6 -> 10; matrix products, arithmetic and copies ran while one was open for 20% -> 15% of each run, Pallas kernels for 0% -> 0%
where the time goes in v2:
time: 291 us; the launch traced here: 288 us
  waiting for transfers between devices  123 us (42%)
  starting transfers between devices  80.3 us (28%)
  matrix products  20.1 us (7%)
  local copies, waits for them, and re-layouts  19.3 us (7%)
  between operations  14.7 us (5%)
  other arithmetic  10.2 us (4%)
  blocking collectives  10.2 us (4%)
  Pallas kernels  9.39 us (3%)
    all_gather x1, waiting for transfers between devices, shards(): w_all = lax.all_gather(w_part, XC, axis=0, tiled=True)  32.3 us
    all_to_all x1, waiting for transfers between devices, shards(): lax.all_to_all(grad_rows, ZX, split_axis=0, concat_axis=0, tiled=True)  30.5 us
    all_to_all x1, waiting for transfers between devices, shards(): recv = lax.all_to_all(out_send, ZX, split_axis=0, concat_axis=0, tiled=True)  23.7 us
    dot_general x16, matrix products, mm(): return lax.dot_general(a, b, (dims, ((), ())), preferred_element_type=F32)  20.1 us
    all_to_all x1, starting transfers between devices, shards(): lax.all_to_all(jnp.broadcast_to(w_in[None], (64,) + w_in.shape), YZ, spli...  17.1 us
    ppermute x3, waiting for transfers between devices, shards(): lax.ppermute(block, 'x', [(i, (i + d) % 4) for i in range(4)])  14.6 us
    ppermute x4, starting transfers between devices, swap_core(): return lax.ppermute(x, 'c', [(0, 1), (1, 0)])  14.5 us
    ppermute x3, starting transfers between devices, shards(): lax.ppermute(block, 'x', [(i, (i + d) % 4) for i in range(4)])  11 us
  transfers between devices with their start and end apart: 14, of which 10 were waited for; matrix products, arithmetic and copies ran while one was open for 15% of the time, Pallas kernels for 0%

profile of v2, /device:TPU:1, one launch (start us, length us, event | category | flops | bytes accessed | tf_op | source)
XLA Modules:
  0.0 287.8 jit_solution(9353586034596935751)
XLA Ops:
  7.2 1.6 broadcast_in_dim.33
  8.8 17.1 %all-to-all-start = ((bf16[64,8,512]{2,1,0:T(8,128)(2,1)}), bf16[64,8,512]{2,1,0:T(8,128)(2,1)S(1)}, u32[]{:S(2)}, u32[]{:S(2)}) async-start(bf16[64,8,512]{2,1,0:T(8,128)(2,1)} %broadcast_in_dim.33), calls=%async_computation | async-start | bytes 1048576 | tf_op jit(solution)/shard_map/all_to_all | solution.py:101
  26.1 2.5 fusion.8
  28.6 1.9 fusion.15
  32.3 2.4 fusion.16
  34.7 7.6 %all-to-all-done = bf16[64,8,512]{2,1,0:T(8,128)(2,1)S(1)} async-done(((bf16[64,8,512]{2,1,0:T(8,128)(2,1)}), bf16[64,8,512]{2,1,0:T(8,128)(2,1)S(1)}, u32[]{:S(2)}, u32[]{:S(2)}) %all-to-all-start) | async-done | bytes 524320 | tf_op jit(solution)/shard_map/all_to_all | solution.py:101
  44.5 1.2 fusion.86
  45.7 1.7 fusion.9
  47.4 8.1 %all-to-all-start.1 = ((bf16[32,40,512]{2,1,0:T(8,128)(2,1)}), bf16[32,40,512]{2,1,0:T(8,128)(2,1)S(1)}, u32[]{:S(2)}, u32[]{:S(2)}) async-start(bf16[32,40,512]{2,1,0:T(8,128)(2,1)} %bitcast.6), calls=%async_computation.1 | async-start | bytes 2621440 | tf_op jit(solution)/shard_map/all_to_all | solution.py:142
  59.5 32.3 %all-gather.2.cloned.1.call-done = bf16[4096,512]{1,0:T(8,128)(2,1)} async-done(((bf16[512,512]{1,0:T(8,128)(2,1)}), bf16[4096,512]{1,0:T(8,128)(2,1)}) %all-gather.2.cloned.1.call-update) | async-done | bytes 4194320 | tf_op jit(solution)/shard_map/all_gather | solution.py:104
  91.8 4.5 %convolution_convert_fusion.1 = bf16[1280,512]{1,0:T(8,128)(2,1)} fusion(pred[128,1280]{1,0:T(32,128)(4,1)S(1)} %convolution_compare_fusion, bf16[128,4096]{0,1:T(8,128)(2,1)S(1)} %constant_dynamic-update-slice_fusion, bf16[4096,512]{1,0:T(8,128)(2,1)} %all-gather.2.cloned.1.call-done), kind=kOutput, calls=%fused_computation.22 | convolution fusion | flops 705363968 | bytes 6717440 | tf_op jit(solution)/shard_map/dot_general | solution.py:19
  96.3 7.9 %all-to-all-start.2 = ((bf16[32,40,512]{2,1,0:T(8,128)(2,1)}), bf16[32,40,512]{2,1,0:T(8,128)(2,1)}, u32[]{:S(2)}, u32[]{:S(2)}) async-start(bf16[32,40,512]{2,1,0:T(8,128)(2,1)} %bitcast.5), calls=%async_computation.2 | async-start | bytes 2621440 | tf_op jit(solution)/shard_map/all_to_all | solution.py:148
  104.2 2.5 collective-permute-start
  106.7 1.9 collective-permute-start.1
  108.6 1.9 collective-permute-done.1
  110.5 1.1 pad_maximum_fusion.1.down_ref
  111.6 1.4 pad_maximum_fusion.up_ref
  113.0 23.7 %all-to-all-done.2 = bf16[32,40,512]{2,1,0:T(8,128)(2,1)} async-done(((bf16[32,40,512]{2,1,0:T(8,128)(2,1)}), bf16[32,40,512]{2,1,0:T(8,128)(2,1)}, u32[]{:S(2)}, u32[]{:S(2)}) %all-to-all-start.2) | async-done | bytes 1310752 | tf_op jit(solution)/shard_map/all_to_all | solution.py:148
  136.7 1.2 copy-done.2
  137.9 9.4 %shard_map.94 = (bf16[16,80,512]{2,1,0:T(8,128)(2,1)S(1)}, bf16[16,80,512]{2,1,0:T(8,128)(2,1)}) custom-call(bf16[16,80,512]{2,1,0:T(8,128)(2,1)} %bitcast.7.x_ref, bf16[16,80,512]{2,1,0:T(8,128)(2,1)S(1)} %bitcast.74, bf16[2,512,1024]{2,1,0:T(8,128)(2,1)S(1)} %pad_maximum_fusion.up_ref, bf16[2,512,512]{2,1,0:T(8,128)(2,1)S(1)} %copy-done.2), custom_call_target="tpu_custom_call" | custom-call | flops 4800000000 | bytes 8500000 | tf_op jit(solution)/shard_map/pallas_call | solution.py:78
  147.3 1.1 copy-done.1
  148.4 5.7 %all-to-all-start.3 = ((bf16[32,40,512]{2,1,0:T(8,128)(2,1)}), bf16[32,40,512]{2,1,0:T(8,128)(2,1)S(1)}, u32[]{:S(2)}, u32[]{:S(2)}) async-start(bf16[32,40,512]{2,1,0:T(8,128)(2,1)} %bitcast.75), calls=%async_computation.3 | async-start | bytes 2621440 | tf_op jit(solution)/shard_map/all_to_all | solution.py:168
  154.2 30.5 %all-to-all-done.3 = bf16[32,40,512]{2,1,0:T(8,128)(2,1)S(1)} async-done(((bf16[32,40,512]{2,1,0:T(8,128)(2,1)}), bf16[32,40,512]{2,1,0:T(8,128)(2,1)S(1)}, u32[]{:S(2)}, u32[]{:S(2)}) %all-to-all-start.3) | async-done | bytes 1310752 | tf_op jit(solution)/shard_map/all_to_all | solution.py:168
  184.6 7.2 %all-to-all-start.4 = ((bf16[32,40,512]{2,1,0:T(8,128)(2,1)}), bf16[32,40,512]{2,1,0:T(8,128)(2,1)S(1)}, u32[]{:S(2)}, u32[]{:S(2)}) async-start(bf16[32,40,512]{2,1,0:T(8,128)(2,1)} %bitcast.13), calls=%async_computation.4 | async-start | bytes 2621440 | tf_op jit(solution)/shard_map/all_to_all | solution.py:170
  191.8 2.1 dynamic-slice_bitcast_fusion
  193.9 4.4 %collective-permute-start.2 = (bf16[4,128,512]{1,2,0:T(8,128)(2,1)}, bf16[4,128,512]{1,2,0:T(8,128)(2,1)}, u32[]{:S(2)}, u32[]{:S(2)}) collective-permute-start(bf16[4,128,512]{1,2,0:T(8,128)(2,1)} %get-tuple-element.25), channel_id=1, source_target_pairs={{0,1},{1,0},{2,3},{3,2},{4,5},{5,4},{6,7},{7,6},{8,9},{9,8},{10,11... | collective-permute-start | bytes 1572872 | tf_op jit(solution)/shard_map/ppermute | solution.py:27
  198.4 1.8 collective-permute-done.2
  200.2 2.0 fusion.46
  202.2 3.4 %collective-permute-start.3 = (bf16[2,128,512]{1,2,0:T(8,128)(2,1)}, bf16[2,128,512]{1,2,0:T(8,128)(2,1)S(1)}, u32[]{:S(2)}, u32[]{:S(2)}) collective-permute-start(bf16[2,128,512]{1,2,0:T(8,128)(2,1)} %get-tuple-element.22), channel_id=1, source_target_pairs={{0,2},{2,4},{4,6},{6,0},{1,3},{3,5},{5,7},{7,1},{8,10},{10,12},{12... | collective-permute-start | bytes 786440 | tf_op jit(solution)/shard_map/ppermute | solution.py:159
  205.6 4.5 %collective-permute-start.4 = (bf16[2,128,512]{1,2,0:T(8,128)(2,1)}, bf16[2,128,512]{1,2,0:T(8,128)(2,1)}, u32[]{:S(2)}, u32[]{:S(2)}) collective-permute-start(bf16[2,128,512]{1,2,0:T(8,128)(2,1)} %get-tuple-element.23), channel_id=1, source_target_pairs={{0,4},{2,6},{4,0},{6,2},{1,5},{3,7},{5,1},{7,3},{8,12},{10,14},{12... | collective-permute-start | bytes 786440 | tf_op jit(solution)/shard_map/ppermute | solution.py:159
  210.1 3.1 %collective-permute-start.5 = (bf16[2,128,512]{1,2,0:T(8,128)(2,1)}, bf16[2,128,512]{1,2,0:T(8,128)(2,1)}, u32[]{:S(2)}, u32[]{:S(2)}) collective-permute-start(bf16[2,128,512]{1,2,0:T(8,128)(2,1)} %get-tuple-element.24), channel_id=1, source_target_pairs={{0,6},{2,0},{4,2},{6,4},{1,7},{3,1},{5,3},{7,5},{8,14},{10,8},{12,... | collective-permute-start | bytes 786440 | tf_op jit(solution)/shard_map/ppermute | solution.py:159
  213.3 4.6 %collective-permute-done.3 = bf16[2,128,512]{1,2,0:T(8,128)(2,1)S(1)} collective-permute-done((bf16[2,128,512]{1,2,0:T(8,128)(2,1)}, bf16[2,128,512]{1,2,0:T(8,128)(2,1)S(1)}, u32[]{:S(2)}, u32[]{:S(2)}) %collective-permute-start.3) | collective-permute-done | bytes 262176 | tf_op jit(solution)/shard_map/ppermute | solution.py:159
  218.0 10.0 %collective-permute-done.4 = bf16[2,128,512]{1,2,0:T(8,128)(2,1)} collective-permute-done((bf16[2,128,512]{1,2,0:T(8,128)(2,1)}, bf16[2,128,512]{1,2,0:T(8,128)(2,1)}, u32[]{:S(2)}, u32[]{:S(2)}) %collective-permute-start.4) | collective-permute-done | bytes 262176 | tf_op jit(solution)/shard_map/ppermute | solution.py:159
  227.9 1.2 pad_maximum_fusion.2
  229.1 0.9 constant_dynamic-slice_fusion.3
  230.0 1.8 copy.30
  231.8 1.8 copy.33
  233.6 0.9 copy.32
  234.6 1.2 pad_maximum_fusion.3
  236.2 10.2 %all_gather.7 = bf16[512,512]{1,0:T(8,128)(2,1)S(1)} all-gather(bf16[128,512]{1,0:T(8,128)(2,1)S(1)} %convolution_convert_fusion.7), channel_id=1, replica_groups=mesh['dp'=8,'z'=8,'x'=4,'c'=2] {'x'}, dimensions={0}, use_global_device_ids=true | all-gather | bytes 655360 | tf_op jit(solution)/shard_map/all_gather | solution.py:173
  246.4 5.6 %collective-permute-start.6 = (bf16[512,512]{1,0:T(8,128)(2,1)S(1)}, bf16[512,512]{1,0:T(8,128)(2,1)S(1)}, u32[]{:S(2)}, u32[]{:S(2)}) collective-permute-start(bf16[512,512]{1,0:T(8,128)(2,1)S(1)} %all_gather.7), channel_id=1, source_target_pairs={{0,1},{1,0},{2,3},{3,2},{4,5},{5,4},{6,7},{7,6},{8,9},{9,8},{10,11... | collective-permute-start | bytes 1572872 | tf_op jit(solution)/shard_map/ppermute | solution.py:27
  252.6 1.0 collective-permute-done.6
  253.6 1.3 fusion.12
  254.9 8.7 %all-to-all-start.5 = ((bf16[64,8,512]{2,1,0:T(8,128)(2,1)}), bf16[64,8,512]{2,1,0:T(8,128)(2,1)S(1)}, u32[]{:S(2)}, u32[]{:S(2)}) async-start(bf16[64,8,512]{2,1,0:T(8,128)(2,1)} %fusion.12), calls=%async_computation.5 | async-start | bytes 1048576 | tf_op jit(solution)/shard_map/all_to_all | solution.py:179
  263.6 2.8 copy.28
  266.4 2.4 convolution_convert_fusion
  269.2 1.0 fusion.17
  270.2 10.1 %all-to-all-done.5 = bf16[64,8,512]{2,1,0:T(8,128)(2,1)S(1)} async-done(((bf16[64,8,512]{2,1,0:T(8,128)(2,1)}), bf16[64,8,512]{2,1,0:T(8,128)(2,1)S(1)}, u32[]{:S(2)}, u32[]{:S(2)}) %all-to-all-start.5) | async-done | bytes 524320 | tf_op jit(solution)/shard_map/all_to_all | solution.py:179
  (89 shorter events, 9.9 us)
Async XLA Ops:
  7.2 38.6 %copy-start = (bf16[128,512]{1,0:T(8,128)(2,1)S(1)}, bf16[128,512]{1,0:T(8,128)(2,1)}, u32[]{:S(2)}) copy-start(bf16[128,512]{1,0:T(8,128)(2,1)} %param.13) | copy-start | bytes 393220
  7.2 23.3 %copy-start.14 = (bf16[128,4096]{1,0:T(8,128)(2,1)S(1)}, bf16[128,4096]{1,0:T(8,128)(2,1)}, u32[]{:S(2)}) copy-start(bf16[128,4096]{1,0:T(8,128)(2,1)} %param.7) | copy-start | bytes 3145732
  8.8 33.5 %all-to-all-start = ((bf16[64,8,512]{2,1,0:T(8,128)(2,1)}), bf16[64,8,512]{2,1,0:T(8,128)(2,1)S(1)}, u32[]{:S(2)}, u32[]{:S(2)}) async-start(bf16[64,8,512]{2,1,0:T(8,128)(2,1)} %broadcast_in_dim.33), calls=%async_computation | async-start | bytes 1048576 | tf_op jit(solution)/shard_map/all_to_all | solution.py:101
  26.0 65.8 %all-gather.2.cloned.1.call-start = ((), (), s32[]{:S(2)}) async-start(), calls=%async_computation.6 | async-start | bytes 4718592 | tf_op jit(solution)/shard_map/all_gather | solution.py:104
  28.6 2.7 copy-start.5
  30.5 1.6 copy-start.12
  30.5 1.6 copy-start.13
  32.1 11.6 %copy-start.10 = (bf16[128,1024]{0,1:T(8,128)(2,1)}, bf16[128,1024]{0,1:T(8,128)(2,1)S(1)}, u32[]{:S(2)}) copy-start(bf16[128,1024]{0,1:T(8,128)(2,1)S(1)} %fusion.13) | copy-start | bytes 786436
  34.6 9.9 %copy-start.11 = (bf16[128,1024]{0,1:T(8,128)(2,1)}, bf16[128,1024]{0,1:T(8,128)(2,1)S(1)}, u32[]{:S(2)}) copy-start(bf16[128,1024]{0,1:T(8,128)(2,1)S(1)} %fusion.16) | copy-start | bytes 786436
  42.3 0.8 copy-start.6
  44.5 47.3 %copy-start.7 = (pred[128,1280]{1,0:T(32,128)(4,1)}, pred[128,1280]{1,0:T(32,128)(4,1)S(1)}, u32[]{:S(2)}) copy-start(pred[128,1280]{1,0:T(32,128)(4,1)S(1)} %convolution_compare_fusion) | copy-start | bytes 491524
  47.4 48.9 %all-to-all-start.1 = ((bf16[32,40,512]{2,1,0:T(8,128)(2,1)}), bf16[32,40,512]{2,1,0:T(8,128)(2,1)S(1)}, u32[]{:S(2)}, u32[]{:S(2)}) async-start(bf16[32,40,512]{2,1,0:T(8,128)(2,1)} %bitcast.6), calls=%async_computation.1 | async-start | bytes 2621440 | tf_op jit(solution)/shard_map/all_to_all | solution.py:142
  59.5 36.8 %copy-start.3 = (bf16[128,4096]{0,1:T(8,128)(2,1)}, bf16[128,4096]{0,1:T(8,128)(2,1)S(1)}, u32[]{:S(2)}) copy-start(bf16[128,4096]{0,1:T(8,128)(2,1)S(1)} %constant_dynamic-update-slice_fusion) | copy-start | bytes 3145732
  59.5 47.2 %copy-start.9 = (bf16[1,512,512]{2,1,0:T(8,128)(2,1)S(1)}, bf16[1,512,512]{2,1,0:T(8,128)(2,1)}, u32[]{:S(2)}) copy-start(bf16[1,512,512]{2,1,0:T(8,128)(2,1)} %param.11) | copy-start | bytes 1572868
  96.3 40.4 %all-to-all-start.2 = ((bf16[32,40,512]{2,1,0:T(8,128)(2,1)}), bf16[32,40,512]{2,1,0:T(8,128)(2,1)}, u32[]{:S(2)}, u32[]{:S(2)}) async-start(bf16[32,40,512]{2,1,0:T(8,128)(2,1)} %bitcast.5), calls=%async_computation.2 | async-start | bytes 2621440 | tf_op jit(solution)/shard_map/all_to_all | solution.py:148
  104.2 7.3 %collective-permute-start = (bf16[512,1024]{1,0:T(8,128)(2,1)}, bf16[512,1024]{1,0:T(8,128)(2,1)S(1)}, u32[]{:S(2)}, u32[]{:S(2)}) collective-permute-start(bf16[512,1024]{1,0:T(8,128)(2,1)} %bitcast.85), channel_id=1, source_target_pairs={{0,1},{1,0},{2,3},{3,2},{4,5},{5,4},{6,7},{7,6},{8,9},{9,8},{10,11... | collective-permute-start | bytes 3145736 | tf_op jit(solution)/shard_map/ppermute | solution.py:27
  106.7 3.8 %collective-permute-start.1 = (bf16[512,512]{1,0:T(8,128)(2,1)S(1)}, bf16[512,512]{1,0:T(8,128)(2,1)S(1)}, u32[]{:S(2)}, u32[]{:S(2)}) collective-permute-start(bf16[512,512]{1,0:T(8,128)(2,1)S(1)} %bitcast.91), channel_id=1, source_target_pairs={{0,1},{1,0},{2,3},{3,2},{4,5},{5,4},{6,7},{7,6},{8,9},{9,8},{10,11... | collective-permute-start | bytes 1572872 | tf_op jit(solution)/shard_map/ppermute | solution.py:27
  136.7 1.2 copy-start.2
  147.3 1.1 copy-start.1
  148.4 36.2 %all-to-all-start.3 = ((bf16[32,40,512]{2,1,0:T(8,128)(2,1)}), bf16[32,40,512]{2,1,0:T(8,128)(2,1)S(1)}, u32[]{:S(2)}, u32[]{:S(2)}) async-start(bf16[32,40,512]{2,1,0:T(8,128)(2,1)} %bitcast.75), calls=%async_computation.3 | async-start | bytes 2621440 | tf_op jit(solution)/shard_map/all_to_all | solution.py:168
  184.6 70.2 %all-to-all-start.4 = ((bf16[32,40,512]{2,1,0:T(8,128)(2,1)}), bf16[32,40,512]{2,1,0:T(8,128)(2,1)S(1)}, u32[]{:S(2)}, u32[]{:S(2)}) async-start(bf16[32,40,512]{2,1,0:T(8,128)(2,1)} %bitcast.13), calls=%async_computation.4 | async-start | bytes 2621440 | tf_op jit(solution)/shard_map/all_to_all | solution.py:170
  193.9 6.3 %collective-permute-start.2 = (bf16[4,128,512]{1,2,0:T(8,128)(2,1)}, bf16[4,128,512]{1,2,0:T(8,128)(2,1)}, u32[]{:S(2)}, u32[]{:S(2)}) collective-permute-start(bf16[4,128,512]{1,2,0:T(8,128)(2,1)} %get-tuple-element.25), channel_id=1, source_target_pairs={{0,1},{1,0},{2,3},{3,2},{4,5},{5,4},{6,7},{7,6},{8,9},{9,8},{10,11... | collective-permute-start | bytes 1572872 | tf_op jit(solution)/shard_map/ppermute | solution.py:27
  202.2 15.7 %collective-permute-start.3 = (bf16[2,128,512]{1,2,0:T(8,128)(2,1)}, bf16[2,128,512]{1,2,0:T(8,128)(2,1)S(1)}, u32[]{:S(2)}, u32[]{:S(2)}) collective-permute-start(bf16[2,128,512]{1,2,0:T(8,128)(2,1)} %get-tuple-element.22), channel_id=1, source_target_pairs={{0,2},{2,4},{4,6},{6,0},{1,3},{3,5},{5,7},{7,1},{8,10},{10,12},{12... | collective-permute-start | bytes 786440 | tf_op jit(solution)/shard_map/ppermute | solution.py:159
  205.6 22.3 %collective-permute-start.4 = (bf16[2,128,512]{1,2,0:T(8,128)(2,1)}, bf16[2,128,512]{1,2,0:T(8,128)(2,1)}, u32[]{:S(2)}, u32[]{:S(2)}) collective-permute-start(bf16[2,128,512]{1,2,0:T(8,128)(2,1)} %get-tuple-element.23), channel_id=1, source_target_pairs={{0,4},{2,6},{4,0},{6,2},{1,5},{3,7},{5,1},{7,3},{8,12},{10,14},{12... | collective-permute-start | bytes 786440 | tf_op jit(solution)/shard_map/ppermute | solution.py:159
  210.1 17.8 %collective-permute-start.5 = (bf16[2,128,512]{1,2,0:T(8,128)(2,1)}, bf16[2,128,512]{1,2,0:T(8,128)(2,1)}, u32[]{:S(2)}, u32[]{:S(2)}) collective-permute-start(bf16[2,128,512]{1,2,0:T(8,128)(2,1)} %get-tuple-element.24), channel_id=1, source_target_pairs={{0,6},{2,0},{4,2},{6,4},{1,7},{3,1},{5,3},{7,5},{8,14},{10,8},{12,... | collective-permute-start | bytes 786440 | tf_op jit(solution)/shard_map/ppermute | solution.py:159
  227.9 7.9 %copy-start.8 = (pred[128,1280]{1,0:T(32,128)(4,1)S(1)}, pred[128,1280]{1,0:T(32,128)(4,1)}, u32[]{:S(2)}) copy-start(pred[128,1280]{1,0:T(32,128)(4,1)} %copy-done.7) | copy-start | bytes 491524
  246.4 7.2 %collective-permute-start.6 = (bf16[512,512]{1,0:T(8,128)(2,1)S(1)}, bf16[512,512]{1,0:T(8,128)(2,1)S(1)}, u32[]{:S(2)}, u32[]{:S(2)}) collective-permute-start(bf16[512,512]{1,0:T(8,128)(2,1)S(1)} %all_gather.7), channel_id=1, source_target_pairs={{0,1},{1,0},{2,3},{3,2},{4,5},{5,4},{6,7},{7,6},{8,9},{9,8},{10,11... | collective-permute-start | bytes 1572872 | tf_op jit(solution)/shard_map/ppermute | solution.py:27
  254.9 25.4 %all-to-all-start.5 = ((bf16[64,8,512]{2,1,0:T(8,128)(2,1)}), bf16[64,8,512]{2,1,0:T(8,128)(2,1)S(1)}, u32[]{:S(2)}, u32[]{:S(2)}) async-start(bf16[64,8,512]{2,1,0:T(8,128)(2,1)} %fusion.12), calls=%async_computation.5 | async-start | bytes 1048576 | tf_op jit(solution)/shard_map/all_to_all | solution.py:179
  266.3 2.5 copy-start.4
Sparse Core Ops, SparseCore 0:
  43.2 48.4 all-gather.1

commit v3 on v2

v3 whole, which is shorter than its diff:
```python
import jax
import jax.numpy as jnp
from jax import lax
from jax.experimental import pallas as pl
from jax.experimental.pallas import tpu as pltpu
from jax.sharding import Mesh, PartitionSpec as P

BF = jnp.bfloat16
F32 = jnp.float32
XC = ("x", "c")
YZ = ("dp", "z")
ZX = ("z", "x")
CAP = 20
MAIN = 16
PAIR = 2 * CAP


def mm(a, b, dims=((1,), (0,))):
    return lax.dot_general(a, b, (dims, ((), ())), preferred_element_type=F32)


def after(x, *deps):
    return lax.optimization_barrier((x,) + deps)[0]


def swap_core(x):
    return lax.ppermute(x, "c", [(0, 1), (1, 0)])


def column_order(tokens):
    a = lax.broadcasted_iota(jnp.int32, (1024, 1024), 0)
    b = lax.broadcasted_iota(jnp.int32, (1024, 1024), 1)
    y, z, xc, i = a // 512, (a // 64) % 8, (a // 8) % 8, a % 8
    pick = (xc * 128 + y * 64 + z * 8 + i == b).astype(BF)
    parts = [mm(tokens[:, p * 1024 : (p + 1) * 1024], pick).astype(BF) for p in range(4)]
    return jnp.concatenate(
        [parts[p][:, xc * 128 : (xc + 1) * 128] for xc in range(8) for p in range(4)], axis=1
    )


def expert_kernel(x_ref, g_ref, up_ref, down_ref, back_ref, out_ref):
    w_up, w_down = up_ref[0], down_ref[0]
    x = x_ref[...].reshape(256, 512)
    g = g_ref[...].reshape(256, 512)
    pre = mm(x, w_up)
    grad_act = mm(g, w_down, ((1,), (1,)))
    gate, upper = pre[:, :512], pre[:, 512:]
    sigma = jax.nn.sigmoid(gate)
    soft = gate * sigma
    act = (soft * upper).astype(BF)
    grad_gate = (grad_act * upper * sigma * (1.0 + gate * (1.0 - sigma))).astype(BF)
    grad_up = (grad_act * soft).astype(BF)
    last = ((1,), (1,))
    back = mm(grad_gate, w_up[:, :512], last) + mm(grad_up, w_up[:, 512:], last)
    back = back.astype(BF).reshape(16, 16, 512)
    out = mm(act, w_down).astype(BF).reshape(16, 16, 512)
    step = pl.program_id(0)

    @pl.when(step != 3)
    def _():
        back_ref[...] = back
        out_ref[...] = out

    @pl.when(step == 3)
    def _():
        keep = (lax.broadcasted_iota(jnp.int32, (16, 16, 512), 1) % 8) < 4
        back_ref[...] = jnp.where(keep, back_ref[...].astype(F32), back.astype(F32)).astype(BF)
        out_ref[...] = jnp.where(keep, out_ref[...].astype(F32), out.astype(F32)).astype(BF)


def expert_rows(x, g, ups, downs):
    def block(i):
        return (0, jnp.where(i == 0, 0, jnp.where(i == 1, 3, jnp.where(i < 4, 2, jnp.where(i == 4, 1, 4)))), 0)

    rows = pl.BlockSpec((16, 16, 512), block)
    shape = jax.ShapeDtypeStruct((16, 80, 512), BF)
    back, out = pl.pallas_call(
        expert_kernel,
        grid=(6,),
        in_specs=[
            rows,
            rows,
            pl.BlockSpec((1, 512, 1024), lambda i: (i // 3, 0, 0)),
            pl.BlockSpec((1, 512, 512), lambda i: (i // 3, 0, 0)),
        ],
        out_specs=[rows, rows],
        out_shape=[shape, shape],
        compiler_params=pltpu.CompilerParams(vmem_limit_bytes=40 * 1024 * 1024),
        cost_estimate=pl.CostEstimate(flops=4_800_000_000, bytes_accessed=8_500_000, transcendentals=800_000),
    )(x.reshape(16, 80, 512), g.reshape(16, 80, 512), ups, downs)
    return back.reshape(32, PAIR, 512), out.reshape(32, PAIR, 512)


def three(x):
    high = x.astype(BF)
    mid = (x - high.astype(F32)).astype(BF)
    low = (x - high.astype(F32) - mid.astype(F32)).astype(BF)
    return high, mid, low


def named_in(routes):
    lanes = lax.broadcasted_iota(jnp.int32, (1,) * routes.ndim + (64,), routes.ndim)
    return routes[..., None] == lanes


def slot_code(named):
    rows = named.shape[-2]
    below = (
        lax.broadcasted_iota(jnp.int32, (rows, rows), 0)
        > lax.broadcasted_iota(jnp.int32, (rows, rows), 1)
    ).astype(BF)
    rank = jnp.einsum("ij,...je->...ie", below, named.astype(BF), preferred_element_type=F32)
    return jnp.where(named, rank, -1.0).astype(BF)


def slot_layout(q, at):
    q = (q + 32 * (at % 2)) % PAIR
    other = jnp.where(q < 2 * MAIN, q // MAIN, (q - 2 * MAIN) // (CAP - MAIN))
    place = jnp.where(q < 2 * MAIN, q % MAIN, MAIN + (q - 2 * MAIN) % (CAP - MAIN))
    return other, place


def shift_x(x, d):
    return lax.ppermute(x, "x", [(i, (i + d) % 4) for i in range(4)])


def take(x, i, axis):
    return lax.dynamic_index_in_dim(x, i, axis, keepdims=False)


def shards(tokens, routes, mix_weights, gate_up, down, w_in, grad_combined):
    rows = tokens.shape[0]
    gate_up, down = gate_up[0], down[0]
    core, at, plane = lax.axis_index("c"), lax.axis_index("x"), lax.axis_index("z")
    slots = 64 * CAP

    w_part = lax.all_to_all(
        jnp.broadcast_to(w_in[None], (64,) + w_in.shape), YZ, split_axis=0, concat_axis=0, tiled=True
    ).reshape(512, 512)

    payload = jnp.concatenate(
        [grad_combined, routes.astype(BF), *three(mix_weights), jnp.zeros((rows, 96), BF)], axis=1
    )
    column = lax.all_gather(payload, "z", axis=0, tiled=True).reshape(8, rows, 640)

    ordered = column_order(tokens)
    feats = ordered.reshape(rows, 4, 2, 512).transpose(2, 1, 0, 3)
    mine = take(feats, core, 0)
    theirs = swap_core(take(feats, 1 - core, 0))
    both = jnp.stack([jnp.where(core == 0, mine, theirs), jnp.where(core == 0, theirs, mine)], axis=1)
    blocks = [take(both, at, 0)]
    for d in (1, 2, 3):
        blocks.append(shift_x(take(both, (at + d) % 4, 0), d))
    blocks = jnp.stack(blocks)
    feature_block = jnp.stack([take(blocks, (at - j) % 4, 0) for j in range(4)])

    gate_up2, down2 = swap_core(gate_up), swap_core(down)
    ups = jnp.stack([gate_up, gate_up2])
    downs = jnp.stack([down, down2])

    partial = mm(feature_block.reshape(8 * rows, 512), w_part).astype(BF).reshape(8, rows, 512)
    partials = lax.all_to_all(partial, XC, split_axis=0, concat_axis=0, tiled=True)
    latent = jnp.sum(partials.astype(F32), axis=0).astype(BF)

    r = lax.broadcasted_iota(jnp.int32, (1, slots), 1)
    other, place = slot_layout(r % PAIR, at)
    spread = (
        lax.broadcasted_iota(jnp.int32, (64, slots), 0) == (r // PAIR) * 2 + (core + other) % 2
    ).astype(BF)
    code = slot_code(jnp.any(named_in(routes), axis=1))
    onehot = (mm(code, spread) == place.astype(F32)).astype(BF)
    out_send = mm(onehot, latent, ((0,), (0,))).astype(BF).reshape(32, PAIR, 512)
    recv = lax.all_to_all(out_send, ZX, split_axis=0, concat_axis=0, tiled=True)

    r = lax.broadcasted_iota(jnp.int32, (1, 4 * PAIR), 1)
    other, place = slot_layout(r % PAIR, at)
    spread = (
        lax.broadcasted_iota(jnp.int32, (64, 4 * PAIR), 0)
        == plane * 8 + (at + r // PAIR) % 4 * 2 + (core + other) % 2
    ).astype(BF)
    hit = named_in(column[:, :, 512:520].astype(jnp.int32))
    code = slot_code(jnp.any(hit, axis=2)).reshape(8 * rows, 64)
    send = (mm(code, spread) == place.astype(F32)).reshape(8, rows, 4 * PAIR)
    at_slot = 0.0
    for i in (1, 2, 3):
        piece = column[:, :, 512 + 8 * i : 520 + 8 * i].astype(F32)
        piece = jnp.sum(jnp.where(hit, piece[..., None], 0.0), axis=2).astype(BF)
        at_slot = at_slot + mm(piece.reshape(8 * rows, 64), spread)
    weight = jnp.where(send, at_slot.reshape(8, rows, 4 * PAIR), 0.0)
    picked = jnp.einsum(
        "ztr,ztl->zrl", send.astype(BF), column[:, :, :512], preferred_element_type=F32
    )
    grad_send = (jnp.sum(weight, axis=1)[..., None] * picked).astype(BF).reshape(8, 4, PAIR, 512)
    blocks = jnp.stack([grad_send[:, 0]] + [shift_x(grad_send[:, d], d) for d in (1, 2, 3)])
    grad_recv = jnp.stack([take(blocks, (at - j) % 4, 0) for j in range(4)], axis=1)

    grad_rows, outputs = expert_rows(recv, grad_recv, ups, downs)
    grad_back = lax.all_to_all(grad_rows, ZX, split_axis=0, concat_axis=0, tiled=True)

    out4 = outputs.reshape(8, 4, PAIR, 512)
    back = [take(out4, at, 1)] + [shift_x(take(out4, (at - d) % 4, 1), -d) for d in (1, 2, 3)]
    back = jnp.stack(back, axis=1).reshape(8, 4 * PAIR, 512)
    weight_hi = weight.astype(BF)
    weight_lo = (weight - weight_hi.astype(F32)).astype(BF)
    mixed = sum(
        jnp.einsum("ztr,zrl->ztl", w, back, preferred_element_type=F32) for w in (weight_hi, weight_lo)
    )
    combined = lax.psum_scatter(
        mixed.astype(BF).reshape(8 * rows, 512), "z", scatter_dimension=0, tiled=True
    )

    grad_latent = mm(onehot, grad_back.reshape(slots, 512)).astype(BF)
    line_grads = lax.all_gather(grad_latent, "x", axis=0, tiled=True)
    other_grads = swap_core(line_grads)
    tokens_mine = take(feature_block, core, 1).reshape(4 * rows, 512)
    tokens_other = take(feature_block, 1 - core, 1).reshape(4 * rows, 512)
    first = ((0,), (0,))
    part = mm(tokens_mine, line_grads, first) + mm(tokens_other, other_grads, first)
    part = part.astype(BF).reshape(64, 8, 512)
    parts = lax.all_to_all(part, YZ, split_axis=0, concat_axis=0, tiled=True)
    grad_w_in = jnp.sum(parts.astype(F32), axis=0) / rows

    w_all = lax.all_gather(after(w_part, recv), XC, axis=0, tiled=True)
    w_natural = w_all.reshape(8, 64, 8, 512).transpose(1, 0, 2, 3).reshape(4096, 512)
    grad_tokens = mm(grad_latent, w_natural, ((1,), (1,))).astype(BF)
    return combined, grad_tokens, grad_w_in


def solution(mesh):
    split = Mesh(mesh.devices.reshape(8, 8, 4, 2), ("dp", "z", "x", "c"))
    every = P(("dp", "z", "x", "c"), None)
    each = P(("z", "x", "c"), None, None)
    return jax.shard_map(
        shards,
        mesh=split,
        in_specs=(every, every, every, each, each, every, every),
        out_specs=(every, every, every),
        check_vma=False,
    )
```

time: 291 us -> 305 us (1.048)
  the two profiles are of different devices: /device:TPU:1 before, /device:TPU:36 now
where the time goes in v3:
time: 305 us; the launch traced here: 303 us
  waiting for transfers between devices  123 us (40%)
  starting transfers between devices  73.4 us (24%)
  blocking collectives  42.9 us (14%)
  matrix products  18.3 us (6%)
  local copies, waits for them, and re-layouts  15.2 us (5%)
  between operations  14.8 us (5%)
  Pallas kernels  8.51 us (3%)
  other arithmetic  7.33 us (2%)
    ppermute x9, waiting for transfers between devices, shift_x(): return lax.ppermute(x, 'x', [(i, (i + d) % 4) for i in range(4)])  50.3 us
    all_to_all x1, waiting for transfers between devices, shards(): recv = lax.all_to_all(out_send, ZX, split_axis=0, concat_axis=0, tiled=True)  36.5 us
    all_to_all x1, blocking collectives, shards(): parts = lax.all_to_all(part, YZ, split_axis=0, concat_axis=0, tiled=True)  28.9 us
    ppermute x9, starting transfers between devices, shift_x(): return lax.ppermute(x, 'x', [(i, (i + d) % 4) for i in range(4)])  27 us
    all_to_all x1, starting transfers between devices, shards(): lax.all_to_all(jnp.broadcast_to(w_in[None], (64,) + w_in.shape), YZ, spli...  16.3 us
    dot_general x15, matrix products, mm(): return lax.dot_general(a, b, (dims, ((), ())), preferred_element_type=F32)  15.4 us
    reduce_scatter x1, waiting for transfers between devices, shards(): lax.psum_scatter(mixed.astype(BF).reshape(8 * rows, 512), 'z', scatter_di...  14.8 us
    all_gather x1, blocking collectives, shards(): line_grads = lax.all_gather(grad_latent, 'x', axis=0, tiled=True)  14 us
  transfers between devices with their start and end apart: 20, of which 14 were waited for; matrix products, arithmetic and copies ran while one was open for 10% of the time, Pallas kernels for 3%

profile of v3, /device:TPU:36, one launch (start us, length us, event | category | flops | bytes accessed | tf_op | source)
XLA Modules:
  0.0 303.4 jit_solution(15855554422080042670)
XLA Ops:
  7.2 2.5 fusion.8
  13.6 1.9 collective-permute-start
  16.4 16.3 %all-to-all-start = ((bf16[64,8,512]{2,1,0:T(8,128)(2,1)}), bf16[64,8,512]{2,1,0:T(8,128)(2,1)S(1)}, u32[]{:S(2)}, u32[]{:S(2)}) async-start(bf16[64,8,512]{2,1,0:T(8,128)(2,1)} %broadcast_in_dim.59), calls=%async_computation | async-start | bytes 1048576 | tf_op jit(solution)/shard_map/all_to_all | solution.py:137
  33.2 3.1 %collective-permute-start.1 = (bf16[2,128,512]{2,1,0:T(8,128)(2,1)S(1)}, bf16[2,128,512]{2,1,0:T(8,128)(2,1)S(1)}, u32[]{:S(2)}, u32[]{:S(2)}) collective-permute-start(bf16[2,128,512]{2,1,0:T(8,128)(2,1)S(1)} %get-tuple-element.35), channel_id=1, source_target_pairs={{0,2},{2,4},{4,6},{6,0},{1,3},{3,5},{5,7},{7,1},{8,10},{10,12},{12... | collective-permute-start | bytes 786440 | tf_op jit(solution)/shard_map/ppermute | solution.py:124
  36.3 2.7 collective-permute-start.2
  39.0 3.0 %collective-permute-start.3 = (bf16[2,128,512]{2,1,0:T(8,128)(2,1)S(1)}, bf16[2,128,512]{2,1,0:T(8,128)(2,1)S(1)}, u32[]{:S(2)}, u32[]{:S(2)}) collective-permute-start(bf16[2,128,512]{2,1,0:T(8,128)(2,1)S(1)} %get-tuple-element.37), channel_id=1, source_target_pairs={{0,6},{2,0},{4,2},{6,4},{1,7},{3,1},{5,3},{7,5},{8,14},{10,8},{12,... | collective-permute-start | bytes 786440 | tf_op jit(solution)/shard_map/ppermute | solution.py:124
  42.2 2.1 collective-permute-done.1
  44.3 4.6 %collective-permute-done.2 = bf16[2,128,512]{2,1,0:T(8,128)(2,1)S(1)} collective-permute-done((bf16[2,128,512]{2,1,0:T(8,128)(2,1)S(1)}, bf16[2,128,512]{2,1,0:T(8,128)(2,1)S(1)}, u32[]{:S(2)}, u32[]{:S(2)}) %collective-permute-start.2) | collective-permute-done | bytes 262176 | tf_op jit(solution)/shard_map/ppermute | solution.py:124
  48.9 3.7 %collective-permute-done.3 = bf16[2,128,512]{2,1,0:T(8,128)(2,1)S(1)} collective-permute-done((bf16[2,128,512]{2,1,0:T(8,128)(2,1)S(1)}, bf16[2,128,512]{2,1,0:T(8,128)(2,1)S(1)}, u32[]{:S(2)}, u32[]{:S(2)}) %collective-permute-start.3) | collective-permute-done | bytes 262176 | tf_op jit(solution)/shard_map/ppermute | solution.py:124
  53.0 1.7 convolution_convert_fusion.2
  54.7 4.8 %all-to-all-start.1 = ((bf16[8,128,512]{2,1,0:T(8,128)(2,1)}), bf16[8,128,512]{2,1,0:T(8,128)(2,1)S(1)}, u32[]{:S(2)}, u32[]{:S(2)}) async-start(bf16[8,128,512]{2,1,0:T(8,128)(2,1)} %bitcast.24), calls=%async_computation.1 | async-start | bytes 2097152 | tf_op jit(solution)/shard_map/all_to_all | solution.py:162
  60.1 12.2 %all-to-all-done.1 = bf16[8,128,512]{2,1,0:T(8,128)(2,1)S(1)} async-done(((bf16[8,128,512]{2,1,0:T(8,128)(2,1)}), bf16[8,128,512]{2,1,0:T(8,128)(2,1)S(1)}, u32[]{:S(2)}, u32[]{:S(2)}) %all-to-all-start.1) | async-done | bytes 1048608 | tf_op jit(solution)/shard_map/all_to_all | solution.py:162
  72.5 1.7 convolution_convert_fusion.1
  74.2 10.7 %all-to-all-start.2 = ((bf16[32,40,512]{2,1,0:T(8,128)(2,1)}), bf16[32,40,512]{2,1,0:T(8,128)(2,1)S(1)}, u32[]{:S(2)}, u32[]{:S(2)}) async-start(bf16[32,40,512]{2,1,0:T(8,128)(2,1)} %bitcast.25), calls=%async_computation.2 | async-start | bytes 2621440 | tf_op jit(solution)/shard_map/all_to_all | solution.py:173
  86.4 36.5 %all-to-all-done.2 = bf16[32,40,512]{2,1,0:T(8,128)(2,1)S(1)} async-done(((bf16[32,40,512]{2,1,0:T(8,128)(2,1)}), bf16[32,40,512]{2,1,0:T(8,128)(2,1)S(1)}, u32[]{:S(2)}, u32[]{:S(2)}) %all-to-all-start.2) | async-done | bytes 1310752 | tf_op jit(solution)/shard_map/all_to_all | solution.py:173
  122.9 1.9 collective-permute-start.7
  124.8 2.6 collective-permute-start.8
  127.5 8.6 %all-gather.3.cloned.1.call-done = bf16[1024,640]{1,0:T(8,128)(2,1)} async-done(((bf16[128,640]{1,0:T(8,128)(2,1)}), bf16[1024,640]{1,0:T(8,128)(2,1)}) %all-gather.3.cloned.1.call-update) | async-done | bytes 1310736 | tf_op jit(solution)/shard_map/all_gather | solution.py:144
  136.1 2.8 fusion.114
  140.0 1.1 copy.136
  141.0 1.1 copy.137
  142.1 1.1 copy.138
  147.6 3.4 %collective-permute-start.4 = (bf16[8,40,512]{2,1,0:T(8,128)(2,1)S(1)}, bf16[8,40,512]{2,1,0:T(8,128)(2,1)S(1)}, u32[]{:S(2)}, u32[]{:S(2)}) collective-permute-start(bf16[8,40,512]{2,1,0:T(8,128)(2,1)S(1)} %get-tuple-element.21), channel_id=1, source_target_pairs={{0,2},{2,4},{4,6},{6,0},{1,3},{3,5},{5,7},{7,1},{8,10},{10,12},{12... | collective-permute-start | bytes 983048 | tf_op jit(solution)/shard_map/ppermute | solution.py:124
  150.9 3.6 %collective-permute-start.5 = (bf16[8,40,512]{2,1,0:T(8,128)(2,1)S(1)}, bf16[8,40,512]{2,1,0:T(8,128)(2,1)S(1)}, u32[]{:S(2)}, u32[]{:S(2)}) collective-permute-start(bf16[8,40,512]{2,1,0:T(8,128)(2,1)S(1)} %get-tuple-element.23), channel_id=1, source_target_pairs={{0,4},{2,6},{4,0},{6,2},{1,5},{3,7},{5,1},{7,3},{8,12},{10,14},{12... | collective-permute-start | bytes 983048 | tf_op jit(solution)/shard_map/ppermute | solution.py:124
  154.5 2.2 collective-permute-start.6
  156.7 1.2 pad_maximum_fusion.6.down_ref
  158.1 8.3 %collective-permute-done.4 = bf16[8,40,512]{2,1,0:T(8,128)(2,1)S(1)} collective-permute-done((bf16[8,40,512]{2,1,0:T(8,128)(2,1)S(1)}, bf16[8,40,512]{2,1,0:T(8,128)(2,1)S(1)}, u32[]{:S(2)}, u32[]{:S(2)}) %collective-permute-start.4) | collective-permute-done | bytes 327712 | tf_op jit(solution)/shard_map/ppermute | solution.py:124
  166.4 11.9 %collective-permute-done.5 = bf16[8,40,512]{2,1,0:T(8,128)(2,1)S(1)} collective-permute-done((bf16[8,40,512]{2,1,0:T(8,128)(2,1)S(1)}, bf16[8,40,512]{2,1,0:T(8,128)(2,1)S(1)}, u32[]{:S(2)}, u32[]{:S(2)}) %collective-permute-start.5) | collective-permute-done | bytes 327712 | tf_op jit(solution)/shard_map/ppermute | solution.py:124
  178.3 4.5 %collective-permute-done.6 = bf16[8,40,512]{2,1,0:T(8,128)(2,1)S(1)} collective-permute-done((bf16[8,40,512]{2,1,0:T(8,128)(2,1)S(1)}, bf16[8,40,512]{2,1,0:T(8,128)(2,1)S(1)}, u32[]{:S(2)}, u32[]{:S(2)}) %collective-permute-start.6) | collective-permute-done | bytes 327712 | tf_op jit(solution)/shard_map/ppermute | solution.py:124
  183.2 8.5 %shard_map.94 = (bf16[16,80,512]{2,1,0:T(8,128)(2,1)}, bf16[16,80,512]{2,1,0:T(8,128)(2,1)S(1)}) custom-call(bf16[16,80,512]{2,1,0:T(8,128)(2,1)S(1)} %bitcast.191, bf16[16,80,512]{2,1,0:T(8,128)(2,1)S(1)} %bitcast.192, bf16[2,512,1024]{2,1,0:T(8,128)(2,1)S(1)} %pad_maximum_fusion.up_ref, bf16[2,512,512]{2,1,0:T(8,128)(2,1)S(1)} %pad_maximum_fusion.6.down_ref), custom_call_target="tpu_custom_call" | custom-call | flops 4800000000 | bytes 8500000 | tf_op jit(solution)/shard_map/pallas_call | solution.py:77
  191.7 6.0 %all-to-all-start.3 = ((bf16[32,40,512]{2,1,0:T(8,128)(2,1)}), bf16[32,40,512]{2,1,0:T(8,128)(2,1)}, u32[]{:S(2)}, u32[]{:S(2)}) async-start(bf16[32,40,512]{2,1,0:T(8,128)(2,1)} %bitcast.53), calls=%async_computation.4 | async-start | bytes 2621440 | tf_op jit(solution)/shard_map/all_to_all | solution.py:198
  197.9 2.5 collective-permute-start.9
  200.4 4.6 %collective-permute-start.10 = (bf16[8,40,512]{2,1,0:T(8,128)(2,1)S(1)}, bf16[8,40,512]{2,1,0:T(8,128)(2,1)S(1)}, u32[]{:S(2)}, u32[]{:S(2)}) collective-permute-start(bf16[8,40,512]{2,1,0:T(8,128)(2,1)S(1)} %get-tuple-element.14), channel_id=1, source_target_pairs={{0,4},{2,6},{4,0},{6,2},{1,5},{3,7},{5,1},{7,3},{8,12},{10,14},{12... | collective-permute-start | bytes 983048 | tf_op jit(solution)/shard_map/ppermute | solution.py:124
  205.0 2.1 collective-permute-start.11
  207.1 1.1 constant_dynamic-slice_fusion
  208.2 6.8 %collective-permute-done.9 = bf16[8,40,512]{2,1,0:T(8,128)(2,1)S(1)} collective-permute-done((bf16[8,40,512]{2,1,0:T(8,128)(2,1)S(1)}, bf16[8,40,512]{2,1,0:T(8,128)(2,1)S(1)}, u32[]{:S(2)}, u32[]{:S(2)}) %collective-permute-start.9) | collective-permute-done | bytes 327712 | tf_op jit(solution)/shard_map/ppermute | solution.py:124
  215.0 4.5 %collective-permute-done.10 = bf16[8,40,512]{2,1,0:T(8,128)(2,1)S(1)} collective-permute-done((bf16[8,40,512]{2,1,0:T(8,128)(2,1)S(1)}, bf16[8,40,512]{2,1,0:T(8,128)(2,1)S(1)}, u32[]{:S(2)}, u32[]{:S(2)}) %collective-permute-start.10) | collective-permute-done | bytes 327712 | tf_op jit(solution)/shard_map/ppermute | solution.py:124
  219.6 3.8 %collective-permute-done.11 = bf16[8,40,512]{2,1,0:T(8,128)(2,1)S(1)} collective-permute-done((bf16[8,40,512]{2,1,0:T(8,128)(2,1)S(1)}, bf16[8,40,512]{2,1,0:T(8,128)(2,1)S(1)}, u32[]{:S(2)}, u32[]{:S(2)}) %collective-permute-start.11) | collective-permute-done | bytes 327712 | tf_op jit(solution)/shard_map/ppermute | solution.py:124
  224.6 1.8 convolution_convert_fusion.7
  226.4 14.0 %all_gather.11 = bf16[512,512]{1,0:T(8,128)(2,1)} all-gather(bf16[128,512]{1,0:T(8,128)(2,1)S(1)} %convolution_convert_fusion.7), channel_id=1, replica_groups=mesh['dp'=8,'z'=8,'x'=4,'c'=2] {'x'}, dimensions={0}, use_global_device_ids=true | all-gather | bytes 655360 | tf_op jit(solution)/shard_map/all_gather | solution.py:213
  240.4 1.9 collective-permute-start.12
  242.3 1.6 add_convert_fusion
  243.9 1.7 fusion.115
  245.7 1.5 fusion.12
  247.2 28.9 %all_to_all.25 = bf16[64,8,512]{2,1,0:T(8,128)(2,1)S(1)} all-to-all(bf16[64,8,512]{2,1,0:T(8,128)(2,1)S(1)} %fusion.12), channel_id=1, replica_groups=mesh['dp'=8,'z'=8,'x'=4,'c'=2] {'dp','z'}, dimensions={0} | all-to-all | bytes 1048576 | tf_op jit(solution)/shard_map/all_to_all | solution.py:220
  276.8 2.8 copy.134
  279.6 2.5 convolution_convert_fusion
  282.0 14.8 %reduce-scatter.2.cloned.1.call-done = bf16[128,512]{1,0:T(8,128)(2,1)} async-done(((bf16[1024,512]{1,0:T(8,128)(2,1)}), bf16[128,512]{1,0:T(8,128)(2,1)}) %reduce-scatter.2.cloned.1.call-update) | async-done | bytes 131088 | tf_op jit(solution)/shard_map/reduce_scatter | solution.py:208
  (139 shorter events, 15.5 us)
Async XLA Ops:
  7.2 2.6 copy-start.18
  13.0 2.5 copy-start.16
  13.6 19.4 %collective-permute-start = (bf16[4,128,512]{2,1,0:T(8,128)(2,1)S(1)}, bf16[4,128,512]{2,1,0:T(8,128)(2,1)S(1)}, u32[]{:S(2)}, u32[]{:S(2)}) collective-permute-start(bf16[4,128,512]{2,1,0:T(8,128)(2,1)S(1)} %bitcast.209), channel_id=1, source_target_pairs={{0,1},{1,0},{2,3},{3,2},{4,5},{5,4},{6,7},{7,6},{8,9},{9,8},{10,11... | collective-permute-start | bytes 1572872 | tf_op jit(solution)/shard_map/ppermute | solution.py:27
  16.4 36.6 %all-to-all-start = ((bf16[64,8,512]{2,1,0:T(8,128)(2,1)}), bf16[64,8,512]{2,1,0:T(8,128)(2,1)S(1)}, u32[]{:S(2)}, u32[]{:S(2)}) async-start(bf16[64,8,512]{2,1,0:T(8,128)(2,1)} %broadcast_in_dim.59), calls=%async_computation | async-start | bytes 1048576 | tf_op jit(solution)/shard_map/all_to_all | solution.py:137
  33.2 11.1 %collective-permute-start.1 = (bf16[2,128,512]{2,1,0:T(8,128)(2,1)S(1)}, bf16[2,128,512]{2,1,0:T(8,128)(2,1)S(1)}, u32[]{:S(2)}, u32[]{:S(2)}) collective-permute-start(bf16[2,128,512]{2,1,0:T(8,128)(2,1)S(1)} %get-tuple-element.35), channel_id=1, source_target_pairs={{0,2},{2,4},{4,6},{6,0},{1,3},{3,5},{5,7},{7,1},{8,10},{10,12},{12... | collective-permute-start | bytes 786440 | tf_op jit(solution)/shard_map/ppermute | solution.py:124
  36.3 12.5 %collective-permute-start.2 = (bf16[2,128,512]{2,1,0:T(8,128)(2,1)S(1)}, bf16[2,128,512]{2,1,0:T(8,128)(2,1)S(1)}, u32[]{:S(2)}, u32[]{:S(2)}) collective-permute-start(bf16[2,128,512]{2,1,0:T(8,128)(2,1)S(1)} %get-tuple-element.36), channel_id=1, source_target_pairs={{0,4},{2,6},{4,0},{6,2},{1,5},{3,7},{5,1},{7,3},{8,12},{10,14},{12... | collective-permute-start | bytes 786440 | tf_op jit(solution)/shard_map/ppermute | solution.py:124
  39.0 13.6 %collective-permute-start.3 = (bf16[2,128,512]{2,1,0:T(8,128)(2,1)S(1)}, bf16[2,128,512]{2,1,0:T(8,128)(2,1)S(1)}, u32[]{:S(2)}, u32[]{:S(2)}) collective-permute-start(bf16[2,128,512]{2,1,0:T(8,128)(2,1)S(1)} %get-tuple-element.37), channel_id=1, source_target_pairs={{0,6},{2,0},{4,2},{6,4},{1,7},{3,1},{5,3},{7,5},{8,14},{10,8},{12,... | collective-permute-start | bytes 786440 | tf_op jit(solution)/shard_map/ppermute | solution.py:124
  53.0 1.7 copy-start.3
  53.0 1.7 copy-start.5
  53.0 6.5 %copy-start.15 = (s32[128,8]{0,1:T(8,128)S(1)}, s32[128,8]{0,1:T(8,128)}, u32[]{:S(2)}) copy-start(s32[128,8]{0,1:T(8,128)} %param.8) | copy-start | bytes 12292
  54.7 17.6 %all-to-all-start.1 = ((bf16[8,128,512]{2,1,0:T(8,128)(2,1)}), bf16[8,128,512]{2,1,0:T(8,128)(2,1)S(1)}, u32[]{:S(2)}, u32[]{:S(2)}) async-start(bf16[8,128,512]{2,1,0:T(8,128)(2,1)} %bitcast.24), calls=%async_computation.1 | async-start | bytes 2097152 | tf_op jit(solution)/shard_map/all_to_all | solution.py:162
  60.1 14.1 %copy-start.12 = (pred[128,1280]{1,0:T(32,128)(4,1)}, pred[128,1280]{1,0:T(32,128)(4,1)S(1)}, u32[]{:S(2)}) copy-start(pred[128,1280]{1,0:T(32,128)(4,1)S(1)} %convolution_compare_fusion) | copy-start | bytes 491524
  72.5 12.5 %copy-start.17 = (f32[128,8]{0,1:T(8,128)S(1)}, f32[128,8]{0,1:T(8,128)}, u32[]{:S(2)}) copy-start(f32[128,8]{0,1:T(8,128)} %param.9) | copy-start | bytes 12292
  72.5 13.0 %copy-start.14 = (bf16[128,512]{1,0:T(8,128)(2,1)S(1)}, bf16[128,512]{1,0:T(8,128)(2,1)}, u32[]{:S(2)}) copy-start(bf16[128,512]{1,0:T(8,128)(2,1)} %param.13) | copy-start | bytes 393220
  74.2 48.7 %copy-start.10 = (bf16[1,512,1024]{2,1,0:T(8,128)(2,1)S(1)}, bf16[1,512,1024]{2,1,0:T(8,128)(2,1)}, u32[]{:S(2)}) copy-start(bf16[1,512,1024]{2,1,0:T(8,128)(2,1)} %param.10) | copy-start | bytes 3145732
  74.2 48.7 %all-to-all-start.2 = ((bf16[32,40,512]{2,1,0:T(8,128)(2,1)}), bf16[32,40,512]{2,1,0:T(8,128)(2,1)S(1)}, u32[]{:S(2)}, u32[]{:S(2)}) async-start(bf16[32,40,512]{2,1,0:T(8,128)(2,1)} %bitcast.25), calls=%async_computation.2 | async-start | bytes 2621440 | tf_op jit(solution)/shard_map/all_to_all | solution.py:173
  84.9 51.2 %all-gather.3.cloned.1.call-start = ((), (), s32[]{:S(2)}) async-start(), calls=%async_computation.6 | async-start | bytes 1474560 | tf_op jit(solution)/shard_map/all_gather | solution.py:144
  86.3 190.5 %all-gather.5.cloned.1.call-start = ((), (), s32[]{:S(2)}) async-start(), calls=%async_computation.8 | async-start | bytes 4718592 | tf_op jit(solution)/shard_map/all_gather | solution.py:223
  122.9 35.0 %collective-permute-start.7 = (bf16[512,1024]{1,0:T(8,128)(2,1)S(1)}, bf16[512,1024]{1,0:T(8,128)(2,1)S(1)}, u32[]{:S(2)}, u32[]{:S(2)}) collective-permute-start(bf16[512,1024]{1,0:T(8,128)(2,1)S(1)} %bitcast.205), channel_id=1, source_target_pairs={{0,1},{1,0},{2,3},{3,2},{4,5},{5,4},{6,7},{7,6},{8,9},{9,8},{10,11... | collective-permute-start | bytes 3145736 | tf_op jit(solution)/shard_map/ppermute | solution.py:27
  124.8 31.8 %collective-permute-start.8 = (bf16[512,512]{1,0:T(8,128)(2,1)}, bf16[512,512]{1,0:T(8,128)(2,1)}, u32[]{:S(2)}, u32[]{:S(2)}) collective-permute-start(bf16[512,512]{1,0:T(8,128)(2,1)} %bitcast.210), channel_id=1, source_target_pairs={{0,1},{1,0},{2,3},{3,2},{4,5},{5,4},{6,7},{7,6},{8,9},{9,8},{10,11... | collective-permute-start | bytes 1572872 | tf_op jit(solution)/shard_map/ppermute | solution.py:27
  144.8 2.1 copy-start.11
  145.4 2.0 copy-start.7
  145.7 0.8 copy-start
  146.9 9.8 %copy-start.13 = (bf16[1,512,512]{2,1,0:T(8,128)(2,1)S(1)}, bf16[1,512,512]{2,1,0:T(8,128)(2,1)}, u32[]{:S(2)}) copy-start(bf16[1,512,512]{2,1,0:T(8,128)(2,1)} %param.11) | copy-start | bytes 1572868
  147.6 18.8 %collective-permute-start.4 = (bf16[8,40,512]{2,1,0:T(8,128)(2,1)S(1)}, bf16[8,40,512]{2,1,0:T(8,128)(2,1)S(1)}, u32[]{:S(2)}, u32[]{:S(2)}) collective-permute-start(bf16[8,40,512]{2,1,0:T(8,128)(2,1)S(1)} %get-tuple-element.21), channel_id=1, source_target_pairs={{0,2},{2,4},{4,6},{6,0},{1,3},{3,5},{5,7},{7,1},{8,10},{10,12},{12... | collective-permute-start | bytes 983048 | tf_op jit(solution)/shard_map/ppermute | solution.py:124
  150.9 27.3 %collective-permute-start.5 = (bf16[8,40,512]{2,1,0:T(8,128)(2,1)S(1)}, bf16[8,40,512]{2,1,0:T(8,128)(2,1)S(1)}, u32[]{:S(2)}, u32[]{:S(2)}) collective-permute-start(bf16[8,40,512]{2,1,0:T(8,128)(2,1)S(1)} %get-tuple-element.23), channel_id=1, source_target_pairs={{0,4},{2,6},{4,0},{6,2},{1,5},{3,7},{5,1},{7,3},{8,12},{10,14},{12... | collective-permute-start | bytes 983048 | tf_op jit(solution)/shard_map/ppermute | solution.py:124
  154.5 28.2 %collective-permute-start.6 = (bf16[8,40,512]{2,1,0:T(8,128)(2,1)S(1)}, bf16[8,40,512]{2,1,0:T(8,128)(2,1)S(1)}, u32[]{:S(2)}, u32[]{:S(2)}) collective-permute-start(bf16[8,40,512]{2,1,0:T(8,128)(2,1)S(1)} %get-tuple-element.22), channel_id=1, source_target_pairs={{0,6},{2,0},{4,2},{6,4},{1,7},{3,1},{5,3},{7,5},{8,14},{10,8},{12,... | collective-permute-start | bytes 983048 | tf_op jit(solution)/shard_map/ppermute | solution.py:124
  191.7 15.4 %copy-start.4 = (bf16[4,2,128,512]{3,2,1,0:T(8,128)(2,1)S(1)}, bf16[4,2,128,512]{3,2,1,0:T(8,128)(2,1)}, u32[]{:S(2)}) copy-start(bf16[4,2,128,512]{3,2,1,0:T(8,128)(2,1)} %copy-done.3) | copy-start | bytes 3145732
  191.7 32.9 %all-to-all-start.3 = ((bf16[32,40,512]{2,1,0:T(8,128)(2,1)}), bf16[32,40,512]{2,1,0:T(8,128)(2,1)}, u32[]{:S(2)}, u32[]{:S(2)}) async-start(bf16[32,40,512]{2,1,0:T(8,128)(2,1)} %bitcast.53), calls=%async_computation.4 | async-start | bytes 2621440 | tf_op jit(solution)/shard_map/all_to_all | solution.py:198
  197.8 99.1 %reduce-scatter.2.cloned.1.call-start = ((), (), s32[]{:S(2)}) async-start(), calls=%async_computation.7 | async-start | bytes 1179648 | tf_op jit(solution)/shard_map/reduce_scatter | solution.py:208
  197.9 17.1 %collective-permute-start.9 = (bf16[8,40,512]{2,1,0:T(8,128)(2,1)S(1)}, bf16[8,40,512]{2,1,0:T(8,128)(2,1)S(1)}, u32[]{:S(2)}, u32[]{:S(2)}) collective-permute-start(bf16[8,40,512]{2,1,0:T(8,128)(2,1)S(1)} %get-tuple-element.15), channel_id=1, source_target_pairs={{0,6},{2,0},{4,2},{6,4},{1,7},{3,1},{5,3},{7,5},{8,14},{10,8},{12,... | collective-permute-start | bytes 983048 | tf_op jit(solution)/shard_map/ppermute | solution.py:124
  200.4 19.2 %collective-permute-start.10 = (bf16[8,40,512]{2,1,0:T(8,128)(2,1)S(1)}, bf16[8,40,512]{2,1,0:T(8,128)(2,1)S(1)}, u32[]{:S(2)}, u32[]{:S(2)}) collective-permute-start(bf16[8,40,512]{2,1,0:T(8,128)(2,1)S(1)} %get-tuple-element.14), channel_id=1, source_target_pairs={{0,4},{2,6},{4,0},{6,2},{1,5},{3,7},{5,1},{7,3},{8,12},{10,14},{12... | collective-permute-start | bytes 983048 | tf_op jit(solution)/shard_map/ppermute | solution.py:124
  205.0 18.6 %copy-start.1 = (f32[20,8,8,128]{3,2,1,0:T(8,128)S(1)}, f32[20,8,8,128]{3,2,1,0:T(8,128)}, u32[]{:S(2)}) copy-start(f32[20,8,8,128]{3,2,1,0:T(8,128)} %copy-done) | copy-start | bytes 1966084
  205.0 18.5 %copy-start.8 = (pred[20,8,8,128]{3,2,1,0:T(8,128)(4,1)S(1)}, pred[20,8,8,128]{3,2,1,0:T(8,128)(4,1)}, u32[]{:S(2)}) copy-start(pred[20,8,8,128]{3,2,1,0:T(8,128)(4,1)} %copy-done.7) | copy-start | bytes 491524
  205.0 18.4 %collective-permute-start.11 = (bf16[8,40,512]{2,1,0:T(8,128)(2,1)S(1)}, bf16[8,40,512]{2,1,0:T(8,128)(2,1)S(1)}, u32[]{:S(2)}, u32[]{:S(2)}) collective-permute-start(bf16[8,40,512]{2,1,0:T(8,128)(2,1)S(1)} %get-tuple-element.13), channel_id=1, source_target_pairs={{0,2},{2,4},{4,6},{6,0},{1,3},{3,5},{5,7},{7,1},{8,10},{10,12},{12... | collective-permute-start | bytes 983048 | tf_op jit(solution)/shard_map/ppermute | solution.py:124
  224.6 17.7 %copy-start.2 = (f32[20,8,8,128]{3,2,1,0:T(8,128)S(1)}, f32[20,8,8,128]{3,2,1,0:T(8,128)}, u32[]{:S(2)}) copy-start(f32[20,8,8,128]{3,2,1,0:T(8,128)} %copy-done) | copy-start | bytes 1966084
  224.6 17.7 %copy-start.9 = (pred[20,8,8,128]{3,2,1,0:T(8,128)(4,1)S(1)}, pred[20,8,8,128]{3,2,1,0:T(8,128)(4,1)}, u32[]{:S(2)}) copy-start(pred[20,8,8,128]{3,2,1,0:T(8,128)(4,1)} %copy-done.7) | copy-start | bytes 491524
  240.4 5.3 %collective-permute-start.12 = (bf16[512,512]{1,0:T(8,128)(2,1)}, bf16[512,512]{1,0:T(8,128)(2,1)}, u32[]{:S(2)}, u32[]{:S(2)}) collective-permute-start(bf16[512,512]{1,0:T(8,128)(2,1)} %all_gather.11), channel_id=1, source_target_pairs={{0,1},{1,0},{2,3},{3,2},{4,5},{5,4},{6,7},{7,6},{8,9},{9,8},{10,11... | collective-permute-start | bytes 1572872 | tf_op jit(solution)/shard_map/ppermute | solution.py:27
  243.9 1.8 copy-start.6
Sparse Core Ops, SparseCore 0:
  88.4 47.6 all-gather.2
  138.3 46.9 all-gather.4
  244.0 52.7 reduce-scatter.1

commit v4 on v3

--- a/solution.py
+++ b/solution.py
@@ -27,15 +27,66 @@
     return lax.ppermute(x, "c", [(0, 1), (1, 0)])
 
 
-def column_order(tokens):
-    a = lax.broadcasted_iota(jnp.int32, (1024, 1024), 0)
-    b = lax.broadcasted_iota(jnp.int32, (1024, 1024), 1)
-    y, z, xc, i = a // 512, (a // 64) % 8, (a // 8) % 8, a % 8
-    pick = (xc * 128 + y * 64 + z * 8 + i == b).astype(BF)
-    parts = [mm(tokens[:, p * 1024 : (p + 1) * 1024], pick).astype(BF) for p in range(4)]
-    return jnp.concatenate(
-        [parts[p][:, xc * 128 : (xc + 1) * 128] for xc in range(8) for p in range(4)], axis=1
-    )
+def column_target(core, at):
+    a = lax.broadcasted_iota(jnp.int32, (1, 1024), 1)
+    y, z, x, c, i = a // 512, (a // 64) % 8, (a // 16) % 4, (a // 8) % 2, a % 8
+    d, m = (x - at) % 4, (c - core) % 2
+    return (d * 2 + m) * 128 + y * 64 + z * 8 + i
+
+
+def make_pick(to_ref, pick_ref):
+    @pl.when(pl.program_id(0) == 0)
+    def _():
+        at = lax.broadcasted_iota(jnp.int32, (1024, 1024), 0)
+        pick_ref[...] = jnp.where(to_ref[...] == at, 1.0, 0.0).astype(BF)
+
+
+def split_kernel(to_ref, tokens_ref, mine_ref, theirs_ref, pick_ref):
+    make_pick(to_ref, pick_ref)
+    out = mm(tokens_ref[...], pick_ref[...], ((1,), (1,))).astype(BF)
+    for d in range(4):
+        mine_ref[d] = out[:, 256 * d : 256 * d + 128]
+        theirs_ref[d] = out[:, 256 * d + 128 : 256 * d + 256]
+
+
+def split_columns(to, tokens):
+    rows = tokens.shape[0]
+    shape = jax.ShapeDtypeStruct((4, rows, 512), BF)
+    part = pl.BlockSpec((4, rows, 128), lambda p: (0, 0, p))
+    return pl.pallas_call(
+        split_kernel,
+        grid=(4,),
+        in_specs=[pl.BlockSpec((1, 1024), lambda p: (0, 0)), pl.BlockSpec((rows, 1024), lambda p: (0, p))],
+        out_specs=[part, part],
+        out_shape=[shape, shape],
+        scratch_shapes=[pltpu.VMEM((1024, 1024), BF)],
+        compiler_params=pltpu.CompilerParams(vmem_limit_bytes=32 * 1024 * 1024),
+        cost_estimate=pl.CostEstimate(flops=1_100_000_000, bytes_accessed=2_100_000, transcendentals=0),
+    )(to, tokens)
+
+
+def join_kernel(to_ref, near_ref, far_ref, b1_ref, b2_ref, b3_ref, out_ref, pick_ref):
+    make_pick(to_ref, pick_ref)
+    parts = [near_ref[...], far_ref[...]]
+    for ref in (b1_ref, b2_ref, b3_ref):
+        parts += [ref[0], ref[1]]
+    out_ref[...] = mm(jnp.concatenate(parts, axis=1), pick_ref[...]).astype(BF)
+
+
+def join_columns(to, near, far, *others):
+    rows = near.shape[0]
+    one = pl.BlockSpec((rows, 128), lambda p: (0, p))
+    two = pl.BlockSpec((2, rows, 128), lambda p: (0, 0, p))
+    return pl.pallas_call(
+        join_kernel,
+        grid=(4,),
+        in_specs=[pl.BlockSpec((1, 1024), lambda p: (0, 0)), one, one, two, two, two],
+        out_specs=pl.BlockSpec((rows, 1024), lambda p: (0, p)),
+        out_shape=jax.ShapeDtypeStruct((rows, 4096), BF),
+        scratch_shapes=[pltpu.VMEM((1024, 1024), BF)],
+        compiler_params=pltpu.CompilerParams(vmem_limit_bytes=32 * 1024 * 1024),
+        cost_estimate=pl.CostEstimate(flops=1_100_000_000, bytes_accessed=2_100_000, transcendentals=0),
+    )(to, near, far, *others)
 
 
 def expert_kernel(x_ref, g_ref, up_ref, down_ref, back_ref, out_ref):
@@ -73,7 +124,8 @@
         return (0, jnp.where(i == 0, 0, jnp.where(i == 1, 3, jnp.where(i < 4, 2, jnp.where(i == 4, 1, 4)))), 0)
 
     rows = pl.BlockSpec((16, 16, 512), block)
-    shape = jax.ShapeDtypeStruct((16, 80, 512), BF)
+    shape = pltpu.HBM((16, 80, 512), BF)
+    hbm = lambda x: pltpu.with_memory_space_constraint(x, pltpu.HBM)
     back, out = pl.pallas_call(
         expert_kernel,
         grid=(6,),
@@ -87,7 +139,7 @@
         out_shape=[shape, shape],
         compiler_params=pltpu.CompilerParams(vmem_limit_bytes=40 * 1024 * 1024),
         cost_estimate=pl.CostEstimate(flops=4_800_000_000, bytes_accessed=8_500_000, transcendentals=800_000),
-    )(x.reshape(16, 80, 512), g.reshape(16, 80, 512), ups, downs)
+    )(x.reshape(16, 80, 512), hbm(g.reshape(16, 80, 512)), hbm(ups), hbm(downs))
     return back.reshape(32, PAIR, 512), out.reshape(32, PAIR, 512)
 
 
@@ -143,16 +195,14 @@
     )
     column = lax.all_gather(payload, "z", axis=0, tiled=True).reshape(8, rows, 640)
 
-    ordered = column_order(tokens)
-    feats = ordered.reshape(rows, 4, 2, 512).transpose(2, 1, 0, 3)
-    mine = take(feats, core, 0)
-    theirs = swap_core(take(feats, 1 - core, 0))
+    to = column_target(core, at)
+    mine, theirs = split_columns(to, tokens)
+    theirs = swap_core(theirs)
     both = jnp.stack([jnp.where(core == 0, mine, theirs), jnp.where(core == 0, theirs, mine)], axis=1)
-    blocks = [take(both, at, 0)]
-    for d in (1, 2, 3):
-        blocks.append(shift_x(take(both, (at + d) % 4, 0), d))
-    blocks = jnp.stack(blocks)
+    blocks = jnp.stack([both[0]] + [shift_x(both[d], d) for d in (1, 2, 3)])
     feature_block = jnp.stack([take(blocks, (at - j) % 4, 0) for j in range(4)])
+    tokens_mine = take(feature_block, core, 1).reshape(4 * rows, 512)
+    tokens_other = take(feature_block, 1 - core, 1).reshape(4 * rows, 512)
 
     gate_up2, down2 = swap_core(gate_up), swap_core(down)
     ups = jnp.stack([gate_up, gate_up2])
@@ -170,6 +220,7 @@
     code = slot_code(jnp.any(named_in(routes), axis=1))
     onehot = (mm(code, spread) == place.astype(F32)).astype(BF)
     out_send = mm(onehot, latent, ((0,), (0,))).astype(BF).reshape(32, PAIR, 512)
+    out_send = after(out_send, column, ups, downs, tokens_mine, tokens_other)
     recv = lax.all_to_all(out_send, ZX, split_axis=0, concat_axis=0, tiled=True)
 
     r = lax.broadcasted_iota(jnp.int32, (1, 4 * PAIR), 1)
@@ -191,8 +242,8 @@
         "ztr,ztl->zrl", send.astype(BF), column[:, :, :512], preferred_element_type=F32
     )
     grad_send = (jnp.sum(weight, axis=1)[..., None] * picked).astype(BF).reshape(8, 4, PAIR, 512)
-    blocks = jnp.stack([grad_send[:, 0]] + [shift_x(grad_send[:, d], d) for d in (1, 2, 3)])
-    grad_recv = jnp.stack([take(blocks, (at - j) % 4, 0) for j in range(4)], axis=1)
+    sent = jnp.stack([grad_send[:, 0]] + [shift_x(grad_send[:, d], d) for d in (1, 2, 3)])
+    grad_recv = jnp.stack([take(sent, (at - j) % 4, 0) for j in range(4)], axis=1)
 
     grad_rows, outputs = expert_rows(recv, grad_recv, ups, downs)
     grad_back = lax.all_to_all(grad_rows, ZX, split_axis=0, concat_axis=0, tiled=True)
@@ -205,24 +256,29 @@
     mixed = sum(
         jnp.einsum("ztr,zrl->ztl", w, back, preferred_element_type=F32) for w in (weight_hi, weight_lo)
     )
-    combined = lax.psum_scatter(
-        mixed.astype(BF).reshape(8 * rows, 512), "z", scatter_dimension=0, tiled=True
-    )
+    mixed = mixed.reshape(8 * rows, 512)
+    combined = lax.psum_scatter(mixed, "z", scatter_dimension=0, tiled=True).astype(BF)
+
+    grad_back = after(grad_back, mixed)
 
     grad_latent = mm(onehot, grad_back.reshape(slots, 512)).astype(BF)
     line_grads = lax.all_gather(grad_latent, "x", axis=0, tiled=True)
     other_grads = swap_core(line_grads)
-    tokens_mine = take(feature_block, core, 1).reshape(4 * rows, 512)
-    tokens_other = take(feature_block, 1 - core, 1).reshape(4 * rows, 512)
     first = ((0,), (0,))
     part = mm(tokens_mine, line_grads, first) + mm(tokens_other, other_grads, first)
     part = part.astype(BF).reshape(64, 8, 512)
     parts = lax.all_to_all(part, YZ, split_axis=0, concat_axis=0, tiled=True)
+
+    last = ((1,), (1,))
+    near = mm(line_grads, w_part, last).astype(BF).reshape(4, rows, 512)
+    far = swap_core(mm(other_grads, w_part, last).astype(BF).reshape(4, rows, 512))
+    back = [take(near, at, 0), take(far, at, 0)]
+    for d in (1, 2, 3):
+        there = (at - d) % 4
+        back.append(shift_x(jnp.stack([take(near, there, 0), take(far, there, 0)]), -d))
+    back[0] = after(back[0], parts)
+    grad_tokens = join_columns(to, *back)
     grad_w_in = jnp.sum(parts.astype(F32), axis=0) / rows
-
-    w_all = lax.all_gather(after(w_part, recv), XC, axis=0, tiled=True)
-    w_natural = w_all.reshape(8, 64, 8, 512).transpose(1, 0, 2, 3).reshape(4096, 512)
-    grad_tokens = mm(grad_latent, w_natural, ((1,), (1,))).astype(BF)
     return combined, grad_tokens, grad_w_in
 
 

time: 305 us -> 244 us (0.80)
  the two profiles are of different devices: /device:TPU:36 before, /device:TPU:1 now
where the time goes in v4:
time: 244 us; the launch traced here: 243 us
  starting transfers between devices  102 us (42%)
  waiting for transfers between devices  65 us (27%)
  Pallas kernels  17.5 us (7%)
  between operations  14.8 us (6%)
  blocking collectives  12.2 us (5%)
  other arithmetic  11.6 us (5%)
  matrix products  11.1 us (5%)
  local copies, waits for them, and re-layouts  9.18 us (4%)
    ppermute x12, waiting for transfers between devices, shift_x(): return lax.ppermute(x, 'x', [(i, (i + d) % 4) for i in range(4)])  47.3 us
    ppermute x12, starting transfers between devices, shift_x(): return lax.ppermute(x, 'x', [(i, (i + d) % 4) for i in range(4)])  38.6 us
    ppermute x5, starting transfers between devices, swap_core(): return lax.ppermute(x, 'c', [(0, 1), (1, 0)])  21 us
    all_gather x1, blocking collectives, shards(): line_grads = lax.all_gather(grad_latent, 'x', axis=0, tiled=True)  12.2 us
    all_to_all x1, starting transfers between devices, shards(): parts = lax.all_to_all(part, YZ, split_axis=0, concat_axis=0, tiled=True)  11.5 us
    all_to_all x1, starting transfers between devices, shards(): lax.all_to_all(jnp.broadcast_to(w_in[None], (64,) + w_in.shape), YZ, spli...  10.9 us
    pallas_call x1, Pallas kernels, expert_rows(): pl.pallas_call(expert_kernel, grid=(6,), in_specs=[rows, rows, pl.BlockSp...  10.2 us
    all_to_all x1, waiting for transfers between devices, shards(): parts = lax.all_to_all(part, YZ, split_axis=0, concat_axis=0, tiled=True)  8.55 us
  transfers between devices with their start and end apart: 24, of which 11 were waited for; matrix products, arithmetic and copies ran while one was open for 11% of the time, Pallas kernels for 1%

profile of v4, /device:TPU:1, one launch (start us, length us, event | category | flops | bytes accessed | tf_op | source)
XLA Modules:
  0.0 243.0 jit_solution(14660441029999919151)
XLA Ops:
  7.3 1.2 copy-done
  8.5 3.9 %shard_map.94 = (bf16[4,128,512]{2,1,0:T(8,128)(2,1)S(1)}, bf16[4,128,512]{2,1,0:T(8,128)(2,1)S(1)}) custom-call(s32[1,1024]{1,0:T(1,128)S(1)} %fusion.69.to_ref, bf16[128,4096]{1,0:T(8,128)(2,1)S(1)} %copy-done), custom_call_target="tpu_custom_call" | custom-call | flops 1100000000 | bytes 2100000 | tf_op jit(solution)/shard_map/pallas_call | solution.py:56
  12.5 8.8 %collective-permute-start = (bf16[4,128,512]{2,1,0:T(8,128)(2,1)S(1)}, bf16[4,128,512]{2,1,0:T(8,128)(2,1)S(1)}, u32[]{:S(2)}, u32[]{:S(2)}) collective-permute-start(bf16[4,128,512]{2,1,0:T(8,128)(2,1)S(1)} %get-tuple-element.11), channel_id=1, source_target_pairs={{0,1},{1,0},{2,3},{3,2},{4,5},{5,4},{6,7},{7,6},{8,9},{9,8},{10,11... | collective-permute-start | bytes 1572872 | tf_op jit(solution)/shard_map/ppermute | solution.py:27
  23.5 10.9 %all-to-all-start = ((bf16[64,8,512]{2,1,0:T(8,128)(2,1)}), bf16[64,8,512]{2,1,0:T(8,128)(2,1)S(1)}, u32[]{:S(2)}, u32[]{:S(2)}) async-start(bf16[64,8,512]{2,1,0:T(8,128)(2,1)} %broadcast_in_dim.59), calls=%async_computation | async-start | bytes 1048576 | tf_op jit(solution)/shard_map/all_to_all | solution.py:189
  34.6 3.3 %collective-permute-start.1 = (bf16[2,128,512]{2,1,0:T(8,128)(2,1)S(1)}, bf16[2,128,512]{2,1,0:T(8,128)(2,1)S(1)}, u32[]{:S(2)}, u32[]{:S(2)}) collective-permute-start(bf16[2,128,512]{2,1,0:T(8,128)(2,1)S(1)} %get-tuple-element.43), channel_id=1, source_target_pairs={{0,2},{2,4},{4,6},{6,0},{1,3},{3,5},{5,7},{7,1},{8,10},{10,12},{12... | collective-permute-start | bytes 786440 | tf_op jit(solution)/shard_map/ppermute | solution.py:176
  37.9 3.4 %collective-permute-start.3 = (bf16[2,128,512]{2,1,0:T(8,128)(2,1)S(1)}, bf16[2,128,512]{2,1,0:T(8,128)(2,1)S(1)}, u32[]{:S(2)}, u32[]{:S(2)}) collective-permute-start(bf16[2,128,512]{2,1,0:T(8,128)(2,1)S(1)} %get-tuple-element.44), channel_id=1, source_target_pairs={{0,6},{2,0},{4,2},{6,4},{1,7},{3,1},{5,3},{7,5},{8,14},{10,8},{12,... | collective-permute-start | bytes 786440 | tf_op jit(solution)/shard_map/ppermute | solution.py:176
  41.3 3.4 %collective-permute-start.2 = (bf16[2,128,512]{2,1,0:T(8,128)(2,1)S(1)}, bf16[2,128,512]{2,1,0:T(8,128)(2,1)S(1)}, u32[]{:S(2)}, u32[]{:S(2)}) collective-permute-start(bf16[2,128,512]{2,1,0:T(8,128)(2,1)S(1)} %get-tuple-element.45), channel_id=1, source_target_pairs={{0,4},{2,6},{4,0},{6,2},{1,5},{3,7},{5,1},{7,3},{8,12},{10,14},{12... | collective-permute-start | bytes 786440 | tf_op jit(solution)/shard_map/ppermute | solution.py:176
  44.7 3.0 %collective-permute-start.5 = (bf16[512,512]{1,0:T(8,128)(2,1)S(1)}, bf16[512,512]{1,0:T(8,128)(2,1)}, u32[]{:S(2)}, u32[]{:S(2)}) collective-permute-start(bf16[512,512]{1,0:T(8,128)(2,1)S(1)} %bitcast.193), channel_id=1, source_target_pairs={{0,1},{1,0},{2,3},{3,2},{4,5},{5,4},{6,7},{7,6},{8,9},{9,8},{10,11... | collective-permute-start | bytes 1572872 | tf_op jit(solution)/shard_map/ppermute | solution.py:27
  47.8 1.9 collective-permute-start.4
  49.8 1.8 collective-permute-done.2
  52.0 1.7 convolution_convert_fusion.1
  53.7 6.7 %all-to-all-start.1 = ((bf16[8,128,512]{2,1,0:T(8,128)(2,1)}), bf16[8,128,512]{2,1,0:T(8,128)(2,1)S(1)}, u32[]{:S(2)}, u32[]{:S(2)}) async-start(bf16[8,128,512]{2,1,0:T(8,128)(2,1)} %bitcast.189), calls=%async_computation.1 | async-start | bytes 2097152 | tf_op jit(solution)/shard_map/all_to_all | solution.py:212
  61.0 2.2 pad_maximum_fusion.6.down_ref
  63.1 1.1 constant_dynamic-slice_fusion.7
  64.3 3.1 %pad_maximum_fusion.up_ref = bf16[2,512,1024]{2,1,0:T(8,128)(2,1)} fusion(bf16[1,512,1024]{2,1,0:T(8,128)(2,1)} %bitcast.16, bf16[1,512,1024]{2,1,0:T(8,128)(2,1)} %param.10), kind=kLoop, calls=%fused_computation.3 | loop fusion | flops 1048576 | bytes 4194304 | tf_op jit(solution)/shard_map/stack | solution.py:208
  67.4 8.1 %all-to-all-done.1 = bf16[8,128,512]{2,1,0:T(8,128)(2,1)S(1)} async-done(((bf16[8,128,512]{2,1,0:T(8,128)(2,1)}), bf16[8,128,512]{2,1,0:T(8,128)(2,1)S(1)}, u32[]{:S(2)}, u32[]{:S(2)}) %all-to-all-start.1) | async-done | bytes 1048608 | tf_op jit(solution)/shard_map/all_to_all | solution.py:212
  75.6 1.7 convolution_convert_fusion
  77.3 1.8 fusion.103
  80.0 7.2 %all-to-all-start.2 = ((bf16[32,40,512]{2,1,0:T(8,128)(2,1)}), bf16[32,40,512]{2,1,0:T(8,128)(2,1)S(1)}, u32[]{:S(2)}, u32[]{:S(2)}) async-start(bf16[32,40,512]{2,1,0:T(8,128)(2,1)} %bitcast.14), calls=%async_computation.2 | async-start | bytes 2621440 | tf_op jit(solution)/shard_map/all_to_all | solution.py:224
  91.0 3.1 %collective-permute-start.6 = (bf16[8,40,512]{2,1,0:T(8,128)(2,1)S(1)}, bf16[8,40,512]{2,1,0:T(8,128)(2,1)S(1)}, u32[]{:S(2)}, u32[]{:S(2)}) collective-permute-start(bf16[8,40,512]{2,1,0:T(8,128)(2,1)S(1)} %get-tuple-element.29), channel_id=1, source_target_pairs={{0,2},{2,4},{4,6},{6,0},{1,3},{3,5},{5,7},{7,1},{8,10},{10,12},{12... | collective-permute-start | bytes 983048 | tf_op jit(solution)/shard_map/ppermute | solution.py:176
  94.2 3.4 %collective-permute-start.8 = (bf16[8,40,512]{2,1,0:T(8,128)(2,1)S(1)}, bf16[8,40,512]{2,1,0:T(8,128)(2,1)S(1)}, u32[]{:S(2)}, u32[]{:S(2)}) collective-permute-start(bf16[8,40,512]{2,1,0:T(8,128)(2,1)S(1)} %get-tuple-element.30), channel_id=1, source_target_pairs={{0,6},{2,0},{4,2},{6,4},{1,7},{3,1},{5,3},{7,5},{8,14},{10,8},{12,... | collective-permute-start | bytes 983048 | tf_op jit(solution)/shard_map/ppermute | solution.py:176
  97.5 3.4 %collective-permute-start.7 = (bf16[8,40,512]{2,1,0:T(8,128)(2,1)S(1)}, bf16[8,40,512]{2,1,0:T(8,128)(2,1)S(1)}, u32[]{:S(2)}, u32[]{:S(2)}) collective-permute-start(bf16[8,40,512]{2,1,0:T(8,128)(2,1)S(1)} %get-tuple-element.31), channel_id=1, source_target_pairs={{0,4},{2,6},{4,0},{6,2},{1,5},{3,7},{5,1},{7,3},{8,12},{10,14},{12... | collective-permute-start | bytes 983048 | tf_op jit(solution)/shard_map/ppermute | solution.py:176
  101.0 7.3 %collective-permute-done.6 = bf16[8,40,512]{2,1,0:T(8,128)(2,1)S(1)} collective-permute-done((bf16[8,40,512]{2,1,0:T(8,128)(2,1)S(1)}, bf16[8,40,512]{2,1,0:T(8,128)(2,1)S(1)}, u32[]{:S(2)}, u32[]{:S(2)}) %collective-permute-start.6) | collective-permute-done | bytes 327712 | tf_op jit(solution)/shard_map/ppermute | solution.py:176
  108.3 5.0 %collective-permute-done.8 = bf16[8,40,512]{2,1,0:T(8,128)(2,1)S(1)} collective-permute-done((bf16[8,40,512]{2,1,0:T(8,128)(2,1)S(1)}, bf16[8,40,512]{2,1,0:T(8,128)(2,1)S(1)}, u32[]{:S(2)}, u32[]{:S(2)}) %collective-permute-start.8) | collective-permute-done | bytes 327712 | tf_op jit(solution)/shard_map/ppermute | solution.py:176
  113.3 8.5 %collective-permute-done.7 = bf16[8,40,512]{2,1,0:T(8,128)(2,1)S(1)} collective-permute-done((bf16[8,40,512]{2,1,0:T(8,128)(2,1)S(1)}, bf16[8,40,512]{2,1,0:T(8,128)(2,1)S(1)}, u32[]{:S(2)}, u32[]{:S(2)}) %collective-permute-start.7) | collective-permute-done | bytes 327712 | tf_op jit(solution)/shard_map/ppermute | solution.py:176
  122.1 1.2 pad_maximum_fusion.2
  123.3 10.2 %shard_map.95 = (bf16[16,80,512]{2,1,0:T(8,128)(2,1)}, bf16[16,80,512]{2,1,0:T(8,128)(2,1)}) custom-call(bf16[16,80,512]{2,1,0:T(8,128)(2,1)S(1)} %bitcast.176, bf16[16,80,512]{2,1,0:T(8,128)(2,1)} %bitcast.186, bf16[2,512,1024]{2,1,0:T(8,128)(2,1)} %pad_maximum_fusion.up_ref, bf16[2,512,512]{2,1,0:T(8,128)(2,1)} %pad_maximum_fusion.6.down_ref), custom_call_target="tpu_custom_call" | custom-call | flops 4800000000 | bytes 8500000 | tf_op jit(solution)/shard_map/pallas_call | solution.py:129
  133.6 5.6 %all-to-all-start.3 = ((bf16[32,40,512]{2,1,0:T(8,128)(2,1)}), bf16[32,40,512]{2,1,0:T(8,128)(2,1)S(1)}, u32[]{:S(2)}, u32[]{:S(2)}) async-start(bf16[32,40,512]{2,1,0:T(8,128)(2,1)} %bitcast.185), calls=%async_computation.4 | async-start | bytes 2621440 | tf_op jit(solution)/shard_map/all_to_all | solution.py:249
  139.3 1.4 constant_dynamic-slice_fusion.6
  140.7 3.1 %collective-permute-start.11 = (bf16[8,40,512]{2,1,0:T(8,128)(2,1)S(1)}, bf16[8,40,512]{2,1,0:T(8,128)(2,1)S(1)}, u32[]{:S(2)}, u32[]{:S(2)}) collective-permute-start(bf16[8,40,512]{2,1,0:T(8,128)(2,1)S(1)} %get-tuple-element.21), channel_id=1, source_target_pairs={{0,2},{2,4},{4,6},{6,0},{1,3},{3,5},{5,7},{7,1},{8,10},{10,12},{12... | collective-permute-start | bytes 983048 | tf_op jit(solution)/shard_map/ppermute | solution.py:176
  143.8 4.3 %collective-permute-start.10 = (bf16[8,40,512]{2,1,0:T(8,128)(2,1)S(1)}, bf16[8,40,512]{2,1,0:T(8,128)(2,1)S(1)}, u32[]{:S(2)}, u32[]{:S(2)}) collective-permute-start(bf16[8,40,512]{2,1,0:T(8,128)(2,1)S(1)} %get-tuple-element.22), channel_id=1, source_target_pairs={{0,4},{2,6},{4,0},{6,2},{1,5},{3,7},{5,1},{7,3},{8,12},{10,14},{12... | collective-permute-start | bytes 983048 | tf_op jit(solution)/shard_map/ppermute | solution.py:176
  148.1 3.1 %collective-permute-start.9 = (bf16[8,40,512]{2,1,0:T(8,128)(2,1)S(1)}, bf16[8,40,512]{2,1,0:T(8,128)(2,1)S(1)}, u32[]{:S(2)}, u32[]{:S(2)}) collective-permute-start(bf16[8,40,512]{2,1,0:T(8,128)(2,1)S(1)} %get-tuple-element.23), channel_id=1, source_target_pairs={{0,6},{2,0},{4,2},{6,4},{1,7},{3,1},{5,3},{7,5},{8,14},{10,8},{12,... | collective-permute-start | bytes 983048 | tf_op jit(solution)/shard_map/ppermute | solution.py:176
  151.2 9.6 %collective-permute-done.11 = bf16[8,40,512]{2,1,0:T(8,128)(2,1)S(1)} collective-permute-done((bf16[8,40,512]{2,1,0:T(8,128)(2,1)S(1)}, bf16[8,40,512]{2,1,0:T(8,128)(2,1)S(1)}, u32[]{:S(2)}, u32[]{:S(2)}) %collective-permute-start.11) | collective-permute-done | bytes 327712 | tf_op jit(solution)/shard_map/ppermute | solution.py:176
  160.8 9.5 %collective-permute-done.10 = bf16[8,40,512]{2,1,0:T(8,128)(2,1)S(1)} collective-permute-done((bf16[8,40,512]{2,1,0:T(8,128)(2,1)S(1)}, bf16[8,40,512]{2,1,0:T(8,128)(2,1)S(1)}, u32[]{:S(2)}, u32[]{:S(2)}) %collective-permute-start.10) | collective-permute-done | bytes 327712 | tf_op jit(solution)/shard_map/ppermute | solution.py:176
  170.3 1.3 collective-permute-done.9
  172.3 1.9 convolution_add_fusion
  174.7 12.2 %all_gather.7 = bf16[512,512]{1,0:T(8,128)(2,1)S(1)} all-gather(bf16[128,512]{1,0:T(8,128)(2,1)S(1)} %convolution_convert_fusion.4), channel_id=1, replica_groups=mesh['dp'=8,'z'=8,'x'=4,'c'=2] {'x'}, dimensions={0}, use_global_device_ids=true | all-gather | bytes 655360 | tf_op jit(solution)/shard_map/all_gather | solution.py:265
  186.9 5.0 %collective-permute-start.12 = (bf16[512,512]{1,0:T(8,128)(2,1)S(1)}, bf16[512,512]{1,0:T(8,128)(2,1)S(1)}, u32[]{:S(2)}, u32[]{:S(2)}) collective-permute-start(bf16[512,512]{1,0:T(8,128)(2,1)S(1)} %all_gather.7), channel_id=1, source_target_pairs={{0,1},{1,0},{2,3},{3,2},{4,5},{5,4},{6,7},{7,6},{8,9},{9,8},{10,11... | collective-permute-start | bytes 1572872 | tf_op jit(solution)/shard_map/ppermute | solution.py:27
  193.8 2.3 collective-permute-start.13
  196.1 1.3 fusion.3
  197.4 11.5 %all-to-all-start.4 = ((bf16[64,8,512]{2,1,0:T(8,128)(2,1)}), bf16[64,8,512]{2,1,0:T(8,128)(2,1)S(1)}, u32[]{:S(2)}, u32[]{:S(2)}) async-start(bf16[64,8,512]{2,1,0:T(8,128)(2,1)} %fusion.3), calls=%async_computation.5 | async-start | bytes 1048576 | tf_op jit(solution)/shard_map/all_to_all | solution.py:270
  209.5 3.7 %collective-permute-start.14 = (bf16[2,128,512]{2,1,0:T(8,128)(2,1)S(1)}, bf16[2,128,512]{2,1,0:T(8,128)(2,1)S(1)}, u32[]{:S(2)}, u32[]{:S(2)}) collective-permute-start(bf16[2,128,512]{2,1,0:T(8,128)(2,1)S(1)} %pad_maximum_fusion.8), channel_id=1, source_target_pairs={{0,6},{2,0},{4,2},{6,4},{1,7},{3,1},{5,3},{7,5},{8,14},{10,8},{12,... | collective-permute-start | bytes 786440 | tf_op jit(solution)/shard_map/ppermute | solution.py:176
  213.2 2.5 %collective-permute-start.15 = (bf16[2,128,512]{2,1,0:T(8,128)(2,1)S(1)}, bf16[2,128,512]{2,1,0:T(8,128)(2,1)S(1)}, u32[]{:S(2)}, u32[]{:S(2)}) collective-permute-start(bf16[2,128,512]{2,1,0:T(8,128)(2,1)S(1)} %pad_maximum_fusion.9), channel_id=1, source_target_pairs={{0,4},{2,6},{4,0},{6,2},{1,5},{3,7},{5,1},{7,3},{8,12},{10,14},{12... | collective-permute-start | bytes 786440 | tf_op jit(solution)/shard_map/ppermute | solution.py:176
  215.7 1.9 collective-permute-start.16
  217.7 8.6 %all-to-all-done.4 = bf16[64,8,512]{2,1,0:T(8,128)(2,1)S(1)} async-done(((bf16[64,8,512]{2,1,0:T(8,128)(2,1)}), bf16[64,8,512]{2,1,0:T(8,128)(2,1)S(1)}, u32[]{:S(2)}, u32[]{:S(2)}) %all-to-all-start.4) | async-done | bytes 524320 | tf_op jit(solution)/shard_map/all_to_all | solution.py:270
  226.2 4.2 %collective-permute-done.16.b3_ref = bf16[2,128,512]{2,1,0:T(8,128)(2,1)S(1)} collective-permute-done((bf16[2,128,512]{2,1,0:T(8,128)(2,1)S(1)}, bf16[2,128,512]{2,1,0:T(8,128)(2,1)S(1)}, u32[]{:S(2)}, u32[]{:S(2)}) %collective-permute-start.16) | collective-permute-done | bytes 262176 | tf_op jit(solution)/shard_map/ppermute | solution.py:176
  230.5 3.3 %shard_map.96 = bf16[128,4096]{1,0:T(8,128)(2,1)} custom-call(s32[1,1024]{1,0:T(1,128)S(1)} %fusion.69.to_ref, bf16[128,512]{1,0:T(8,128)(2,1)S(1)} %get-tuple-element.16.near_ref, bf16[128,512]{1,0:T(8,128)(2,1)S(1)} %get-tuple-element.55.far_ref, bf16[2,128,512]{2,1,0:T(8,128)(2,1)S(1)} %collective-permute-done.14.b1_ref, ...), custom_call_target="tpu_custom_call" | custom-call | flops 1100000000 | bytes 2100000 | tf_op jit(solution)/shard_map/pallas_call | solution.py:80
  234.5 1.6 convert_element_type.146
  (88 shorter events, 12.9 us)
Async XLA Ops:
  7.2 70.1 %all-gather.2.cloned.1.call-start = ((), (), s32[]{:S(2)}) async-start(), calls=%async_computation.6 | async-start | bytes 1474560 | tf_op jit(solution)/shard_map/all_gather | solution.py:196
  7.3 1.2 copy-start
  8.5 12.7 %copy-start.6 = (s32[128,8]{0,1:T(8,128)S(1)}, s32[128,8]{0,1:T(8,128)}, u32[]{:S(2)}) copy-start(s32[128,8]{0,1:T(8,128)} %param.8) | copy-start | bytes 12292
  8.5 12.8 %copy-start.8 = (f32[128,8]{0,1:T(8,128)S(1)}, f32[128,8]{0,1:T(8,128)}, u32[]{:S(2)}) copy-start(f32[128,8]{0,1:T(8,128)} %param.9) | copy-start | bytes 12292
  8.5 13.3 %copy-start.5 = (bf16[128,512]{1,0:T(8,128)(2,1)S(1)}, bf16[128,512]{1,0:T(8,128)(2,1)}, u32[]{:S(2)}) copy-start(bf16[128,512]{1,0:T(8,128)(2,1)} %param.13) | copy-start | bytes 393220
  8.5 14.1 %copy-start.7 = (bf16[8,512]{1,0:T(8,128)(2,1)S(1)}, bf16[8,512]{1,0:T(8,128)(2,1)}, u32[]{:S(2)}) copy-start(bf16[8,512]{1,0:T(8,128)(2,1)} %param.12) | copy-start | bytes 24580
  12.5 22.0 %collective-permute-start = (bf16[4,128,512]{2,1,0:T(8,128)(2,1)S(1)}, bf16[4,128,512]{2,1,0:T(8,128)(2,1)S(1)}, u32[]{:S(2)}, u32[]{:S(2)}) collective-permute-start(bf16[4,128,512]{2,1,0:T(8,128)(2,1)S(1)} %get-tuple-element.11), channel_id=1, source_target_pairs={{0,1},{1,0},{2,3},{3,2},{4,5},{5,4},{6,7},{7,6},{8,9},{9,8},{10,11... | collective-permute-start | bytes 1572872 | tf_op jit(solution)/shard_map/ppermute | solution.py:27
  23.5 28.5 %all-to-all-start = ((bf16[64,8,512]{2,1,0:T(8,128)(2,1)}), bf16[64,8,512]{2,1,0:T(8,128)(2,1)S(1)}, u32[]{:S(2)}, u32[]{:S(2)}) async-start(bf16[64,8,512]{2,1,0:T(8,128)(2,1)} %broadcast_in_dim.59), calls=%async_computation | async-start | bytes 1048576 | tf_op jit(solution)/shard_map/all_to_all | solution.py:189
  34.5 10.2 %copy-start.4 = (bf16[1,512,512]{2,1,0:T(8,128)(2,1)S(1)}, bf16[1,512,512]{2,1,0:T(8,128)(2,1)}, u32[]{:S(2)}) copy-start(bf16[1,512,512]{2,1,0:T(8,128)(2,1)} %param.11) | copy-start | bytes 1572868
  34.6 15.2 %collective-permute-start.1 = (bf16[2,128,512]{2,1,0:T(8,128)(2,1)S(1)}, bf16[2,128,512]{2,1,0:T(8,128)(2,1)S(1)}, u32[]{:S(2)}, u32[]{:S(2)}) collective-permute-start(bf16[2,128,512]{2,1,0:T(8,128)(2,1)S(1)} %get-tuple-element.43), channel_id=1, source_target_pairs={{0,2},{2,4},{4,6},{6,0},{1,3},{3,5},{5,7},{7,1},{8,10},{10,12},{12... | collective-permute-start | bytes 786440 | tf_op jit(solution)/shard_map/ppermute | solution.py:176
  37.9 11.9 %collective-permute-start.3 = (bf16[2,128,512]{2,1,0:T(8,128)(2,1)S(1)}, bf16[2,128,512]{2,1,0:T(8,128)(2,1)S(1)}, u32[]{:S(2)}, u32[]{:S(2)}) collective-permute-start(bf16[2,128,512]{2,1,0:T(8,128)(2,1)S(1)} %get-tuple-element.44), channel_id=1, source_target_pairs={{0,6},{2,0},{4,2},{6,4},{1,7},{3,1},{5,3},{7,5},{8,14},{10,8},{12,... | collective-permute-start | bytes 786440 | tf_op jit(solution)/shard_map/ppermute | solution.py:176
  41.3 10.4 %collective-permute-start.2 = (bf16[2,128,512]{2,1,0:T(8,128)(2,1)S(1)}, bf16[2,128,512]{2,1,0:T(8,128)(2,1)S(1)}, u32[]{:S(2)}, u32[]{:S(2)}) collective-permute-start(bf16[2,128,512]{2,1,0:T(8,128)(2,1)S(1)} %get-tuple-element.45), channel_id=1, source_target_pairs={{0,4},{2,6},{4,0},{6,2},{1,5},{3,7},{5,1},{7,3},{8,12},{10,14},{12... | collective-permute-start | bytes 786440 | tf_op jit(solution)/shard_map/ppermute | solution.py:176
  44.7 16.3 %collective-permute-start.5 = (bf16[512,512]{1,0:T(8,128)(2,1)S(1)}, bf16[512,512]{1,0:T(8,128)(2,1)}, u32[]{:S(2)}, u32[]{:S(2)}) collective-permute-start(bf16[512,512]{1,0:T(8,128)(2,1)S(1)} %bitcast.193), channel_id=1, source_target_pairs={{0,1},{1,0},{2,3},{3,2},{4,5},{5,4},{6,7},{7,6},{8,9},{9,8},{10,11... | collective-permute-start | bytes 1572872 | tf_op jit(solution)/shard_map/ppermute | solution.py:27
  47.8 16.5 %collective-permute-start.4 = (bf16[512,1024]{1,0:T(8,128)(2,1)}, bf16[512,1024]{1,0:T(8,128)(2,1)}, u32[]{:S(2)}, u32[]{:S(2)}) collective-permute-start(bf16[512,1024]{1,0:T(8,128)(2,1)} %bitcast.15), channel_id=1, source_target_pairs={{0,1},{1,0},{2,3},{3,2},{4,5},{5,4},{6,7},{7,6},{8,9},{9,8},{10,11... | collective-permute-start | bytes 3145736 | tf_op jit(solution)/shard_map/ppermute | solution.py:27
  53.7 21.8 %all-to-all-start.1 = ((bf16[8,128,512]{2,1,0:T(8,128)(2,1)}), bf16[8,128,512]{2,1,0:T(8,128)(2,1)S(1)}, u32[]{:S(2)}, u32[]{:S(2)}) async-start(bf16[8,128,512]{2,1,0:T(8,128)(2,1)} %bitcast.189), calls=%async_computation.1 | async-start | bytes 2097152 | tf_op jit(solution)/shard_map/all_to_all | solution.py:212
  80.0 43.3 %all-to-all-start.2 = ((bf16[32,40,512]{2,1,0:T(8,128)(2,1)}), bf16[32,40,512]{2,1,0:T(8,128)(2,1)S(1)}, u32[]{:S(2)}, u32[]{:S(2)}) async-start(bf16[32,40,512]{2,1,0:T(8,128)(2,1)} %bitcast.14), calls=%async_computation.2 | async-start | bytes 2621440 | tf_op jit(solution)/shard_map/all_to_all | solution.py:224
  89.1 1.3 copy-start.3
  91.0 17.3 %collective-permute-start.6 = (bf16[8,40,512]{2,1,0:T(8,128)(2,1)S(1)}, bf16[8,40,512]{2,1,0:T(8,128)(2,1)S(1)}, u32[]{:S(2)}, u32[]{:S(2)}) collective-permute-start(bf16[8,40,512]{2,1,0:T(8,128)(2,1)S(1)} %get-tuple-element.29), channel_id=1, source_target_pairs={{0,2},{2,4},{4,6},{6,0},{1,3},{3,5},{5,7},{7,1},{8,10},{10,12},{12... | collective-permute-start | bytes 983048 | tf_op jit(solution)/shard_map/ppermute | solution.py:176
  94.2 19.1 %collective-permute-start.8 = (bf16[8,40,512]{2,1,0:T(8,128)(2,1)S(1)}, bf16[8,40,512]{2,1,0:T(8,128)(2,1)S(1)}, u32[]{:S(2)}, u32[]{:S(2)}) collective-permute-start(bf16[8,40,512]{2,1,0:T(8,128)(2,1)S(1)} %get-tuple-element.30), channel_id=1, source_target_pairs={{0,6},{2,0},{4,2},{6,4},{1,7},{3,1},{5,3},{7,5},{8,14},{10,8},{12,... | collective-permute-start | bytes 983048 | tf_op jit(solution)/shard_map/ppermute | solution.py:176
  97.5 24.3 %collective-permute-start.7 = (bf16[8,40,512]{2,1,0:T(8,128)(2,1)S(1)}, bf16[8,40,512]{2,1,0:T(8,128)(2,1)S(1)}, u32[]{:S(2)}, u32[]{:S(2)}) collective-permute-start(bf16[8,40,512]{2,1,0:T(8,128)(2,1)S(1)} %get-tuple-element.31), channel_id=1, source_target_pairs={{0,4},{2,6},{4,0},{6,2},{1,5},{3,7},{5,1},{7,3},{8,12},{10,14},{12... | collective-permute-start | bytes 983048 | tf_op jit(solution)/shard_map/ppermute | solution.py:176
  133.6 40.7 %all-to-all-start.3 = ((bf16[32,40,512]{2,1,0:T(8,128)(2,1)}), bf16[32,40,512]{2,1,0:T(8,128)(2,1)S(1)}, u32[]{:S(2)}, u32[]{:S(2)}) async-start(bf16[32,40,512]{2,1,0:T(8,128)(2,1)} %bitcast.185), calls=%async_computation.4 | async-start | bytes 2621440 | tf_op jit(solution)/shard_map/all_to_all | solution.py:249
  139.2 95.3 %reduce-scatter.2.cloned.1.call-start = ((), (), s32[]{:S(2)}) async-start(), calls=%async_computation.7 | async-start | bytes 2359296 | tf_op jit(solution)/shard_map/reduce_scatter | solution.py:260
  140.7 20.2 %collective-permute-start.11 = (bf16[8,40,512]{2,1,0:T(8,128)(2,1)S(1)}, bf16[8,40,512]{2,1,0:T(8,128)(2,1)S(1)}, u32[]{:S(2)}, u32[]{:S(2)}) collective-permute-start(bf16[8,40,512]{2,1,0:T(8,128)(2,1)S(1)} %get-tuple-element.21), channel_id=1, source_target_pairs={{0,2},{2,4},{4,6},{6,0},{1,3},{3,5},{5,7},{7,1},{8,10},{10,12},{12... | collective-permute-start | bytes 983048 | tf_op jit(solution)/shard_map/ppermute | solution.py:176
  143.8 26.5 %collective-permute-start.10 = (bf16[8,40,512]{2,1,0:T(8,128)(2,1)S(1)}, bf16[8,40,512]{2,1,0:T(8,128)(2,1)S(1)}, u32[]{:S(2)}, u32[]{:S(2)}) collective-permute-start(bf16[8,40,512]{2,1,0:T(8,128)(2,1)S(1)} %get-tuple-element.22), channel_id=1, source_target_pairs={{0,4},{2,6},{4,0},{6,2},{1,5},{3,7},{5,1},{7,3},{8,12},{10,14},{12... | collective-permute-start | bytes 983048 | tf_op jit(solution)/shard_map/ppermute | solution.py:176
  148.1 23.5 %collective-permute-start.9 = (bf16[8,40,512]{2,1,0:T(8,128)(2,1)S(1)}, bf16[8,40,512]{2,1,0:T(8,128)(2,1)S(1)}, u32[]{:S(2)}, u32[]{:S(2)}) collective-permute-start(bf16[8,40,512]{2,1,0:T(8,128)(2,1)S(1)} %get-tuple-element.23), channel_id=1, source_target_pairs={{0,6},{2,0},{4,2},{6,4},{1,7},{3,1},{5,3},{7,5},{8,14},{10,8},{12,... | collective-permute-start | bytes 983048 | tf_op jit(solution)/shard_map/ppermute | solution.py:176
  174.3 17.6 %copy-start.2 = (bf16[4,1,128,512]{3,2,1,0:T(8,128)(2,1)S(1)}, bf16[4,1,128,512]{3,2,1,0:T(8,128)(2,1)}, u32[]{:S(2)}) copy-start(bf16[4,1,128,512]{3,2,1,0:T(8,128)(2,1)} %get-tuple-element.37) | copy-start | bytes 1572868
  186.9 6.5 %collective-permute-start.12 = (bf16[512,512]{1,0:T(8,128)(2,1)S(1)}, bf16[512,512]{1,0:T(8,128)(2,1)S(1)}, u32[]{:S(2)}, u32[]{:S(2)}) collective-permute-start(bf16[512,512]{1,0:T(8,128)(2,1)S(1)} %all_gather.7), channel_id=1, source_target_pairs={{0,1},{1,0},{2,3},{3,2},{4,5},{5,4},{6,7},{7,6},{8,9},{9,8},{10,11... | collective-permute-start | bytes 1572872 | tf_op jit(solution)/shard_map/ppermute | solution.py:27
  192.3 3.8 %copy-start.1 = (bf16[4,1,128,512]{3,2,1,0:T(8,128)(2,1)S(1)}, bf16[4,1,128,512]{3,2,1,0:T(8,128)(2,1)}, u32[]{:S(2)}) copy-start(bf16[4,1,128,512]{3,2,1,0:T(8,128)(2,1)} %get-tuple-element.36) | copy-start | bytes 1572868
  193.8 15.6 %collective-permute-start.13 = (bf16[4,128,512]{2,1,0:T(8,128)(2,1)S(1)}, bf16[4,128,512]{2,1,0:T(8,128)(2,1)S(1)}, u32[]{:S(2)}, u32[]{:S(2)}) collective-permute-start(bf16[4,128,512]{2,1,0:T(8,128)(2,1)S(1)} %bitcast.192), channel_id=1, source_target_pairs={{0,1},{1,0},{2,3},{3,2},{4,5},{5,4},{6,7},{7,6},{8,9},{9,8},{10,11... | collective-permute-start | bytes 1572872 | tf_op jit(solution)/shard_map/ppermute | solution.py:27
  197.4 28.8 %all-to-all-start.4 = ((bf16[64,8,512]{2,1,0:T(8,128)(2,1)}), bf16[64,8,512]{2,1,0:T(8,128)(2,1)S(1)}, u32[]{:S(2)}, u32[]{:S(2)}) async-start(bf16[64,8,512]{2,1,0:T(8,128)(2,1)} %fusion.3), calls=%async_computation.5 | async-start | bytes 1048576 | tf_op jit(solution)/shard_map/all_to_all | solution.py:270
  209.5 16.7 %collective-permute-start.14 = (bf16[2,128,512]{2,1,0:T(8,128)(2,1)S(1)}, bf16[2,128,512]{2,1,0:T(8,128)(2,1)S(1)}, u32[]{:S(2)}, u32[]{:S(2)}) collective-permute-start(bf16[2,128,512]{2,1,0:T(8,128)(2,1)S(1)} %pad_maximum_fusion.8), channel_id=1, source_target_pairs={{0,6},{2,0},{4,2},{6,4},{1,7},{3,1},{5,3},{7,5},{8,14},{10,8},{12,... | collective-permute-start | bytes 786440 | tf_op jit(solution)/shard_map/ppermute | solution.py:176
  213.2 13.0 %collective-permute-start.15 = (bf16[2,128,512]{2,1,0:T(8,128)(2,1)S(1)}, bf16[2,128,512]{2,1,0:T(8,128)(2,1)S(1)}, u32[]{:S(2)}, u32[]{:S(2)}) collective-permute-start(bf16[2,128,512]{2,1,0:T(8,128)(2,1)S(1)} %pad_maximum_fusion.9), channel_id=1, source_target_pairs={{0,4},{2,6},{4,0},{6,2},{1,5},{3,7},{5,1},{7,3},{8,12},{10,14},{12... | collective-permute-start | bytes 786440 | tf_op jit(solution)/shard_map/ppermute | solution.py:176
  215.7 14.7 %collective-permute-start.16 = (bf16[2,128,512]{2,1,0:T(8,128)(2,1)S(1)}, bf16[2,128,512]{2,1,0:T(8,128)(2,1)S(1)}, u32[]{:S(2)}, u32[]{:S(2)}) collective-permute-start(bf16[2,128,512]{2,1,0:T(8,128)(2,1)S(1)} %pad_maximum_fusion.10), channel_id=1, source_target_pairs={{0,2},{2,4},{4,6},{6,0},{1,3},{3,5},{5,7},{7,1},{8,10},{10,12},{12... | collective-permute-start | bytes 786440 | tf_op jit(solution)/shard_map/ppermute | solution.py:176
Sparse Core Ops, SparseCore 0:
  22.8 46.0 all-gather.1
  174.4 51.7 reduce-scatter.1

commit v5 on v4

--- a/solution.py
+++ b/solution.py
@@ -62,7 +62,7 @@
         scratch_shapes=[pltpu.VMEM((1024, 1024), BF)],
         compiler_params=pltpu.CompilerParams(vmem_limit_bytes=32 * 1024 * 1024),
         cost_estimate=pl.CostEstimate(flops=1_100_000_000, bytes_accessed=2_100_000, transcendentals=0),
-    )(to, tokens)
+    )(to, pltpu.with_memory_space_constraint(tokens, pltpu.HBM))
 
 
 def join_kernel(to_ref, near_ref, far_ref, b1_ref, b2_ref, b3_ref, out_ref, pick_ref):
@@ -85,12 +85,87 @@
         out_shape=jax.ShapeDtypeStruct((rows, 4096), BF),
         scratch_shapes=[pltpu.VMEM((1024, 1024), BF)],
         compiler_params=pltpu.CompilerParams(vmem_limit_bytes=32 * 1024 * 1024),
-        cost_estimate=pl.CostEstimate(flops=1_100_000_000, bytes_accessed=2_100_000, transcendentals=0),
+        cost_estimate=pl.CostEstimate(flops=6_000_000_000, bytes_accessed=18_000_000, transcendentals=0),
     )(to, near, far, *others)
 
 
-def expert_kernel(x_ref, g_ref, up_ref, down_ref, back_ref, out_ref):
-    w_up, w_down = up_ref[0], down_ref[0]
+def cotangent_kernel(
+    expert_ref, place_ref, col_ref, s0_ref, s1_ref, s2_ref, s3_ref, hi_ref, mid_ref, wide_ref, fold_ref, before_ref
+):
+    @pl.when(pl.program_id(0) == 0)
+    def _():
+        row = lax.broadcasted_iota(jnp.int32, (2048, 128), 0)
+        lane = lax.broadcasted_iota(jnp.int32, (2048, 128), 1)
+        wide_ref[...] = jnp.where(lane == row // 64, 1.0, 0.0).astype(BF)
+        lane = lax.broadcasted_iota(jnp.int32, (160, 512), 1) % 64
+        fold_ref[...] = jnp.where(lane == expert_ref[...], 1.0, 0.0).astype(BF)
+        u = lax.broadcasted_iota(jnp.int32, (512, 512), 0)
+        t = lax.broadcasted_iota(jnp.int32, (512, 512), 1)
+        same = jnp.logical_and(u // 128 == t // 128, u < t)
+        before_ref[...] = jnp.where(same, 1.0, 0.0).astype(BF)
+
+    col = col_ref[...].reshape(512, 640)
+    spread = mm(wide_ref[...], col[:, 512:], ((1,), (1,)))
+    row = lax.broadcasted_iota(jnp.int32, (512, 512), 0) % 64
+    hit = spread[:512] == row.astype(F32)
+    fold = fold_ref[...]
+    named = mm(fold, jnp.where(hit, 1.0, 0.0).astype(BF))
+    rank = mm(named.astype(BF), before_ref[...])
+    send = jnp.logical_and(named > 0.5, rank == place_ref[...].astype(F32))
+    parts = []
+    for i in range(3):
+        part = mm(fold, jnp.where(hit, spread[512 * (i + 1) : 512 * (i + 2)], 0.0).astype(BF))
+        parts.append(jnp.where(send, part, 0.0).astype(BF))
+    for j in range(4):
+        one = [part[:, 128 * j : 128 * (j + 1)] for part in parts]
+        hi_ref[j], mid_ref[j] = one[0], one[1]
+        g = col[128 * j : 128 * (j + 1), :512]
+        total = mm(jnp.concatenate(one, axis=1), jnp.concatenate([g, g, g], axis=0))
+        for d, ref in enumerate((s0_ref, s1_ref, s2_ref, s3_ref)):
+            ref[j] = total[PAIR * d : PAIR * (d + 1)].astype(BF)
+
+
+def cotangent_rows(expert, place, column):
+    rows = column.shape[1]
+    step = lambda *shape: pl.BlockSpec((4,) + shape, lambda z: (z, 0, 0))
+    const = pl.BlockSpec((160, 1), lambda z: (0, 0))
+    sent = jax.ShapeDtypeStruct((8, PAIR, 512), BF)
+    weight = jax.ShapeDtypeStruct((8, 160, rows), BF)
+    return pl.pallas_call(
+        cotangent_kernel,
+        grid=(2,),
+        in_specs=[const, const, step(rows, 640)],
+        out_specs=[step(PAIR, 512)] * 4 + [step(160, rows)] * 2,
+        out_shape=[sent] * 4 + [weight] * 2,
+        scratch_shapes=[pltpu.VMEM((2048, 128), BF), pltpu.VMEM((160, 512), BF), pltpu.VMEM((512, 512), BF)],
+        compiler_params=pltpu.CompilerParams(vmem_limit_bytes=32 * 1024 * 1024),
+        cost_estimate=pl.CostEstimate(flops=1_000_000_000, bytes_accessed=3_000_000, transcendentals=0),
+    )(expert, place, pltpu.with_memory_space_constraint(column, pltpu.HBM))
+
+
+def expert_kernel(x_ref, g_ref, up1, down1, up2, down2, back_ref, out_ref, up_ref, down_ref, sems):
+    step = pl.program_id(0)
+    copies = [
+        [
+            pltpu.make_async_copy(up, up_ref.at[e], sems.at[e, 0]),
+            pltpu.make_async_copy(down, down_ref.at[e], sems.at[e, 1]),
+        ]
+        for e, (up, down) in enumerate(((up1, down1), (up2, down2)))
+    ]
+
+    @pl.when(step == 0)
+    def _():
+        for copy in copies[0] + copies[1]:
+            copy.start()
+        for copy in copies[0]:
+            copy.wait()
+
+    @pl.when(step == 3)
+    def _():
+        for copy in copies[1]:
+            copy.wait()
+
+    w_up, w_down = up_ref[step // 3], down_ref[step // 3]
     x = x_ref[...].reshape(256, 512)
     g = g_ref[...].reshape(256, 512)
     pre = mm(x, w_up)
@@ -105,7 +180,6 @@
     back = mm(grad_gate, w_up[:, :512], last) + mm(grad_up, w_up[:, 512:], last)
     back = back.astype(BF).reshape(16, 16, 512)
     out = mm(act, w_down).astype(BF).reshape(16, 16, 512)
-    step = pl.program_id(0)
 
     @pl.when(step != 3)
     def _():
@@ -119,7 +193,7 @@
         out_ref[...] = jnp.where(keep, out_ref[...].astype(F32), out.astype(F32)).astype(BF)
 
 
-def expert_rows(x, g, ups, downs):
+def expert_rows(x, g, *weights):
     def block(i):
         return (0, jnp.where(i == 0, 0, jnp.where(i == 1, 3, jnp.where(i < 4, 2, jnp.where(i == 4, 1, 4)))), 0)
 
@@ -132,14 +206,18 @@
         in_specs=[
             rows,
             rows,
-            pl.BlockSpec((1, 512, 1024), lambda i: (i // 3, 0, 0)),
-            pl.BlockSpec((1, 512, 512), lambda i: (i // 3, 0, 0)),
+            *[pl.BlockSpec(memory_space=pl.ANY)] * 4,
         ],
         out_specs=[rows, rows],
         out_shape=[shape, shape],
+        scratch_shapes=[
+            pltpu.VMEM((2, 512, 1024), BF),
+            pltpu.VMEM((2, 512, 512), BF),
+            pltpu.SemaphoreType.DMA((2, 2)),
+        ],
         compiler_params=pltpu.CompilerParams(vmem_limit_bytes=40 * 1024 * 1024),
         cost_estimate=pl.CostEstimate(flops=4_800_000_000, bytes_accessed=8_500_000, transcendentals=800_000),
-    )(x.reshape(16, 80, 512), hbm(g.reshape(16, 80, 512)), hbm(ups), hbm(downs))
+    )(x.reshape(16, 80, 512), hbm(g.reshape(16, 80, 512)), *map(hbm, weights))
     return back.reshape(32, PAIR, 512), out.reshape(32, PAIR, 512)
 
 
@@ -204,12 +282,17 @@
     tokens_mine = take(feature_block, core, 1).reshape(4 * rows, 512)
     tokens_other = take(feature_block, 1 - core, 1).reshape(4 * rows, 512)
 
-    gate_up2, down2 = swap_core(gate_up), swap_core(down)
-    ups = jnp.stack([gate_up, gate_up2])
-    downs = jnp.stack([down, down2])
+    gate_up2, down2 = swap_core(after(gate_up, w_part)), swap_core(after(down, w_part))
+    w_other = swap_core(w_part)
 
     partial = mm(feature_block.reshape(8 * rows, 512), w_part).astype(BF).reshape(8, rows, 512)
     partials = lax.all_to_all(partial, XC, split_axis=0, concat_axis=0, tiled=True)
+
+    r = lax.broadcasted_iota(jnp.int32, (4 * PAIR, 1), 0)
+    other, place = slot_layout(r % PAIR, at)
+    expert = plane * 8 + (at + r // PAIR) % 4 * 2 + (core + other) % 2
+    *grad_send, weight_hi, weight_mid = cotangent_rows(expert, place, column)
+    partials = after(partials, *grad_send)
     latent = jnp.sum(partials.astype(F32), axis=0).astype(BF)
 
     r = lax.broadcasted_iota(jnp.int32, (1, slots), 1)
@@ -220,41 +303,20 @@
     code = slot_code(jnp.any(named_in(routes), axis=1))
     onehot = (mm(code, spread) == place.astype(F32)).astype(BF)
     out_send = mm(onehot, latent, ((0,), (0,))).astype(BF).reshape(32, PAIR, 512)
-    out_send = after(out_send, column, ups, downs, tokens_mine, tokens_other)
+    out_send = after(out_send, gate_up2, down2, tokens_mine, tokens_other, w_other)
     recv = lax.all_to_all(out_send, ZX, split_axis=0, concat_axis=0, tiled=True)
 
-    r = lax.broadcasted_iota(jnp.int32, (1, 4 * PAIR), 1)
-    other, place = slot_layout(r % PAIR, at)
-    spread = (
-        lax.broadcasted_iota(jnp.int32, (64, 4 * PAIR), 0)
-        == plane * 8 + (at + r // PAIR) % 4 * 2 + (core + other) % 2
-    ).astype(BF)
-    hit = named_in(column[:, :, 512:520].astype(jnp.int32))
-    code = slot_code(jnp.any(hit, axis=2)).reshape(8 * rows, 64)
-    send = (mm(code, spread) == place.astype(F32)).reshape(8, rows, 4 * PAIR)
-    at_slot = 0.0
-    for i in (1, 2, 3):
-        piece = column[:, :, 512 + 8 * i : 520 + 8 * i].astype(F32)
-        piece = jnp.sum(jnp.where(hit, piece[..., None], 0.0), axis=2).astype(BF)
-        at_slot = at_slot + mm(piece.reshape(8 * rows, 64), spread)
-    weight = jnp.where(send, at_slot.reshape(8, rows, 4 * PAIR), 0.0)
-    picked = jnp.einsum(
-        "ztr,ztl->zrl", send.astype(BF), column[:, :, :512], preferred_element_type=F32
-    )
-    grad_send = (jnp.sum(weight, axis=1)[..., None] * picked).astype(BF).reshape(8, 4, PAIR, 512)
-    sent = jnp.stack([grad_send[:, 0]] + [shift_x(grad_send[:, d], d) for d in (1, 2, 3)])
+    sent = jnp.stack([grad_send[0]] + [shift_x(grad_send[d], d) for d in (1, 2, 3)])
     grad_recv = jnp.stack([take(sent, (at - j) % 4, 0) for j in range(4)], axis=1)
 
-    grad_rows, outputs = expert_rows(recv, grad_recv, ups, downs)
+    grad_rows, outputs = expert_rows(recv, grad_recv, gate_up, down, gate_up2, down2)
     grad_back = lax.all_to_all(grad_rows, ZX, split_axis=0, concat_axis=0, tiled=True)
 
     out4 = outputs.reshape(8, 4, PAIR, 512)
     back = [take(out4, at, 1)] + [shift_x(take(out4, (at - d) % 4, 1), -d) for d in (1, 2, 3)]
     back = jnp.stack(back, axis=1).reshape(8, 4 * PAIR, 512)
-    weight_hi = weight.astype(BF)
-    weight_lo = (weight - weight_hi.astype(F32)).astype(BF)
     mixed = sum(
-        jnp.einsum("ztr,zrl->ztl", w, back, preferred_element_type=F32) for w in (weight_hi, weight_lo)
+        jnp.einsum("zrt,zrl->ztl", w, back, preferred_element_type=F32) for w in (weight_hi, weight_mid)
     )
     mixed = mixed.reshape(8 * rows, 512)
     combined = lax.psum_scatter(mixed, "z", scatter_dimension=0, tiled=True).astype(BF)
@@ -271,7 +333,7 @@
 
     last = ((1,), (1,))
     near = mm(line_grads, w_part, last).astype(BF).reshape(4, rows, 512)
-    far = swap_core(mm(other_grads, w_part, last).astype(BF).reshape(4, rows, 512))
+    far = mm(line_grads, w_other, last).astype(BF).reshape(4, rows, 512)
     back = [take(near, at, 0), take(far, at, 0)]
     for d in (1, 2, 3):
         there = (at - d) % 4

time: 244 us -> 242 us (level)
  other arithmetic: 11.6 us -> 5.04 us
  Pallas kernels: 17.5 us -> 24 us
  local copies, waits for them, and re-layouts: 9.18 us -> 3.63 us
    ppermute x12, waiting for transfers between devices: 47.3 us -> 58.1 us  [shift_x(): return lax.ppermute(x, 'x', [(i, (i + d) % 4) for i in range(4)])]
    all_to_all x1, waiting for transfers between devices: 8.12 us -> 2.1 us  [shards(): lax.all_to_all(partial, XC, split_axis=0, concat_axis=0, tiled=True)]
    pallas_call x1 -> x2, Pallas kernels: 10.2 us -> 15.7 us  [the longest x1 11 us: expert_rows(): pl.pallas_call(expert_kernel, grid=(6,), in_specs=[rows, rows, *[pl.Block...]
    another operation x3 -> x1, other arithmetic: 5.41 us -> 0.16 us  [shards(): jnp.stack([grad_send[0]] + [shift_x(grad_send[d], d) for d in (1, 2, 3)])]
    all_to_all x1, waiting for transfers between devices: 8.55 us -> 5.46 us  [shards(): parts = lax.all_to_all(part, YZ, split_axis=0, concat_axis=0, tiled=True)]
    dot_general x12 -> x8, matrix products: 7.91 us -> 9.91 us  [mm(): return lax.dot_general(a, b, (dims, ((), ())), preferred_element_type=F32)]
  transfers between devices with their start and end apart: 24 -> 24, of which waited for: 11 -> 13; matrix products, arithmetic and copies ran while one was open for 11% -> 8% of each run, Pallas kernels for 1% -> 3%
where the time goes in v5:
time: 242 us; the launch traced here: 241 us
  starting transfers between devices  103 us (43%)
  waiting for transfers between devices  66.7 us (28%)
  Pallas kernels  24 us (10%)
  between operations  14.6 us (6%)
  matrix products  12.3 us (5%)
  blocking collectives  11.4 us (5%)
  other arithmetic  5.04 us (2%)
  local copies, waits for them, and re-layouts  3.63 us (2%)
    ppermute x12, waiting for transfers between devices, shift_x(): return lax.ppermute(x, 'x', [(i, (i + d) % 4) for i in range(4)])  58.1 us
    ppermute x12, starting transfers between devices, shift_x(): return lax.ppermute(x, 'x', [(i, (i + d) % 4) for i in range(4)])  39.2 us
    ppermute x5, starting transfers between devices, swap_core(): return lax.ppermute(x, 'c', [(0, 1), (1, 0)])  19.4 us
    all_to_all x1, starting transfers between devices, shards(): parts = lax.all_to_all(part, YZ, split_axis=0, concat_axis=0, tiled=True)  11.7 us
    all_gather x1, blocking collectives, shards(): line_grads = lax.all_gather(grad_latent, 'x', axis=0, tiled=True)  11.4 us
    all_to_all x1, starting transfers between devices, shards(): lax.all_to_all(jnp.broadcast_to(w_in[None], (64,) + w_in.shape), YZ, spli...  11.2 us
    pallas_call x1, Pallas kernels, expert_rows(): pl.pallas_call(expert_kernel, grid=(6,), in_specs=[rows, rows, *[pl.Block...  11 us
    dot_general x8, matrix products, mm(): return lax.dot_general(a, b, (dims, ((), ())), preferred_element_type=F32)  9.91 us
  transfers between devices with their start and end apart: 24, of which 13 were waited for; matrix products, arithmetic and copies ran while one was open for 8% of the time, Pallas kernels for 3%

profile of v5, /device:TPU:1, one launch (start us, length us, event | category | flops | bytes accessed | tf_op | source)
XLA Modules:
  0.0 240.7 jit_solution(17195204047984341213)
XLA Ops:
  7.3 4.9 %shard_map.95 = (bf16[4,128,512]{2,1,0:T(8,128)(2,1)S(1)}, bf16[4,128,512]{2,1,0:T(8,128)(2,1)S(1)}) custom-call(s32[1,1024]{1,0:T(1,128)S(1)} %fusion.63.to_ref, bf16[128,4096]{1,0:T(8,128)(2,1)} %tokens_ref.1), custom_call_target="tpu_custom_call" | custom-call | flops 1100000000 | bytes 2100000 | tf_op jit(solution)/shard_map/pallas_call | solution.py:56
  12.3 8.8 %collective-permute-start = (bf16[4,128,512]{2,1,0:T(8,128)(2,1)S(1)}, bf16[4,128,512]{2,1,0:T(8,128)(2,1)S(1)}, u32[]{:S(2)}, u32[]{:S(2)}) collective-permute-start(bf16[4,128,512]{2,1,0:T(8,128)(2,1)S(1)} %get-tuple-element.21), channel_id=1, source_target_pairs={{0,1},{1,0},{2,3},{3,2},{4,5},{5,4},{6,7},{7,6},{8,9},{9,8},{10,11... | collective-permute-start | bytes 1572872 | tf_op jit(solution)/shard_map/ppermute | solution.py:27
  23.3 11.2 %all-to-all-start = ((bf16[64,8,512]{2,1,0:T(8,128)(2,1)}), bf16[64,8,512]{2,1,0:T(8,128)(2,1)}, u32[]{:S(2)}, u32[]{:S(2)}) async-start(bf16[64,8,512]{2,1,0:T(8,128)(2,1)} %broadcast_in_dim.16), calls=%async_computation | async-start | bytes 1048576 | tf_op jit(solution)/shard_map/all_to_all | solution.py:267
  34.7 3.1 %collective-permute-start.1 = (bf16[2,128,512]{2,1,0:T(8,128)(2,1)S(1)}, bf16[2,128,512]{2,1,0:T(8,128)(2,1)S(1)}, u32[]{:S(2)}, u32[]{:S(2)}) collective-permute-start(bf16[2,128,512]{2,1,0:T(8,128)(2,1)S(1)} %get-tuple-element.50), channel_id=1, source_target_pairs={{0,2},{2,4},{4,6},{6,0},{1,3},{3,5},{5,7},{7,1},{8,10},{10,12},{12... | collective-permute-start | bytes 786440 | tf_op jit(solution)/shard_map/ppermute | solution.py:254
  37.8 3.4 %collective-permute-start.3 = (bf16[2,128,512]{2,1,0:T(8,128)(2,1)S(1)}, bf16[2,128,512]{2,1,0:T(8,128)(2,1)S(1)}, u32[]{:S(2)}, u32[]{:S(2)}) collective-permute-start(bf16[2,128,512]{2,1,0:T(8,128)(2,1)S(1)} %get-tuple-element.51), channel_id=1, source_target_pairs={{0,6},{2,0},{4,2},{6,4},{1,7},{3,1},{5,3},{7,5},{8,14},{10,8},{12,... | collective-permute-start | bytes 786440 | tf_op jit(solution)/shard_map/ppermute | solution.py:254
  41.2 3.4 %collective-permute-start.2 = (bf16[2,128,512]{2,1,0:T(8,128)(2,1)S(1)}, bf16[2,128,512]{2,1,0:T(8,128)(2,1)S(1)}, u32[]{:S(2)}, u32[]{:S(2)}) collective-permute-start(bf16[2,128,512]{2,1,0:T(8,128)(2,1)S(1)} %get-tuple-element.52), channel_id=1, source_target_pairs={{0,4},{2,6},{4,0},{6,2},{1,5},{3,7},{5,1},{7,3},{8,12},{10,14},{12... | collective-permute-start | bytes 786440 | tf_op jit(solution)/shard_map/ppermute | solution.py:254
  45.5 1.6 collective-permute-done.3
  47.1 4.6 %collective-permute-done.2 = bf16[2,128,512]{2,1,0:T(8,128)(2,1)S(1)} collective-permute-done((bf16[2,128,512]{2,1,0:T(8,128)(2,1)S(1)}, bf16[2,128,512]{2,1,0:T(8,128)(2,1)S(1)}, u32[]{:S(2)}, u32[]{:S(2)}) %collective-permute-start.2) | collective-permute-done | bytes 262176 | tf_op jit(solution)/shard_map/ppermute | solution.py:254
  52.1 2.7 %convolution_convert_fusion.1 = bf16[1024,512]{1,0:T(8,128)(2,1)} fusion(bf16[1024,512]{1,0:T(8,128)(2,1)S(1)} %bitcast.92, bf16[64,8,512]{2,1,0:T(8,128)(2,1)} %all-to-all-done), kind=kOutput, calls=%fused_computation.3 | convolution fusion | flops 537395200 | bytes 2621440 | tf_op jit(solution)/shard_map/dot_general | solution.py:19
  54.8 6.6 %all-to-all-start.1 = ((bf16[8,128,512]{2,1,0:T(8,128)(2,1)}), bf16[8,128,512]{2,1,0:T(8,128)(2,1)S(1)}, u32[]{:S(2)}, u32[]{:S(2)}) async-start(bf16[8,128,512]{2,1,0:T(8,128)(2,1)} %bitcast.11), calls=%async_computation.1 | async-start | bytes 2097152 | tf_op jit(solution)/shard_map/all_to_all | solution.py:289
  61.4 1.9 collective-permute-start.4
  63.9 2.4 collective-permute-start.6
  66.3 1.9 collective-permute-start.5
  68.5 1.1 constant_dynamic-slice_fusion.7
  69.6 4.8 %shard_map.94 = (bf16[8,40,512]{2,1,0:T(8,128)(2,1)S(1)}, bf16[8,40,512]{2,1,0:T(8,128)(2,1)S(1)}, bf16[8,40,512]{2,1,0:T(8,128)(2,1)S(1)}, bf16[8,40,512]{2,1,0...) custom-call(s32[160,1]{1,0:T(8,128)S(1)} %get-tuple-element.68.expert_ref, ...), custom_call_target="tpu_custom_call" | custom-call | flops 1000000000 | bytes 3000000 | tf_op jit(solution)/shard_map/pallas_call | solution.py:134
  74.4 2.1 all-to-all-done.1
  76.6 1.6 convolution_convert_fusion
  78.3 7.4 %all-to-all-start.2 = ((bf16[32,40,512]{2,1,0:T(8,128)(2,1)}), bf16[32,40,512]{2,1,0:T(8,128)(2,1)S(1)}, u32[]{:S(2)}, u32[]{:S(2)}) async-start(bf16[32,40,512]{2,1,0:T(8,128)(2,1)} %bitcast.91), calls=%async_computation.2 | async-start | bytes 2621440 | tf_op jit(solution)/shard_map/all_to_all | solution.py:307
  85.7 3.1 %collective-permute-start.7 = (bf16[8,40,512]{2,1,0:T(8,128)(2,1)S(1)}, bf16[8,40,512]{2,1,0:T(8,128)(2,1)S(1)}, u32[]{:S(2)}, u32[]{:S(2)}) collective-permute-start(bf16[8,40,512]{2,1,0:T(8,128)(2,1)S(1)} %get-tuple-element.23), channel_id=1, source_target_pairs={{0,2},{2,4},{4,6},{6,0},{1,3},{3,5},{5,7},{7,1},{8,10},{10,12},{12... | collective-permute-start | bytes 983048 | tf_op jit(solution)/shard_map/ppermute | solution.py:254
  88.8 4.3 %collective-permute-start.8 = (bf16[8,40,512]{2,1,0:T(8,128)(2,1)S(1)}, bf16[8,40,512]{2,1,0:T(8,128)(2,1)S(1)}, u32[]{:S(2)}, u32[]{:S(2)}) collective-permute-start(bf16[8,40,512]{2,1,0:T(8,128)(2,1)S(1)} %get-tuple-element.24), channel_id=1, source_target_pairs={{0,4},{2,6},{4,0},{6,2},{1,5},{3,7},{5,1},{7,3},{8,12},{10,14},{12... | collective-permute-start | bytes 983048 | tf_op jit(solution)/shard_map/ppermute | solution.py:254
  93.1 3.1 %collective-permute-start.9 = (bf16[8,40,512]{2,1,0:T(8,128)(2,1)S(1)}, bf16[8,40,512]{2,1,0:T(8,128)(2,1)S(1)}, u32[]{:S(2)}, u32[]{:S(2)}) collective-permute-start(bf16[8,40,512]{2,1,0:T(8,128)(2,1)S(1)} %get-tuple-element.25), channel_id=1, source_target_pairs={{0,6},{2,0},{4,2},{6,4},{1,7},{3,1},{5,3},{7,5},{8,14},{10,8},{12,... | collective-permute-start | bytes 983048 | tf_op jit(solution)/shard_map/ppermute | solution.py:254
  96.2 9.3 %collective-permute-done.7 = bf16[8,40,512]{2,1,0:T(8,128)(2,1)S(1)} collective-permute-done((bf16[8,40,512]{2,1,0:T(8,128)(2,1)S(1)}, bf16[8,40,512]{2,1,0:T(8,128)(2,1)S(1)}, u32[]{:S(2)}, u32[]{:S(2)}) %collective-permute-start.7) | collective-permute-done | bytes 327712 | tf_op jit(solution)/shard_map/ppermute | solution.py:254
  105.6 10.8 %collective-permute-done.8 = bf16[8,40,512]{2,1,0:T(8,128)(2,1)S(1)} collective-permute-done((bf16[8,40,512]{2,1,0:T(8,128)(2,1)S(1)}, bf16[8,40,512]{2,1,0:T(8,128)(2,1)S(1)}, u32[]{:S(2)}, u32[]{:S(2)}) %collective-permute-start.8) | collective-permute-done | bytes 327712 | tf_op jit(solution)/shard_map/ppermute | solution.py:254
  116.4 2.4 collective-permute-done.9
  119.1 1.2 pad_maximum_fusion.1
  120.3 11.0 %shard_map.96 = (bf16[16,80,512]{2,1,0:T(8,128)(2,1)}, bf16[16,80,512]{2,1,0:T(8,128)(2,1)}) custom-call(bf16[16,80,512]{2,1,0:T(8,128)(2,1)S(1)} %bitcast.85, bf16[16,80,512]{2,1,0:T(8,128)(2,1)} %bitcast.98, bf16[512,1024]{1,0:T(8,128)(2,1)} %bitcast.111, bf16[512,512]{1,0:T(8,128)(2,1)} %bitcast.14.down1, bf16[512,1024]{1,0:T(8,128)(2,1)} %collective-permute-done.4.up2, ...), custom_call_target="tpu_custom_call" | custom-call | flops 4800000000 | bytes 8500000 | tf_op jit(solution)/shard_map/pallas_call | solution.py:203
  131.3 7.3 %all-to-all-start.3 = ((bf16[32,40,512]{2,1,0:T(8,128)(2,1)}), bf16[32,40,512]{2,1,0:T(8,128)(2,1)S(1)}, u32[]{:S(2)}, u32[]{:S(2)}) async-start(bf16[32,40,512]{2,1,0:T(8,128)(2,1)} %bitcast.97), calls=%async_computation.4 | async-start | bytes 2621440 | tf_op jit(solution)/shard_map/all_to_all | solution.py:313
  138.8 3.1 %collective-permute-start.12 = (bf16[8,40,512]{2,1,0:T(8,128)(2,1)S(1)}, bf16[8,40,512]{2,1,0:T(8,128)(2,1)S(1)}, u32[]{:S(2)}, u32[]{:S(2)}) collective-permute-start(bf16[8,40,512]{2,1,0:T(8,128)(2,1)S(1)} %get-tuple-element.36), channel_id=1, source_target_pairs={{0,2},{2,4},{4,6},{6,0},{1,3},{3,5},{5,7},{7,1},{8,10},{10,12},{12... | collective-permute-start | bytes 983048 | tf_op jit(solution)/shard_map/ppermute | solution.py:254
  141.9 4.3 %collective-permute-start.11 = (bf16[8,40,512]{2,1,0:T(8,128)(2,1)S(1)}, bf16[8,40,512]{2,1,0:T(8,128)(2,1)S(1)}, u32[]{:S(2)}, u32[]{:S(2)}) collective-permute-start(bf16[8,40,512]{2,1,0:T(8,128)(2,1)S(1)} %get-tuple-element.37), channel_id=1, source_target_pairs={{0,4},{2,6},{4,0},{6,2},{1,5},{3,7},{5,1},{7,3},{8,12},{10,14},{12... | collective-permute-start | bytes 983048 | tf_op jit(solution)/shard_map/ppermute | solution.py:254
  146.2 3.3 %collective-permute-start.10 = (bf16[8,40,512]{2,1,0:T(8,128)(2,1)S(1)}, bf16[8,40,512]{2,1,0:T(8,128)(2,1)S(1)}, u32[]{:S(2)}, u32[]{:S(2)}) collective-permute-start(bf16[8,40,512]{2,1,0:T(8,128)(2,1)S(1)} %get-tuple-element.38), channel_id=1, source_target_pairs={{0,6},{2,0},{4,2},{6,4},{1,7},{3,1},{5,3},{7,5},{8,14},{10,8},{12,... | collective-permute-start | bytes 983048 | tf_op jit(solution)/shard_map/ppermute | solution.py:254
  149.5 6.9 %collective-permute-done.12 = bf16[8,40,512]{2,1,0:T(8,128)(2,1)S(1)} collective-permute-done((bf16[8,40,512]{2,1,0:T(8,128)(2,1)S(1)}, bf16[8,40,512]{2,1,0:T(8,128)(2,1)S(1)}, u32[]{:S(2)}, u32[]{:S(2)}) %collective-permute-start.12) | collective-permute-done | bytes 327712 | tf_op jit(solution)/shard_map/ppermute | solution.py:254
  156.4 13.0 %collective-permute-done.11 = bf16[8,40,512]{2,1,0:T(8,128)(2,1)S(1)} collective-permute-done((bf16[8,40,512]{2,1,0:T(8,128)(2,1)S(1)}, bf16[8,40,512]{2,1,0:T(8,128)(2,1)S(1)}, u32[]{:S(2)}, u32[]{:S(2)}) %collective-permute-start.11) | collective-permute-done | bytes 327712 | tf_op jit(solution)/shard_map/ppermute | solution.py:254
  169.4 2.1 collective-permute-done.10
  172.2 1.9 convolution_add_fusion
  174.5 11.4 %all_gather.7 = bf16[512,512]{1,0:T(8,128)(2,1)S(1)} all-gather(bf16[128,512]{1,0:T(8,128)(2,1)S(1)} %convolution_convert_fusion.4), channel_id=1, replica_groups=mesh['dp'=8,'z'=8,'x'=4,'c'=2] {'x'}, dimensions={0}, use_global_device_ids=true | all-gather | bytes 655360 | tf_op jit(solution)/shard_map/all_gather | solution.py:327
  185.9 4.4 %collective-permute-start.13 = (bf16[512,512]{1,0:T(8,128)(2,1)S(1)}, bf16[512,512]{1,0:T(8,128)(2,1)S(1)}, u32[]{:S(2)}, u32[]{:S(2)}) collective-permute-start(bf16[512,512]{1,0:T(8,128)(2,1)S(1)} %all_gather.7), channel_id=1, source_target_pairs={{0,1},{1,0},{2,3},{3,2},{4,5},{5,4},{6,7},{7,6},{8,9},{9,8},{10,11... | collective-permute-start | bytes 1572872 | tf_op jit(solution)/shard_map/ppermute | solution.py:27
  190.8 1.0 collective-permute-done.13
  191.8 1.3 fusion.1
  193.1 11.7 %all-to-all-start.4 = ((bf16[64,8,512]{2,1,0:T(8,128)(2,1)}), bf16[64,8,512]{2,1,0:T(8,128)(2,1)S(1)}, u32[]{:S(2)}, u32[]{:S(2)}) async-start(bf16[64,8,512]{2,1,0:T(8,128)(2,1)} %fusion.1), calls=%async_computation.5 | async-start | bytes 1048576 | tf_op jit(solution)/shard_map/all_to_all | solution.py:332
  204.8 1.5 convolution_convert_fusion.3
  206.4 1.5 convolution_convert_fusion.2
  208.0 3.6 %collective-permute-start.14 = (bf16[2,128,512]{2,1,0:T(8,128)(2,1)S(1)}, bf16[2,128,512]{2,1,0:T(8,128)(2,1)S(1)}, u32[]{:S(2)}, u32[]{:S(2)}) collective-permute-start(bf16[2,128,512]{2,1,0:T(8,128)(2,1)S(1)} %pad_maximum_fusion.6), channel_id=1, source_target_pairs={{0,6},{2,0},{4,2},{6,4},{1,7},{3,1},{5,3},{7,5},{8,14},{10,8},{12,... | collective-permute-start | bytes 786440 | tf_op jit(solution)/shard_map/ppermute | solution.py:254
  211.6 2.5 %collective-permute-start.15 = (bf16[2,128,512]{2,1,0:T(8,128)(2,1)S(1)}, bf16[2,128,512]{2,1,0:T(8,128)(2,1)S(1)}, u32[]{:S(2)}, u32[]{:S(2)}) collective-permute-start(bf16[2,128,512]{2,1,0:T(8,128)(2,1)S(1)} %pad_maximum_fusion.7), channel_id=1, source_target_pairs={{0,4},{2,6},{4,0},{6,2},{1,5},{3,7},{5,1},{7,3},{8,12},{10,14},{12... | collective-permute-start | bytes 786440 | tf_op jit(solution)/shard_map/ppermute | solution.py:254
  214.2 1.9 collective-permute-start.16
  216.1 5.5 %all-to-all-done.4 = bf16[64,8,512]{2,1,0:T(8,128)(2,1)S(1)} async-done(((bf16[64,8,512]{2,1,0:T(8,128)(2,1)}), bf16[64,8,512]{2,1,0:T(8,128)(2,1)S(1)}, u32[]{:S(2)}, u32[]{:S(2)}) %all-to-all-start.4) | async-done | bytes 524320 | tf_op jit(solution)/shard_map/all_to_all | solution.py:332
  222.3 6.6 %collective-permute-done.16.b3_ref = bf16[2,128,512]{2,1,0:T(8,128)(2,1)S(1)} collective-permute-done((bf16[2,128,512]{2,1,0:T(8,128)(2,1)S(1)}, bf16[2,128,512]{2,1,0:T(8,128)(2,1)S(1)}, u32[]{:S(2)}, u32[]{:S(2)}) %collective-permute-start.16) | collective-permute-done | bytes 262176 | tf_op jit(solution)/shard_map/ppermute | solution.py:254
  228.9 3.3 %shard_map.97 = bf16[128,4096]{1,0:T(8,128)(2,1)} custom-call(s32[1,1024]{1,0:T(1,128)S(1)} %fusion.63.to_ref, bf16[128,512]{1,0:T(8,128)(2,1)S(1)} %get-tuple-element.34.near_ref, bf16[128,512]{1,0:T(8,128)(2,1)S(1)} %get-tuple-element.62.far_ref, bf16[2,128,512]{2,1,0:T(8,128)(2,1)S(1)} %collective-permute-done.14.b1_ref, ...), custom_call_target="tpu_custom_call" | custom-call | flops 6000000000 | bytes 18000000 | tf_op jit(solution)/shard_map/pallas_call | solution.py:80
  232.2 1.6 convert_element_type.70
  (64 shorter events, 7.4 us)
Async XLA Ops:
  7.2 62.5 %all-gather.2.cloned.1.call-start = ((), (), s32[]{:S(2)}) async-start(), calls=%async_computation.6 | async-start | bytes 1474560 | tf_op jit(solution)/shard_map/all_gather | solution.py:274
  7.3 13.8 %copy-start.4 = (s32[128,8]{0,1:T(8,128)S(1)}, s32[128,8]{0,1:T(8,128)}, u32[]{:S(2)}) copy-start(s32[128,8]{0,1:T(8,128)} %param.8) | copy-start | bytes 12292
  7.3 13.8 %copy-start.6 = (f32[128,8]{0,1:T(8,128)S(1)}, f32[128,8]{0,1:T(8,128)}, u32[]{:S(2)}) copy-start(f32[128,8]{0,1:T(8,128)} %param.9) | copy-start | bytes 12292
  7.3 14.3 %copy-start.3 = (bf16[128,512]{1,0:T(8,128)(2,1)S(1)}, bf16[128,512]{1,0:T(8,128)(2,1)}, u32[]{:S(2)}) copy-start(bf16[128,512]{1,0:T(8,128)(2,1)} %param.13) | copy-start | bytes 393220
  7.3 15.1 %copy-start.5 = (bf16[8,512]{1,0:T(8,128)(2,1)S(1)}, bf16[8,512]{1,0:T(8,128)(2,1)}, u32[]{:S(2)}) copy-start(bf16[8,512]{1,0:T(8,128)(2,1)} %param.12) | copy-start | bytes 24580
  12.3 22.2 %collective-permute-start = (bf16[4,128,512]{2,1,0:T(8,128)(2,1)S(1)}, bf16[4,128,512]{2,1,0:T(8,128)(2,1)S(1)}, u32[]{:S(2)}, u32[]{:S(2)}) collective-permute-start(bf16[4,128,512]{2,1,0:T(8,128)(2,1)S(1)} %get-tuple-element.21), channel_id=1, source_target_pairs={{0,1},{1,0},{2,3},{3,2},{4,5},{5,4},{6,7},{7,6},{8,9},{9,8},{10,11... | collective-permute-start | bytes 1572872 | tf_op jit(solution)/shard_map/ppermute | solution.py:27
  23.3 28.8 %all-to-all-start = ((bf16[64,8,512]{2,1,0:T(8,128)(2,1)}), bf16[64,8,512]{2,1,0:T(8,128)(2,1)}, u32[]{:S(2)}, u32[]{:S(2)}) async-start(bf16[64,8,512]{2,1,0:T(8,128)(2,1)} %broadcast_in_dim.16), calls=%async_computation | async-start | bytes 1048576 | tf_op jit(solution)/shard_map/all_to_all | solution.py:267
  34.7 10.8 %collective-permute-start.1 = (bf16[2,128,512]{2,1,0:T(8,128)(2,1)S(1)}, bf16[2,128,512]{2,1,0:T(8,128)(2,1)S(1)}, u32[]{:S(2)}, u32[]{:S(2)}) collective-permute-start(bf16[2,128,512]{2,1,0:T(8,128)(2,1)S(1)} %get-tuple-element.50), channel_id=1, source_target_pairs={{0,2},{2,4},{4,6},{6,0},{1,3},{3,5},{5,7},{7,1},{8,10},{10,12},{12... | collective-permute-start | bytes 786440 | tf_op jit(solution)/shard_map/ppermute | solution.py:254
  37.8 9.3 %collective-permute-start.3 = (bf16[2,128,512]{2,1,0:T(8,128)(2,1)S(1)}, bf16[2,128,512]{2,1,0:T(8,128)(2,1)S(1)}, u32[]{:S(2)}, u32[]{:S(2)}) collective-permute-start(bf16[2,128,512]{2,1,0:T(8,128)(2,1)S(1)} %get-tuple-element.51), channel_id=1, source_target_pairs={{0,6},{2,0},{4,2},{6,4},{1,7},{3,1},{5,3},{7,5},{8,14},{10,8},{12,... | collective-permute-start | bytes 786440 | tf_op jit(solution)/shard_map/ppermute | solution.py:254
  41.2 10.5 %collective-permute-start.2 = (bf16[2,128,512]{2,1,0:T(8,128)(2,1)S(1)}, bf16[2,128,512]{2,1,0:T(8,128)(2,1)S(1)}, u32[]{:S(2)}, u32[]{:S(2)}) collective-permute-start(bf16[2,128,512]{2,1,0:T(8,128)(2,1)S(1)} %get-tuple-element.52), channel_id=1, source_target_pairs={{0,4},{2,6},{4,0},{6,2},{1,5},{3,7},{5,1},{7,3},{8,12},{10,14},{12... | collective-permute-start | bytes 786440 | tf_op jit(solution)/shard_map/ppermute | solution.py:254
  54.8 21.7 %all-to-all-start.1 = ((bf16[8,128,512]{2,1,0:T(8,128)(2,1)}), bf16[8,128,512]{2,1,0:T(8,128)(2,1)S(1)}, u32[]{:S(2)}, u32[]{:S(2)}) async-start(bf16[8,128,512]{2,1,0:T(8,128)(2,1)} %bitcast.11), calls=%async_computation.1 | async-start | bytes 2097152 | tf_op jit(solution)/shard_map/all_to_all | solution.py:289
  61.4 16.9 %collective-permute-start.4 = (bf16[512,1024]{1,0:T(8,128)(2,1)}, bf16[512,1024]{1,0:T(8,128)(2,1)}, u32[]{:S(2)}, u32[]{:S(2)}) collective-permute-start(bf16[512,1024]{1,0:T(8,128)(2,1)} %bitcast.110), channel_id=1, source_target_pairs={{0,1},{1,0},{2,3},{3,2},{4,5},{5,4},{6,7},{7,6},{8,9},{9,8},{10,11... | collective-permute-start | bytes 3145736 | tf_op jit(solution)/shard_map/ppermute | solution.py:27
  63.9 14.4 %collective-permute-start.6 = (bf16[512,512]{1,0:T(8,128)(2,1)}, bf16[512,512]{1,0:T(8,128)(2,1)}, u32[]{:S(2)}, u32[]{:S(2)}) collective-permute-start(bf16[512,512]{1,0:T(8,128)(2,1)} %bitcast.10), channel_id=1, source_target_pairs={{0,1},{1,0},{2,3},{3,2},{4,5},{5,4},{6,7},{7,6},{8,9},{9,8},{10,11... | collective-permute-start | bytes 1572872 | tf_op jit(solution)/shard_map/ppermute | solution.py:27
  66.3 12.0 %collective-permute-start.5 = (bf16[512,512]{1,0:T(8,128)(2,1)}, bf16[512,512]{1,0:T(8,128)(2,1)}, u32[]{:S(2)}, u32[]{:S(2)}) collective-permute-start(bf16[512,512]{1,0:T(8,128)(2,1)} %bitcast.14.down1), channel_id=1, source_target_pairs={{0,1},{1,0},{2,3},{3,2},{4,5},{5,4},{6,7},{7,6},{8,9},{9,8},{10,11... | collective-permute-start | bytes 1572872 | tf_op jit(solution)/shard_map/ppermute | solution.py:27
  78.3 42.0 %all-to-all-start.2 = ((bf16[32,40,512]{2,1,0:T(8,128)(2,1)}), bf16[32,40,512]{2,1,0:T(8,128)(2,1)S(1)}, u32[]{:S(2)}, u32[]{:S(2)}) async-start(bf16[32,40,512]{2,1,0:T(8,128)(2,1)} %bitcast.91), calls=%async_computation.2 | async-start | bytes 2621440 | tf_op jit(solution)/shard_map/all_to_all | solution.py:307
  85.7 19.9 %collective-permute-start.7 = (bf16[8,40,512]{2,1,0:T(8,128)(2,1)S(1)}, bf16[8,40,512]{2,1,0:T(8,128)(2,1)S(1)}, u32[]{:S(2)}, u32[]{:S(2)}) collective-permute-start(bf16[8,40,512]{2,1,0:T(8,128)(2,1)S(1)} %get-tuple-element.23), channel_id=1, source_target_pairs={{0,2},{2,4},{4,6},{6,0},{1,3},{3,5},{5,7},{7,1},{8,10},{10,12},{12... | collective-permute-start | bytes 983048 | tf_op jit(solution)/shard_map/ppermute | solution.py:254
  88.8 27.6 %collective-permute-start.8 = (bf16[8,40,512]{2,1,0:T(8,128)(2,1)S(1)}, bf16[8,40,512]{2,1,0:T(8,128)(2,1)S(1)}, u32[]{:S(2)}, u32[]{:S(2)}) collective-permute-start(bf16[8,40,512]{2,1,0:T(8,128)(2,1)S(1)} %get-tuple-element.24), channel_id=1, source_target_pairs={{0,4},{2,6},{4,0},{6,2},{1,5},{3,7},{5,1},{7,3},{8,12},{10,14},{12... | collective-permute-start | bytes 983048 | tf_op jit(solution)/shard_map/ppermute | solution.py:254
  93.1 25.6 %collective-permute-start.9 = (bf16[8,40,512]{2,1,0:T(8,128)(2,1)S(1)}, bf16[8,40,512]{2,1,0:T(8,128)(2,1)S(1)}, u32[]{:S(2)}, u32[]{:S(2)}) collective-permute-start(bf16[8,40,512]{2,1,0:T(8,128)(2,1)S(1)} %get-tuple-element.25), channel_id=1, source_target_pairs={{0,6},{2,0},{4,2},{6,4},{1,7},{3,1},{5,3},{7,5},{8,14},{10,8},{12,... | collective-permute-start | bytes 983048 | tf_op jit(solution)/shard_map/ppermute | solution.py:254
  131.3 7.4 %copy-start.2 = (bf16[16,80,512]{2,1,0:T(8,128)(2,1)S(1)}, bf16[16,80,512]{2,1,0:T(8,128)(2,1)}, u32[]{:S(2)}) copy-start(bf16[16,80,512]{2,1,0:T(8,128)(2,1)} %get-tuple-element.30) | copy-start | bytes 3932164
  131.3 42.8 %all-to-all-start.3 = ((bf16[32,40,512]{2,1,0:T(8,128)(2,1)}), bf16[32,40,512]{2,1,0:T(8,128)(2,1)S(1)}, u32[]{:S(2)}, u32[]{:S(2)}) async-start(bf16[32,40,512]{2,1,0:T(8,128)(2,1)} %bitcast.97), calls=%async_computation.4 | async-start | bytes 2621440 | tf_op jit(solution)/shard_map/all_to_all | solution.py:313
  138.6 93.6 %reduce-scatter.2.cloned.1.call-start = ((), (), s32[]{:S(2)}) async-start(), calls=%async_computation.7 | async-start | bytes 2359296 | tf_op jit(solution)/shard_map/reduce_scatter | solution.py:322
  138.8 17.6 %collective-permute-start.12 = (bf16[8,40,512]{2,1,0:T(8,128)(2,1)S(1)}, bf16[8,40,512]{2,1,0:T(8,128)(2,1)S(1)}, u32[]{:S(2)}, u32[]{:S(2)}) collective-permute-start(bf16[8,40,512]{2,1,0:T(8,128)(2,1)S(1)} %get-tuple-element.36), channel_id=1, source_target_pairs={{0,2},{2,4},{4,6},{6,0},{1,3},{3,5},{5,7},{7,1},{8,10},{10,12},{12... | collective-permute-start | bytes 983048 | tf_op jit(solution)/shard_map/ppermute | solution.py:254
  141.9 27.5 %collective-permute-start.11 = (bf16[8,40,512]{2,1,0:T(8,128)(2,1)S(1)}, bf16[8,40,512]{2,1,0:T(8,128)(2,1)S(1)}, u32[]{:S(2)}, u32[]{:S(2)}) collective-permute-start(bf16[8,40,512]{2,1,0:T(8,128)(2,1)S(1)} %get-tuple-element.37), channel_id=1, source_target_pairs={{0,4},{2,6},{4,0},{6,2},{1,5},{3,7},{5,1},{7,3},{8,12},{10,14},{12... | collective-permute-start | bytes 983048 | tf_op jit(solution)/shard_map/ppermute | solution.py:254
  146.2 25.2 %collective-permute-start.10 = (bf16[8,40,512]{2,1,0:T(8,128)(2,1)S(1)}, bf16[8,40,512]{2,1,0:T(8,128)(2,1)S(1)}, u32[]{:S(2)}, u32[]{:S(2)}) collective-permute-start(bf16[8,40,512]{2,1,0:T(8,128)(2,1)S(1)} %get-tuple-element.38), channel_id=1, source_target_pairs={{0,6},{2,0},{4,2},{6,4},{1,7},{3,1},{5,3},{7,5},{8,14},{10,8},{12,... | collective-permute-start | bytes 983048 | tf_op jit(solution)/shard_map/ppermute | solution.py:254
  174.1 16.2 %copy-start.1 = (bf16[4,1,128,512]{3,2,1,0:T(8,128)(2,1)S(1)}, bf16[4,1,128,512]{3,2,1,0:T(8,128)(2,1)}, u32[]{:S(2)}) copy-start(bf16[4,1,128,512]{3,2,1,0:T(8,128)(2,1)} %get-tuple-element.44) | copy-start | bytes 1572868
  174.5 17.3 %copy-start = (bf16[4,1,128,512]{3,2,1,0:T(8,128)(2,1)S(1)}, bf16[4,1,128,512]{3,2,1,0:T(8,128)(2,1)}, u32[]{:S(2)}) copy-start(bf16[4,1,128,512]{3,2,1,0:T(8,128)(2,1)} %get-tuple-element.43) | copy-start | bytes 1572868
  185.9 5.9 %collective-permute-start.13 = (bf16[512,512]{1,0:T(8,128)(2,1)S(1)}, bf16[512,512]{1,0:T(8,128)(2,1)S(1)}, u32[]{:S(2)}, u32[]{:S(2)}) collective-permute-start(bf16[512,512]{1,0:T(8,128)(2,1)S(1)} %all_gather.7), channel_id=1, source_target_pairs={{0,1},{1,0},{2,3},{3,2},{4,5},{5,4},{6,7},{7,6},{8,9},{9,8},{10,11... | collective-permute-start | bytes 1572872 | tf_op jit(solution)/shard_map/ppermute | solution.py:27
  193.1 28.5 %all-to-all-start.4 = ((bf16[64,8,512]{2,1,0:T(8,128)(2,1)}), bf16[64,8,512]{2,1,0:T(8,128)(2,1)S(1)}, u32[]{:S(2)}, u32[]{:S(2)}) async-start(bf16[64,8,512]{2,1,0:T(8,128)(2,1)} %fusion.1), calls=%async_computation.5 | async-start | bytes 1048576 | tf_op jit(solution)/shard_map/all_to_all | solution.py:332
  208.0 14.3 %collective-permute-start.14 = (bf16[2,128,512]{2,1,0:T(8,128)(2,1)S(1)}, bf16[2,128,512]{2,1,0:T(8,128)(2,1)S(1)}, u32[]{:S(2)}, u32[]{:S(2)}) collective-permute-start(bf16[2,128,512]{2,1,0:T(8,128)(2,1)S(1)} %pad_maximum_fusion.6), channel_id=1, source_target_pairs={{0,6},{2,0},{4,2},{6,4},{1,7},{3,1},{5,3},{7,5},{8,14},{10,8},{12,... | collective-permute-start | bytes 786440 | tf_op jit(solution)/shard_map/ppermute | solution.py:254
  211.6 10.6 %collective-permute-start.15 = (bf16[2,128,512]{2,1,0:T(8,128)(2,1)S(1)}, bf16[2,128,512]{2,1,0:T(8,128)(2,1)S(1)}, u32[]{:S(2)}, u32[]{:S(2)}) collective-permute-start(bf16[2,128,512]{2,1,0:T(8,128)(2,1)S(1)} %pad_maximum_fusion.7), channel_id=1, source_target_pairs={{0,4},{2,6},{4,0},{6,2},{1,5},{3,7},{5,1},{7,3},{8,12},{10,14},{12... | collective-permute-start | bytes 786440 | tf_op jit(solution)/shard_map/ppermute | solution.py:254
  214.2 14.7 %collective-permute-start.16 = (bf16[2,128,512]{2,1,0:T(8,128)(2,1)S(1)}, bf16[2,128,512]{2,1,0:T(8,128)(2,1)S(1)}, u32[]{:S(2)}, u32[]{:S(2)}) collective-permute-start(bf16[2,128,512]{2,1,0:T(8,128)(2,1)S(1)} %pad_maximum_fusion.8), channel_id=1, source_target_pairs={{0,2},{2,4},{4,6},{6,0},{1,3},{3,5},{5,7},{7,1},{8,10},{10,12},{12... | collective-permute-start | bytes 786440 | tf_op jit(solution)/shard_map/ppermute | solution.py:254
Sparse Core Ops, SparseCore 0:
  22.6 45.9 all-gather.1
  174.2 51.2 reduce-scatter.1

commit v6 on v5

--- a/solution.py
+++ b/solution.py
@@ -65,28 +65,26 @@
     )(to, pltpu.with_memory_space_constraint(tokens, pltpu.HBM))
 
 
-def join_kernel(to_ref, near_ref, far_ref, b1_ref, b2_ref, b3_ref, out_ref, pick_ref):
+def join_kernel(to_ref, *refs):
+    *parts, out_ref, pick_ref = refs
     make_pick(to_ref, pick_ref)
-    parts = [near_ref[...], far_ref[...]]
-    for ref in (b1_ref, b2_ref, b3_ref):
-        parts += [ref[0], ref[1]]
-    out_ref[...] = mm(jnp.concatenate(parts, axis=1), pick_ref[...]).astype(BF)
-
-
-def join_columns(to, near, far, *others):
-    rows = near.shape[0]
-    one = pl.BlockSpec((rows, 128), lambda p: (0, p))
-    two = pl.BlockSpec((2, rows, 128), lambda p: (0, 0, p))
+    out_ref[...] = mm(jnp.concatenate([ref[...] for ref in parts], axis=1), pick_ref[...]).astype(BF)
+
+
+def join_columns(to, *slices):
+    rows = slices[0].shape[0]
+    near = pl.BlockSpec((rows, 128), lambda p: (0, p))
+    far = pl.BlockSpec((rows, 128), lambda p: (0, p + 4))
     return pl.pallas_call(
         join_kernel,
         grid=(4,),
-        in_specs=[pl.BlockSpec((1, 1024), lambda p: (0, 0)), one, one, two, two, two],
+        in_specs=[pl.BlockSpec((1, 1024), lambda p: (0, 0))] + [near, far] * 4,
         out_specs=pl.BlockSpec((rows, 1024), lambda p: (0, p)),
         out_shape=jax.ShapeDtypeStruct((rows, 4096), BF),
         scratch_shapes=[pltpu.VMEM((1024, 1024), BF)],
         compiler_params=pltpu.CompilerParams(vmem_limit_bytes=32 * 1024 * 1024),
-        cost_estimate=pl.CostEstimate(flops=6_000_000_000, bytes_accessed=18_000_000, transcendentals=0),
-    )(to, near, far, *others)
+        cost_estimate=pl.CostEstimate(flops=9_000_000_000, bytes_accessed=28_000_000, transcendentals=0),
+    )(to, *[x for pair in slices for x in (pair, pair)])
 
 
 def cotangent_kernel(
@@ -143,31 +141,10 @@
     )(expert, place, pltpu.with_memory_space_constraint(column, pltpu.HBM))
 
 
-def expert_kernel(x_ref, g_ref, up1, down1, up2, down2, back_ref, out_ref, up_ref, down_ref, sems):
-    step = pl.program_id(0)
-    copies = [
-        [
-            pltpu.make_async_copy(up, up_ref.at[e], sems.at[e, 0]),
-            pltpu.make_async_copy(down, down_ref.at[e], sems.at[e, 1]),
-        ]
-        for e, (up, down) in enumerate(((up1, down1), (up2, down2)))
-    ]
-
-    @pl.when(step == 0)
-    def _():
-        for copy in copies[0] + copies[1]:
-            copy.start()
-        for copy in copies[0]:
-            copy.wait()
-
-    @pl.when(step == 3)
-    def _():
-        for copy in copies[1]:
-            copy.wait()
-
-    w_up, w_down = up_ref[step // 3], down_ref[step // 3]
-    x = x_ref[...].reshape(256, 512)
-    g = g_ref[...].reshape(256, 512)
+ORDER = (0, 3, 2, 1, 4)
+
+
+def expert_block(x, g, w_up, w_down):
     pre = mm(x, w_up)
     grad_act = mm(g, w_down, ((1,), (1,)))
     gate, upper = pre[:, :512], pre[:, 512:]
@@ -176,44 +153,95 @@
     act = (soft * upper).astype(BF)
     grad_gate = (grad_act * upper * sigma * (1.0 + gate * (1.0 - sigma))).astype(BF)
     grad_up = (grad_act * soft).astype(BF)
-    last = ((1,), (1,))
-    back = mm(grad_gate, w_up[:, :512], last) + mm(grad_up, w_up[:, 512:], last)
-    back = back.astype(BF).reshape(16, 16, 512)
-    out = mm(act, w_down).astype(BF).reshape(16, 16, 512)
-
-    @pl.when(step != 3)
-    def _():
-        back_ref[...] = back
-        out_ref[...] = out
-
-    @pl.when(step == 3)
-    def _():
-        keep = (lax.broadcasted_iota(jnp.int32, (16, 16, 512), 1) % 8) < 4
-        back_ref[...] = jnp.where(keep, back_ref[...].astype(F32), back.astype(F32)).astype(BF)
-        out_ref[...] = jnp.where(keep, out_ref[...].astype(F32), out.astype(F32)).astype(BF)
+    back = mm(jnp.concatenate([grad_gate, grad_up], axis=1), w_up, ((1,), (1,)))
+    return back, mm(act, w_down)
+
+
+def start(*groups):
+    for copies in groups:
+        for copy in copies:
+            copy.start()
+
+
+def wait(copies):
+    for copy in copies:
+        copy.wait()
+
+
+def expert_kernel(
+    x_ref, g_ref, up1, down1, up2, down2, back_ref, out_ref,
+    x_in, g_in, back_to, out_to, up_ref, down_ref, w_sems, in_sems, out_sems
+):
+    weights = [
+        [
+            pltpu.make_async_copy(up, up_ref.at[e], w_sems.at[e, 0]),
+            pltpu.make_async_copy(down, down_ref.at[e], w_sems.at[e, 1]),
+        ]
+        for e, (up, down) in enumerate(((up1, down1), (up2, down2)))
+    ]
+    rows, sent = [], []
+    for n, b in enumerate(ORDER):
+        part = (slice(None), pl.ds(16 * b, 16))
+        rows.append([
+            pltpu.make_async_copy(x_ref.at[part], x_in.at[n], in_sems.at[n, 0]),
+            pltpu.make_async_copy(g_ref.at[part], g_in.at[n], in_sems.at[n, 1]),
+        ])
+        sent.append([
+            pltpu.make_async_copy(back_to.at[n], back_ref.at[part], out_sems.at[n, 0]),
+            pltpu.make_async_copy(out_to.at[n], out_ref.at[part], out_sems.at[n, 1]),
+        ])
+    start(rows[0], weights[0])
+
+    def step(e, n):
+        return expert_block(
+            x_in[n].reshape(256, 512), g_in[n].reshape(256, 512), up_ref[e], down_ref[e]
+        )
+
+    wait(weights[0])
+    start(*rows[1:], weights[1])
+    for n in (0, 1):
+        wait(rows[n])
+        back, out = step(0, n)
+        back_to[n] = back.astype(BF).reshape(16, 16, 512)
+        out_to[n] = out.astype(BF).reshape(16, 16, 512)
+        start(sent[n])
+    wait(rows[2])
+    own_back, own_out = step(0, 2)
+    wait(weights[1])
+    back, out = step(1, 2)
+    keep = (lax.broadcasted_iota(jnp.int32, (256, 512), 0) % 8) < 4
+    back_to[2] = jnp.where(keep, own_back, back).astype(BF).reshape(16, 16, 512)
+    out_to[2] = jnp.where(keep, own_out, out).astype(BF).reshape(16, 16, 512)
+    start(sent[2])
+    for n in (3, 4):
+        wait(rows[n])
+        back, out = step(1, n)
+        back_to[n] = back.astype(BF).reshape(16, 16, 512)
+        out_to[n] = out.astype(BF).reshape(16, 16, 512)
+        start(sent[n])
+    for copies in sent:
+        wait(copies)
 
 
 def expert_rows(x, g, *weights):
-    def block(i):
-        return (0, jnp.where(i == 0, 0, jnp.where(i == 1, 3, jnp.where(i < 4, 2, jnp.where(i == 4, 1, 4)))), 0)
-
-    rows = pl.BlockSpec((16, 16, 512), block)
     shape = pltpu.HBM((16, 80, 512), BF)
     hbm = lambda x: pltpu.with_memory_space_constraint(x, pltpu.HBM)
+    block = pltpu.VMEM((5, 16, 16, 512), BF)
     back, out = pl.pallas_call(
         expert_kernel,
-        grid=(6,),
-        in_specs=[
-            rows,
-            rows,
-            *[pl.BlockSpec(memory_space=pl.ANY)] * 4,
-        ],
-        out_specs=[rows, rows],
+        in_specs=[pl.BlockSpec(memory_space=pl.ANY)] * 6,
+        out_specs=[pl.BlockSpec(memory_space=pl.ANY)] * 2,
         out_shape=[shape, shape],
         scratch_shapes=[
+            block,
+            block,
+            block,
+            block,
             pltpu.VMEM((2, 512, 1024), BF),
             pltpu.VMEM((2, 512, 512), BF),
             pltpu.SemaphoreType.DMA((2, 2)),
+            pltpu.SemaphoreType.DMA((5, 2)),
+            pltpu.SemaphoreType.DMA((5, 2)),
         ],
         compiler_params=pltpu.CompilerParams(vmem_limit_bytes=40 * 1024 * 1024),
         cost_estimate=pl.CostEstimate(flops=4_800_000_000, bytes_accessed=8_500_000, transcendentals=800_000),
@@ -283,7 +311,7 @@
     tokens_other = take(feature_block, 1 - core, 1).reshape(4 * rows, 512)
 
     gate_up2, down2 = swap_core(after(gate_up, w_part)), swap_core(after(down, w_part))
-    w_other = swap_core(w_part)
+    w_both = jnp.concatenate([w_part, swap_core(w_part)])
 
     partial = mm(feature_block.reshape(8 * rows, 512), w_part).astype(BF).reshape(8, rows, 512)
     partials = lax.all_to_all(partial, XC, split_axis=0, concat_axis=0, tiled=True)
@@ -303,7 +331,9 @@
     code = slot_code(jnp.any(named_in(routes), axis=1))
     onehot = (mm(code, spread) == place.astype(F32)).astype(BF)
     out_send = mm(onehot, latent, ((0,), (0,))).astype(BF).reshape(32, PAIR, 512)
-    out_send = after(out_send, gate_up2, down2, tokens_mine, tokens_other, w_other)
+    out_send, w_both, *_ = lax.optimization_barrier(
+        (out_send, w_both, gate_up2, down2, tokens_mine, tokens_other)
+    )
     recv = lax.all_to_all(out_send, ZX, split_axis=0, concat_axis=0, tiled=True)
 
     sent = jnp.stack([grad_send[0]] + [shift_x(grad_send[d], d) for d in (1, 2, 3)])
@@ -329,15 +359,11 @@
     first = ((0,), (0,))
     part = mm(tokens_mine, line_grads, first) + mm(tokens_other, other_grads, first)
     part = part.astype(BF).reshape(64, 8, 512)
+
+    slices = mm(line_grads, w_both, ((1,), (1,))).astype(BF).reshape(4, rows, 1024)
+    part = after(part, slices)
     parts = lax.all_to_all(part, YZ, split_axis=0, concat_axis=0, tiled=True)
-
-    last = ((1,), (1,))
-    near = mm(line_grads, w_part, last).astype(BF).reshape(4, rows, 512)
-    far = mm(line_grads, w_other, last).astype(BF).reshape(4, rows, 512)
-    back = [take(near, at, 0), take(far, at, 0)]
-    for d in (1, 2, 3):
-        there = (at - d) % 4
-        back.append(shift_x(jnp.stack([take(near, there, 0), take(far, there, 0)]), -d))
+    back = [take(slices, at, 0)] + [shift_x(take(slices, (at - d) % 4, 0), -d) for d in (1, 2, 3)]
     back[0] = after(back[0], parts)
     grad_tokens = join_columns(to, *back)
     grad_w_in = jnp.sum(parts.astype(F32), axis=0) / rows

time: 242 us -> 237 us (0.979)
  waiting for transfers between devices: 66.7 us -> 60.4 us
  matrix products: 12.3 us -> 9.01 us
  starting transfers between devices: 103 us -> 106 us
    ppermute x12, waiting for transfers between devices: 58.1 us -> 52.4 us  [shift_x(): return lax.ppermute(x, 'x', [(i, (i + d) % 4) for i in range(4)])]
    dot_general x8 -> x7, matrix products: 9.91 us -> 6.57 us  [mm(): return lax.dot_general(a, b, (dims, ((), ())), preferred_element_type=F32)]
  transfers between devices with their start and end apart: 24 -> 24, of which waited for: 13 -> 12; matrix products, arithmetic and copies ran while one was open for 8% -> 8% of each run, Pallas kernels for 3% -> 4%
where the time goes in v6:
time: 237 us; the launch traced here: 234 us
  starting transfers between devices  106 us (45%)
  waiting for transfers between devices  60.4 us (25%)
  Pallas kernels  22.6 us (10%)
  between operations  14.6 us (6%)
  blocking collectives  11.5 us (5%)
  matrix products  9.01 us (4%)
  other arithmetic  7.04 us (3%)
  local copies, waits for them, and re-layouts  3.67 us (2%)
    ppermute x12, waiting for transfers between devices, shift_x(): return lax.ppermute(x, 'x', [(i, (i + d) % 4) for i in range(4)])  52.4 us
    ppermute x12, starting transfers between devices, shift_x(): return lax.ppermute(x, 'x', [(i, (i + d) % 4) for i in range(4)])  40.1 us
    ppermute x5, starting transfers between devices, swap_core(): return lax.ppermute(x, 'c', [(0, 1), (1, 0)])  19.6 us
    all_to_all x1, starting transfers between devices, shards(): parts = lax.all_to_all(part, YZ, split_axis=0, concat_axis=0, tiled=True)  11.5 us
    all_gather x1, blocking collectives, shards(): line_grads = lax.all_gather(grad_latent, 'x', axis=0, tiled=True)  11.5 us
    all_to_all x1, starting transfers between devices, shards(): lax.all_to_all(jnp.broadcast_to(w_in[None], (64,) + w_in.shape), YZ, spli...  10.9 us
    all_to_all x1, starting transfers between devices, shards(): recv = lax.all_to_all(out_send, ZX, split_axis=0, concat_axis=0, tiled=True)  9.55 us
    pallas_call x1, Pallas kernels, expert_rows(): pl.pallas_call(expert_kernel, in_specs=[pl.BlockSpec(memory_space=pl.ANY)...  9.44 us
  transfers between devices with their start and end apart: 24, of which 12 were waited for; matrix products, arithmetic and copies ran while one was open for 8% of the time, Pallas kernels for 4%

profile of v6, /device:TPU:1, one launch (start us, length us, event | category | flops | bytes accessed | tf_op | source)
XLA Modules:
  0.0 234.5 jit_solution(14767019390895259887)
XLA Ops:
  7.3 4.9 %shard_map.95 = (bf16[4,128,512]{2,1,0:T(8,128)(2,1)S(1)}, bf16[4,128,512]{2,1,0:T(8,128)(2,1)S(1)}) custom-call(s32[1,1024]{1,0:T(1,128)S(1)} %fusion.63.to_ref, bf16[128,4096]{1,0:T(8,128)(2,1)} %tokens_ref.1), custom_call_target="tpu_custom_call" | custom-call | flops 1100000000 | bytes 2100000 | tf_op jit(solution)/shard_map/pallas_call | solution.py:56
  12.3 8.8 %collective-permute-start = (bf16[4,128,512]{2,1,0:T(8,128)(2,1)S(1)}, bf16[4,128,512]{2,1,0:T(8,128)(2,1)S(1)}, u32[]{:S(2)}, u32[]{:S(2)}) collective-permute-start(bf16[4,128,512]{2,1,0:T(8,128)(2,1)S(1)} %get-tuple-element.23), channel_id=1, source_target_pairs={{0,1},{1,0},{2,3},{3,2},{4,5},{5,4},{6,7},{7,6},{8,9},{9,8},{10,11... | collective-permute-start | bytes 1572872 | tf_op jit(solution)/shard_map/ppermute | solution.py:27
  21.6 0.8 concatenate.6
  22.5 0.8 broadcast_in_dim.16
  23.3 10.9 %all-to-all-start = ((bf16[64,8,512]{2,1,0:T(8,128)(2,1)}), bf16[64,8,512]{2,1,0:T(8,128)(2,1)S(1)}, u32[]{:S(2)}, u32[]{:S(2)}) async-start(bf16[64,8,512]{2,1,0:T(8,128)(2,1)} %broadcast_in_dim.16), calls=%async_computation | async-start | bytes 1048576 | tf_op jit(solution)/shard_map/all_to_all | solution.py:295
  34.4 3.1 %collective-permute-start.1 = (bf16[2,128,512]{2,1,0:T(8,128)(2,1)S(1)}, bf16[2,128,512]{2,1,0:T(8,128)(2,1)S(1)}, u32[]{:S(2)}, u32[]{:S(2)}) collective-permute-start(bf16[2,128,512]{2,1,0:T(8,128)(2,1)S(1)} %get-tuple-element.58), channel_id=1, source_target_pairs={{0,2},{2,4},{4,6},{6,0},{1,3},{3,5},{5,7},{7,1},{8,10},{10,12},{12... | collective-permute-start | bytes 786440 | tf_op jit(solution)/shard_map/ppermute | solution.py:282
  37.6 3.4 %collective-permute-start.3 = (bf16[2,128,512]{2,1,0:T(8,128)(2,1)S(1)}, bf16[2,128,512]{2,1,0:T(8,128)(2,1)S(1)}, u32[]{:S(2)}, u32[]{:S(2)}) collective-permute-start(bf16[2,128,512]{2,1,0:T(8,128)(2,1)S(1)} %get-tuple-element.59), channel_id=1, source_target_pairs={{0,6},{2,0},{4,2},{6,4},{1,7},{3,1},{5,3},{7,5},{8,14},{10,8},{12,... | collective-permute-start | bytes 786440 | tf_op jit(solution)/shard_map/ppermute | solution.py:282
  40.9 3.4 %collective-permute-start.2 = (bf16[2,128,512]{2,1,0:T(8,128)(2,1)S(1)}, bf16[2,128,512]{2,1,0:T(8,128)(2,1)S(1)}, u32[]{:S(2)}, u32[]{:S(2)}) collective-permute-start(bf16[2,128,512]{2,1,0:T(8,128)(2,1)S(1)} %get-tuple-element.60), channel_id=1, source_target_pairs={{0,4},{2,6},{4,0},{6,2},{1,5},{3,7},{5,1},{7,3},{8,12},{10,14},{12... | collective-permute-start | bytes 786440 | tf_op jit(solution)/shard_map/ppermute | solution.py:282
  44.5 0.8 collective-permute-done.1
  45.3 1.6 collective-permute-done.3
  46.8 4.5 %collective-permute-done.2 = bf16[2,128,512]{2,1,0:T(8,128)(2,1)S(1)} collective-permute-done((bf16[2,128,512]{2,1,0:T(8,128)(2,1)S(1)}, bf16[2,128,512]{2,1,0:T(8,128)(2,1)S(1)}, u32[]{:S(2)}, u32[]{:S(2)}) %collective-permute-start.2) | collective-permute-done | bytes 262176 | tf_op jit(solution)/shard_map/ppermute | solution.py:282
  51.7 1.7 convolution_convert_fusion.2
  53.4 6.7 %all-to-all-start.1 = ((bf16[8,128,512]{2,1,0:T(8,128)(2,1)}), bf16[8,128,512]{2,1,0:T(8,128)(2,1)S(1)}, u32[]{:S(2)}, u32[]{:S(2)}) async-start(bf16[8,128,512]{2,1,0:T(8,128)(2,1)} %bitcast.101), calls=%async_computation.1 | async-start | bytes 2097152 | tf_op jit(solution)/shard_map/all_to_all | solution.py:317
  60.1 1.9 collective-permute-start.4
  62.0 2.4 %collective-permute-start.5 = (bf16[512,1024]{1,0:T(8,128)(2,1)}, bf16[512,1024]{1,0:T(8,128)(2,1)}, u32[]{:S(2)}, u32[]{:S(2)}) collective-permute-start(bf16[512,1024]{1,0:T(8,128)(2,1)} %bitcast.112), channel_id=1, source_target_pairs={{0,1},{1,0},{2,3},{3,2},{4,5},{5,4},{6,7},{7,6},{8,9},{9,8},{10,11... | collective-permute-start | bytes 3145736 | tf_op jit(solution)/shard_map/ppermute | solution.py:27
  65.3 1.9 collective-permute-start.6
  67.2 1.1 constant_dynamic-slice_fusion.1
  68.3 2.1 pad_maximum_fusion.5
  70.4 4.8 %shard_map.94 = (bf16[8,40,512]{2,1,0:T(8,128)(2,1)S(1)}, bf16[8,40,512]{2,1,0:T(8,128)(2,1)S(1)}, bf16[8,40,512]{2,1,0:T(8,128)(2,1)S(1)}, bf16[8,40,512]{2,1,0...) custom-call(s32[160,1]{1,0:T(8,128)S(1)} %get-tuple-element.68.expert_ref, ...), custom_call_target="tpu_custom_call" | custom-call | flops 1000000000 | bytes 3000000 | tf_op jit(solution)/shard_map/pallas_call | solution.py:132
  75.4 1.6 convolution_convert_fusion
  77.0 9.6 %all-to-all-start.2 = ((bf16[32,40,512]{2,1,0:T(8,128)(2,1)}), bf16[32,40,512]{2,1,0:T(8,128)(2,1)S(1)}, u32[]{:S(2)}, u32[]{:S(2)}) async-start(bf16[32,40,512]{2,1,0:T(8,128)(2,1)} %bitcast.91), calls=%async_computation.2 | async-start | bytes 2621440 | tf_op jit(solution)/shard_map/all_to_all | solution.py:337
  86.6 3.1 %collective-permute-start.7 = (bf16[8,40,512]{2,1,0:T(8,128)(2,1)S(1)}, bf16[8,40,512]{2,1,0:T(8,128)(2,1)S(1)}, u32[]{:S(2)}, u32[]{:S(2)}) collective-permute-start(bf16[8,40,512]{2,1,0:T(8,128)(2,1)S(1)} %get-tuple-element.25), channel_id=1, source_target_pairs={{0,2},{2,4},{4,6},{6,0},{1,3},{3,5},{5,7},{7,1},{8,10},{10,12},{12... | collective-permute-start | bytes 983048 | tf_op jit(solution)/shard_map/ppermute | solution.py:282
  89.7 4.3 %collective-permute-start.8 = (bf16[8,40,512]{2,1,0:T(8,128)(2,1)S(1)}, bf16[8,40,512]{2,1,0:T(8,128)(2,1)S(1)}, u32[]{:S(2)}, u32[]{:S(2)}) collective-permute-start(bf16[8,40,512]{2,1,0:T(8,128)(2,1)S(1)} %get-tuple-element.26), channel_id=1, source_target_pairs={{0,4},{2,6},{4,0},{6,2},{1,5},{3,7},{5,1},{7,3},{8,12},{10,14},{12... | collective-permute-start | bytes 983048 | tf_op jit(solution)/shard_map/ppermute | solution.py:282
  94.0 3.3 %collective-permute-start.9 = (bf16[8,40,512]{2,1,0:T(8,128)(2,1)S(1)}, bf16[8,40,512]{2,1,0:T(8,128)(2,1)S(1)}, u32[]{:S(2)}, u32[]{:S(2)}) collective-permute-start(bf16[8,40,512]{2,1,0:T(8,128)(2,1)S(1)} %get-tuple-element.27), channel_id=1, source_target_pairs={{0,6},{2,0},{4,2},{6,4},{1,7},{3,1},{5,3},{7,5},{8,14},{10,8},{12,... | collective-permute-start | bytes 983048 | tf_op jit(solution)/shard_map/ppermute | solution.py:282
  97.3 9.6 %collective-permute-done.7 = bf16[8,40,512]{2,1,0:T(8,128)(2,1)S(1)} collective-permute-done((bf16[8,40,512]{2,1,0:T(8,128)(2,1)S(1)}, bf16[8,40,512]{2,1,0:T(8,128)(2,1)S(1)}, u32[]{:S(2)}, u32[]{:S(2)}) %collective-permute-start.7) | collective-permute-done | bytes 327712 | tf_op jit(solution)/shard_map/ppermute | solution.py:282
  106.8 11.5 %collective-permute-done.8 = bf16[8,40,512]{2,1,0:T(8,128)(2,1)S(1)} collective-permute-done((bf16[8,40,512]{2,1,0:T(8,128)(2,1)S(1)}, bf16[8,40,512]{2,1,0:T(8,128)(2,1)S(1)}, u32[]{:S(2)}, u32[]{:S(2)}) %collective-permute-start.8) | collective-permute-done | bytes 327712 | tf_op jit(solution)/shard_map/ppermute | solution.py:282
  118.3 1.6 collective-permute-done.9
  120.2 1.2 pad_maximum_fusion.1
  121.5 9.4 %shard_map.96 = (bf16[16,80,512]{2,1,0:T(8,128)(2,1)}, bf16[16,80,512]{2,1,0:T(8,128)(2,1)}) custom-call(bf16[16,80,512]{2,1,0:T(8,128)(2,1)S(1)} %bitcast.85, bf16[16,80,512]{2,1,0:T(8,128)(2,1)} %bitcast.98, bf16[512,1024]{1,0:T(8,128)(2,1)} %bitcast.113, bf16[512,512]{1,0:T(8,128)(2,1)} %bitcast.115, bf16[512,1024]{1,0:T(8,128)(2,1)} %collective-permute-done.5.up2, ...), custom_call_target="tpu_custom_call" | custom-call | flops 4800000000 | bytes 8500000 | tf_op jit(solution)/shard_map/pallas_call | solution.py:230
  130.9 7.0 %all-to-all-start.3 = ((bf16[32,40,512]{2,1,0:T(8,128)(2,1)}), bf16[32,40,512]{2,1,0:T(8,128)(2,1)S(1)}, u32[]{:S(2)}, u32[]{:S(2)}) async-start(bf16[32,40,512]{2,1,0:T(8,128)(2,1)} %bitcast.97), calls=%async_computation.4 | async-start | bytes 2621440 | tf_op jit(solution)/shard_map/all_to_all | solution.py:343
  138.2 3.1 %collective-permute-start.12 = (bf16[8,40,512]{2,1,0:T(8,128)(2,1)S(1)}, bf16[8,40,512]{2,1,0:T(8,128)(2,1)S(1)}, u32[]{:S(2)}, u32[]{:S(2)}) collective-permute-start(bf16[8,40,512]{2,1,0:T(8,128)(2,1)S(1)} %get-tuple-element.40), channel_id=1, source_target_pairs={{0,2},{2,4},{4,6},{6,0},{1,3},{3,5},{5,7},{7,1},{8,10},{10,12},{12... | collective-permute-start | bytes 983048 | tf_op jit(solution)/shard_map/ppermute | solution.py:282
  141.3 4.3 %collective-permute-start.11 = (bf16[8,40,512]{2,1,0:T(8,128)(2,1)S(1)}, bf16[8,40,512]{2,1,0:T(8,128)(2,1)S(1)}, u32[]{:S(2)}, u32[]{:S(2)}) collective-permute-start(bf16[8,40,512]{2,1,0:T(8,128)(2,1)S(1)} %get-tuple-element.41), channel_id=1, source_target_pairs={{0,4},{2,6},{4,0},{6,2},{1,5},{3,7},{5,1},{7,3},{8,12},{10,14},{12... | collective-permute-start | bytes 983048 | tf_op jit(solution)/shard_map/ppermute | solution.py:282
  145.6 3.1 %collective-permute-start.10 = (bf16[8,40,512]{2,1,0:T(8,128)(2,1)S(1)}, bf16[8,40,512]{2,1,0:T(8,128)(2,1)S(1)}, u32[]{:S(2)}, u32[]{:S(2)}) collective-permute-start(bf16[8,40,512]{2,1,0:T(8,128)(2,1)S(1)} %get-tuple-element.42), channel_id=1, source_target_pairs={{0,6},{2,0},{4,2},{6,4},{1,7},{3,1},{5,3},{7,5},{8,14},{10,8},{12,... | collective-permute-start | bytes 983048 | tf_op jit(solution)/shard_map/ppermute | solution.py:282
  148.7 6.3 %collective-permute-done.12 = bf16[8,40,512]{2,1,0:T(8,128)(2,1)S(1)} collective-permute-done((bf16[8,40,512]{2,1,0:T(8,128)(2,1)S(1)}, bf16[8,40,512]{2,1,0:T(8,128)(2,1)S(1)}, u32[]{:S(2)}, u32[]{:S(2)}) %collective-permute-start.12) | collective-permute-done | bytes 327712 | tf_op jit(solution)/shard_map/ppermute | solution.py:282
  155.0 13.4 %collective-permute-done.11 = bf16[8,40,512]{2,1,0:T(8,128)(2,1)S(1)} collective-permute-done((bf16[8,40,512]{2,1,0:T(8,128)(2,1)S(1)}, bf16[8,40,512]{2,1,0:T(8,128)(2,1)S(1)}, u32[]{:S(2)}, u32[]{:S(2)}) %collective-permute-start.11) | collective-permute-done | bytes 327712 | tf_op jit(solution)/shard_map/ppermute | solution.py:282
  168.4 2.2 collective-permute-done.10
  171.3 1.9 convolution_add_fusion
  173.6 11.5 %all_gather.7 = bf16[512,512]{1,0:T(8,128)(2,1)S(1)} all-gather(bf16[128,512]{1,0:T(8,128)(2,1)S(1)} %convolution_convert_fusion.3), channel_id=1, replica_groups=mesh['dp'=8,'z'=8,'x'=4,'c'=2] {'x'}, dimensions={0}, use_global_device_ids=true | all-gather | bytes 655360 | tf_op jit(solution)/shard_map/all_gather | solution.py:357
  185.1 4.5 %collective-permute-start.13 = (bf16[512,512]{1,0:T(8,128)(2,1)S(1)}, bf16[512,512]{1,0:T(8,128)(2,1)S(1)}, u32[]{:S(2)}, u32[]{:S(2)}) collective-permute-start(bf16[512,512]{1,0:T(8,128)(2,1)S(1)} %all_gather.7), channel_id=1, source_target_pairs={{0,1},{1,0},{2,3},{3,2},{4,5},{5,4},{6,7},{7,6},{8,9},{9,8},{10,11... | collective-permute-start | bytes 1572872 | tf_op jit(solution)/shard_map/ppermute | solution.py:27
  191.2 1.3 fusion.1
  192.5 11.5 %all-to-all-start.4 = ((bf16[64,8,512]{2,1,0:T(8,128)(2,1)}), bf16[64,8,512]{2,1,0:T(8,128)(2,1)S(1)}, u32[]{:S(2)}, u32[]{:S(2)}) async-start(bf16[64,8,512]{2,1,0:T(8,128)(2,1)} %fusion.1), calls=%async_computation.5 | async-start | bytes 1048576 | tf_op jit(solution)/shard_map/all_to_all | solution.py:365
  204.1 2.4 %collective-permute-start.16 = (bf16[128,1024]{1,0:T(8,128)(2,1)S(1)}, bf16[128,1024]{1,0:T(8,128)(2,1)S(1)}, u32[]{:S(2)}, u32[]{:S(2)}) collective-permute-start(bf16[128,1024]{1,0:T(8,128)(2,1)S(1)} %get-tuple-element.47), channel_id=1, source_target_pairs={{0,2},{2,4},{4,6},{6,0},{1,3},{3,5},{5,7},{7,1},{8,10},{10,12},{12... | collective-permute-start | bytes 786440 | tf_op jit(solution)/shard_map/ppermute | solution.py:282
  206.5 4.3 %collective-permute-start.15 = (bf16[128,1024]{1,0:T(8,128)(2,1)S(1)}, bf16[128,1024]{1,0:T(8,128)(2,1)S(1)}, u32[]{:S(2)}, u32[]{:S(2)}) collective-permute-start(bf16[128,1024]{1,0:T(8,128)(2,1)S(1)} %get-tuple-element.48), channel_id=1, source_target_pairs={{0,4},{2,6},{4,0},{6,2},{1,5},{3,7},{5,1},{7,3},{8,12},{10,14},{12... | collective-permute-start | bytes 786440 | tf_op jit(solution)/shard_map/ppermute | solution.py:282
  210.8 2.2 collective-permute-start.14
  213.1 7.7 %all-to-all-done.4 = bf16[64,8,512]{2,1,0:T(8,128)(2,1)S(1)} async-done(((bf16[64,8,512]{2,1,0:T(8,128)(2,1)}), bf16[64,8,512]{2,1,0:T(8,128)(2,1)S(1)}, u32[]{:S(2)}, u32[]{:S(2)}) %all-to-all-start.4) | async-done | bytes 524320 | tf_op jit(solution)/shard_map/all_to_all | solution.py:365
  221.5 1.0 collective-permute-done.14.refs_2_.refs_3_
  222.5 3.5 %shard_map.97 = bf16[128,4096]{1,0:T(8,128)(2,1)} custom-call(s32[1,1024]{1,0:T(1,128)S(1)} %fusion.63.to_ref, bf16[128,1024]{1,0:T(8,128)(2,1)S(1)} %get-tuple-element.38.refs_0_.refs_1_, bf16[128,1024]{1,0:T(8,128)(2,1)S(1)} %get-tuple-element.38.refs_0_.refs_1_, bf16[128,1024]{1,0:T(8,128)(2,1)S(1)} %collective-permute-done.14.refs_2_.refs_3_, ...), custom_call_target="tpu_custom_call" | custom-call | flops 8999999488 | bytes 28000000 | tf_op jit(solution)/shard_map/pallas_call | solution.py:78
  226.0 1.6 convert_element_type.67
  (62 shorter events, 6.0 us)
Async XLA Ops:
  7.2 63.3 %all-gather.2.cloned.1.call-start = ((), (), s32[]{:S(2)}) async-start(), calls=%async_computation.6 | async-start | bytes 1474560 | tf_op jit(solution)/shard_map/all_gather | solution.py:302
  7.3 13.8 %copy-start.5 = (s32[128,8]{0,1:T(8,128)S(1)}, s32[128,8]{0,1:T(8,128)}, u32[]{:S(2)}) copy-start(s32[128,8]{0,1:T(8,128)} %param.8) | copy-start | bytes 12292
  7.3 13.8 %copy-start.7 = (f32[128,8]{0,1:T(8,128)S(1)}, f32[128,8]{0,1:T(8,128)}, u32[]{:S(2)}) copy-start(f32[128,8]{0,1:T(8,128)} %param.9) | copy-start | bytes 12292
  7.3 14.3 %copy-start.4 = (bf16[128,512]{1,0:T(8,128)(2,1)S(1)}, bf16[128,512]{1,0:T(8,128)(2,1)}, u32[]{:S(2)}) copy-start(bf16[128,512]{1,0:T(8,128)(2,1)} %param.13) | copy-start | bytes 393220
  7.3 15.1 %copy-start.6 = (bf16[8,512]{1,0:T(8,128)(2,1)S(1)}, bf16[8,512]{1,0:T(8,128)(2,1)}, u32[]{:S(2)}) copy-start(bf16[8,512]{1,0:T(8,128)(2,1)} %param.12) | copy-start | bytes 24580
  12.3 22.0 %collective-permute-start = (bf16[4,128,512]{2,1,0:T(8,128)(2,1)S(1)}, bf16[4,128,512]{2,1,0:T(8,128)(2,1)S(1)}, u32[]{:S(2)}, u32[]{:S(2)}) collective-permute-start(bf16[4,128,512]{2,1,0:T(8,128)(2,1)S(1)} %get-tuple-element.23), channel_id=1, source_target_pairs={{0,1},{1,0},{2,3},{3,2},{4,5},{5,4},{6,7},{7,6},{8,9},{9,8},{10,11... | collective-permute-start | bytes 1572872 | tf_op jit(solution)/shard_map/ppermute | solution.py:27
  23.3 28.4 %all-to-all-start = ((bf16[64,8,512]{2,1,0:T(8,128)(2,1)}), bf16[64,8,512]{2,1,0:T(8,128)(2,1)S(1)}, u32[]{:S(2)}, u32[]{:S(2)}) async-start(bf16[64,8,512]{2,1,0:T(8,128)(2,1)} %broadcast_in_dim.16), calls=%async_computation | async-start | bytes 1048576 | tf_op jit(solution)/shard_map/all_to_all | solution.py:295
  34.4 10.8 %collective-permute-start.1 = (bf16[2,128,512]{2,1,0:T(8,128)(2,1)S(1)}, bf16[2,128,512]{2,1,0:T(8,128)(2,1)S(1)}, u32[]{:S(2)}, u32[]{:S(2)}) collective-permute-start(bf16[2,128,512]{2,1,0:T(8,128)(2,1)S(1)} %get-tuple-element.58), channel_id=1, source_target_pairs={{0,2},{2,4},{4,6},{6,0},{1,3},{3,5},{5,7},{7,1},{8,10},{10,12},{12... | collective-permute-start | bytes 786440 | tf_op jit(solution)/shard_map/ppermute | solution.py:282
  37.6 9.3 %collective-permute-start.3 = (bf16[2,128,512]{2,1,0:T(8,128)(2,1)S(1)}, bf16[2,128,512]{2,1,0:T(8,128)(2,1)S(1)}, u32[]{:S(2)}, u32[]{:S(2)}) collective-permute-start(bf16[2,128,512]{2,1,0:T(8,128)(2,1)S(1)} %get-tuple-element.59), channel_id=1, source_target_pairs={{0,6},{2,0},{4,2},{6,4},{1,7},{3,1},{5,3},{7,5},{8,14},{10,8},{12,... | collective-permute-start | bytes 786440 | tf_op jit(solution)/shard_map/ppermute | solution.py:282
  40.9 10.4 %collective-permute-start.2 = (bf16[2,128,512]{2,1,0:T(8,128)(2,1)S(1)}, bf16[2,128,512]{2,1,0:T(8,128)(2,1)S(1)}, u32[]{:S(2)}, u32[]{:S(2)}) collective-permute-start(bf16[2,128,512]{2,1,0:T(8,128)(2,1)S(1)} %get-tuple-element.60), channel_id=1, source_target_pairs={{0,4},{2,6},{4,0},{6,2},{1,5},{3,7},{5,1},{7,3},{8,12},{10,14},{12... | collective-permute-start | bytes 786440 | tf_op jit(solution)/shard_map/ppermute | solution.py:282
  53.4 21.8 %all-to-all-start.1 = ((bf16[8,128,512]{2,1,0:T(8,128)(2,1)}), bf16[8,128,512]{2,1,0:T(8,128)(2,1)S(1)}, u32[]{:S(2)}, u32[]{:S(2)}) async-start(bf16[8,128,512]{2,1,0:T(8,128)(2,1)} %bitcast.101), calls=%async_computation.1 | async-start | bytes 2097152 | tf_op jit(solution)/shard_map/all_to_all | solution.py:317
  60.1 8.2 %collective-permute-start.4 = (bf16[512,512]{1,0:T(8,128)(2,1)S(1)}, bf16[512,512]{1,0:T(8,128)(2,1)}, u32[]{:S(2)}, u32[]{:S(2)}) collective-permute-start(bf16[512,512]{1,0:T(8,128)(2,1)S(1)} %bitcast.94), channel_id=1, source_target_pairs={{0,1},{1,0},{2,3},{3,2},{4,5},{5,4},{6,7},{7,6},{8,9},{9,8},{10,11... | collective-permute-start | bytes 1572872 | tf_op jit(solution)/shard_map/ppermute | solution.py:27
  62.0 15.0 %collective-permute-start.5 = (bf16[512,1024]{1,0:T(8,128)(2,1)}, bf16[512,1024]{1,0:T(8,128)(2,1)}, u32[]{:S(2)}, u32[]{:S(2)}) collective-permute-start(bf16[512,1024]{1,0:T(8,128)(2,1)} %bitcast.112), channel_id=1, source_target_pairs={{0,1},{1,0},{2,3},{3,2},{4,5},{5,4},{6,7},{7,6},{8,9},{9,8},{10,11... | collective-permute-start | bytes 3145736 | tf_op jit(solution)/shard_map/ppermute | solution.py:27
  65.3 11.7 %collective-permute-start.6 = (bf16[512,512]{1,0:T(8,128)(2,1)}, bf16[512,512]{1,0:T(8,128)(2,1)}, u32[]{:S(2)}, u32[]{:S(2)}) collective-permute-start(bf16[512,512]{1,0:T(8,128)(2,1)} %bitcast.114), channel_id=1, source_target_pairs={{0,1},{1,0},{2,3},{3,2},{4,5},{5,4},{6,7},{7,6},{8,9},{9,8},{10,11... | collective-permute-start | bytes 1572872 | tf_op jit(solution)/shard_map/ppermute | solution.py:27
  77.0 44.5 %all-to-all-start.2 = ((bf16[32,40,512]{2,1,0:T(8,128)(2,1)}), bf16[32,40,512]{2,1,0:T(8,128)(2,1)S(1)}, u32[]{:S(2)}, u32[]{:S(2)}) async-start(bf16[32,40,512]{2,1,0:T(8,128)(2,1)} %bitcast.91), calls=%async_computation.2 | async-start | bytes 2621440 | tf_op jit(solution)/shard_map/all_to_all | solution.py:337
  86.6 20.3 %collective-permute-start.7 = (bf16[8,40,512]{2,1,0:T(8,128)(2,1)S(1)}, bf16[8,40,512]{2,1,0:T(8,128)(2,1)S(1)}, u32[]{:S(2)}, u32[]{:S(2)}) collective-permute-start(bf16[8,40,512]{2,1,0:T(8,128)(2,1)S(1)} %get-tuple-element.25), channel_id=1, source_target_pairs={{0,2},{2,4},{4,6},{6,0},{1,3},{3,5},{5,7},{7,1},{8,10},{10,12},{12... | collective-permute-start | bytes 983048 | tf_op jit(solution)/shard_map/ppermute | solution.py:282
  89.7 28.6 %collective-permute-start.8 = (bf16[8,40,512]{2,1,0:T(8,128)(2,1)S(1)}, bf16[8,40,512]{2,1,0:T(8,128)(2,1)S(1)}, u32[]{:S(2)}, u32[]{:S(2)}) collective-permute-start(bf16[8,40,512]{2,1,0:T(8,128)(2,1)S(1)} %get-tuple-element.26), channel_id=1, source_target_pairs={{0,4},{2,6},{4,0},{6,2},{1,5},{3,7},{5,1},{7,3},{8,12},{10,14},{12... | collective-permute-start | bytes 983048 | tf_op jit(solution)/shard_map/ppermute | solution.py:282
  94.0 25.9 %collective-permute-start.9 = (bf16[8,40,512]{2,1,0:T(8,128)(2,1)S(1)}, bf16[8,40,512]{2,1,0:T(8,128)(2,1)S(1)}, u32[]{:S(2)}, u32[]{:S(2)}) collective-permute-start(bf16[8,40,512]{2,1,0:T(8,128)(2,1)S(1)} %get-tuple-element.27), channel_id=1, source_target_pairs={{0,6},{2,0},{4,2},{6,4},{1,7},{3,1},{5,3},{7,5},{8,14},{10,8},{12,... | collective-permute-start | bytes 983048 | tf_op jit(solution)/shard_map/ppermute | solution.py:282
  130.9 7.1 %copy-start.2 = (bf16[16,80,512]{2,1,0:T(8,128)(2,1)S(1)}, bf16[16,80,512]{2,1,0:T(8,128)(2,1)}, u32[]{:S(2)}) copy-start(bf16[16,80,512]{2,1,0:T(8,128)(2,1)} %get-tuple-element.32) | copy-start | bytes 3932164
  130.9 42.3 %all-to-all-start.3 = ((bf16[32,40,512]{2,1,0:T(8,128)(2,1)}), bf16[32,40,512]{2,1,0:T(8,128)(2,1)S(1)}, u32[]{:S(2)}, u32[]{:S(2)}) async-start(bf16[32,40,512]{2,1,0:T(8,128)(2,1)} %bitcast.97), calls=%async_computation.4 | async-start | bytes 2621440 | tf_op jit(solution)/shard_map/all_to_all | solution.py:343
  138.0 88.0 %reduce-scatter.2.cloned.1.call-start = ((), (), s32[]{:S(2)}) async-start(), calls=%async_computation.7 | async-start | bytes 2359296 | tf_op jit(solution)/shard_map/reduce_scatter | solution.py:352
  138.2 16.8 %collective-permute-start.12 = (bf16[8,40,512]{2,1,0:T(8,128)(2,1)S(1)}, bf16[8,40,512]{2,1,0:T(8,128)(2,1)S(1)}, u32[]{:S(2)}, u32[]{:S(2)}) collective-permute-start(bf16[8,40,512]{2,1,0:T(8,128)(2,1)S(1)} %get-tuple-element.40), channel_id=1, source_target_pairs={{0,2},{2,4},{4,6},{6,0},{1,3},{3,5},{5,7},{7,1},{8,10},{10,12},{12... | collective-permute-start | bytes 983048 | tf_op jit(solution)/shard_map/ppermute | solution.py:282
  141.3 27.1 %collective-permute-start.11 = (bf16[8,40,512]{2,1,0:T(8,128)(2,1)S(1)}, bf16[8,40,512]{2,1,0:T(8,128)(2,1)S(1)}, u32[]{:S(2)}, u32[]{:S(2)}) collective-permute-start(bf16[8,40,512]{2,1,0:T(8,128)(2,1)S(1)} %get-tuple-element.41), channel_id=1, source_target_pairs={{0,4},{2,6},{4,0},{6,2},{1,5},{3,7},{5,1},{7,3},{8,12},{10,14},{12... | collective-permute-start | bytes 983048 | tf_op jit(solution)/shard_map/ppermute | solution.py:282
  145.6 25.0 %collective-permute-start.10 = (bf16[8,40,512]{2,1,0:T(8,128)(2,1)S(1)}, bf16[8,40,512]{2,1,0:T(8,128)(2,1)S(1)}, u32[]{:S(2)}, u32[]{:S(2)}) collective-permute-start(bf16[8,40,512]{2,1,0:T(8,128)(2,1)S(1)} %get-tuple-element.42), channel_id=1, source_target_pairs={{0,6},{2,0},{4,2},{6,4},{1,7},{3,1},{5,3},{7,5},{8,14},{10,8},{12,... | collective-permute-start | bytes 983048 | tf_op jit(solution)/shard_map/ppermute | solution.py:282
  173.3 16.4 %copy-start.1 = (bf16[4,1,128,512]{3,2,1,0:T(8,128)(2,1)S(1)}, bf16[4,1,128,512]{3,2,1,0:T(8,128)(2,1)}, u32[]{:S(2)}) copy-start(bf16[4,1,128,512]{3,2,1,0:T(8,128)(2,1)} %get-tuple-element.52) | copy-start | bytes 1572868
  173.6 16.5 %copy-start.3 = (bf16[1024,512]{1,0:T(8,128)(2,1)S(1)}, bf16[1024,512]{1,0:T(8,128)(2,1)}, u32[]{:S(2)}) copy-start(bf16[1024,512]{1,0:T(8,128)(2,1)} %pad_maximum_fusion.5) | copy-start | bytes 3145732
  185.1 6.1 %collective-permute-start.13 = (bf16[512,512]{1,0:T(8,128)(2,1)S(1)}, bf16[512,512]{1,0:T(8,128)(2,1)S(1)}, u32[]{:S(2)}, u32[]{:S(2)}) collective-permute-start(bf16[512,512]{1,0:T(8,128)(2,1)S(1)} %all_gather.7), channel_id=1, source_target_pairs={{0,1},{1,0},{2,3},{3,2},{4,5},{5,4},{6,7},{7,6},{8,9},{9,8},{10,11... | collective-permute-start | bytes 1572872 | tf_op jit(solution)/shard_map/ppermute | solution.py:27
  190.2 1.0 copy-start
  192.5 28.3 %all-to-all-start.4 = ((bf16[64,8,512]{2,1,0:T(8,128)(2,1)}), bf16[64,8,512]{2,1,0:T(8,128)(2,1)S(1)}, u32[]{:S(2)}, u32[]{:S(2)}) async-start(bf16[64,8,512]{2,1,0:T(8,128)(2,1)} %fusion.1), calls=%async_computation.5 | async-start | bytes 1048576 | tf_op jit(solution)/shard_map/all_to_all | solution.py:365
  204.1 17.4 %collective-permute-start.16 = (bf16[128,1024]{1,0:T(8,128)(2,1)S(1)}, bf16[128,1024]{1,0:T(8,128)(2,1)S(1)}, u32[]{:S(2)}, u32[]{:S(2)}) collective-permute-start(bf16[128,1024]{1,0:T(8,128)(2,1)S(1)} %get-tuple-element.47), channel_id=1, source_target_pairs={{0,2},{2,4},{4,6},{6,0},{1,3},{3,5},{5,7},{7,1},{8,10},{10,12},{12... | collective-permute-start | bytes 786440 | tf_op jit(solution)/shard_map/ppermute | solution.py:282
  206.5 15.0 %collective-permute-start.15 = (bf16[128,1024]{1,0:T(8,128)(2,1)S(1)}, bf16[128,1024]{1,0:T(8,128)(2,1)S(1)}, u32[]{:S(2)}, u32[]{:S(2)}) collective-permute-start(bf16[128,1024]{1,0:T(8,128)(2,1)S(1)} %get-tuple-element.48), channel_id=1, source_target_pairs={{0,4},{2,6},{4,0},{6,2},{1,5},{3,7},{5,1},{7,3},{8,12},{10,14},{12... | collective-permute-start | bytes 786440 | tf_op jit(solution)/shard_map/ppermute | solution.py:282
  210.8 11.7 %collective-permute-start.14 = (bf16[128,1024]{1,0:T(8,128)(2,1)S(1)}, bf16[128,1024]{1,0:T(8,128)(2,1)S(1)}, u32[]{:S(2)}, u32[]{:S(2)}) collective-permute-start(bf16[128,1024]{1,0:T(8,128)(2,1)S(1)} %get-tuple-element.49), channel_id=1, source_target_pairs={{0,6},{2,0},{4,2},{6,4},{1,7},{3,1},{5,3},{7,5},{8,14},{10,8},{12,... | collective-permute-start | bytes 786440 | tf_op jit(solution)/shard_map/ppermute | solution.py:282
Sparse Core Ops, SparseCore 0:
  22.6 46.0 all-gather.1
  173.4 51.3 reduce-scatter.1

commit v7 on v6

--- a/solution.py
+++ b/solution.py
@@ -42,21 +42,25 @@
 
 
 def split_kernel(to_ref, tokens_ref, mine_ref, theirs_ref, pick_ref):
-    make_pick(to_ref, pick_ref)
-    out = mm(tokens_ref[...], pick_ref[...], ((1,), (1,))).astype(BF)
-    for d in range(4):
-        mine_ref[d] = out[:, 256 * d : 256 * d + 128]
-        theirs_ref[d] = out[:, 256 * d + 128 : 256 * d + 256]
+    at = lax.broadcasted_iota(jnp.int32, (1024, 1024), 0)
+    pick_ref[...] = jnp.where(to_ref[...] == at, 1.0, 0.0).astype(BF)
+    tokens = jnp.concatenate([tokens_ref[:, 1024 * p : 1024 * (p + 1)] for p in range(4)], axis=0)
+    out = mm(tokens, pick_ref[...], ((1,), (1,))).astype(BF)
+    for p in range(4):
+        for d in range(4):
+            part = out[128 * p : 128 * (p + 1), 256 * d : 256 * (d + 1)]
+            mine_ref[d, :, 128 * p : 128 * (p + 1)] = part[:, :128]
+            theirs_ref[d, :, 128 * p : 128 * (p + 1)] = part[:, 128:]
 
 
 def split_columns(to, tokens):
     rows = tokens.shape[0]
     shape = jax.ShapeDtypeStruct((4, rows, 512), BF)
-    part = pl.BlockSpec((4, rows, 128), lambda p: (0, 0, p))
+    part = pl.BlockSpec((4, rows, 512), lambda p: (0, 0, 0))
     return pl.pallas_call(
         split_kernel,
-        grid=(4,),
-        in_specs=[pl.BlockSpec((1, 1024), lambda p: (0, 0)), pl.BlockSpec((rows, 1024), lambda p: (0, p))],
+        grid=(1,),
+        in_specs=[pl.BlockSpec((1, 1024), lambda p: (0, 0)), pl.BlockSpec((rows, 4096), lambda p: (0, 0))],
         out_specs=[part, part],
         out_shape=[shape, shape],
         scratch_shapes=[pltpu.VMEM((1024, 1024), BF)],

time: 237 us -> 235 us (level)
  Pallas kernels: 22.6 us -> 20.2 us
    pallas_call x1, Pallas kernels: 4.93 us -> 2.55 us  [split_columns(): pl.pallas_call(split_kernel, grid=(1,), in_specs=[pl.BlockSpec((1, 1024),...]
where the time goes in v7:
time: 235 us; the launch traced here: 232 us
  starting transfers between devices  106 us (45%)
  waiting for transfers between devices  60.4 us (26%)
  Pallas kernels  20.2 us (9%)
  between operations  14.6 us (6%)
  blocking collectives  11.5 us (5%)
  matrix products  9.01 us (4%)
  other arithmetic  7.04 us (3%)
  local copies, waits for them, and re-layouts  3.66 us (2%)
    ppermute x12, waiting for transfers between devices, shift_x(): return lax.ppermute(x, 'x', [(i, (i + d) % 4) for i in range(4)])  52.4 us
    ppermute x12, starting transfers between devices, shift_x(): return lax.ppermute(x, 'x', [(i, (i + d) % 4) for i in range(4)])  40.1 us
    ppermute x5, starting transfers between devices, swap_core(): return lax.ppermute(x, 'c', [(0, 1), (1, 0)])  19.6 us
    all_to_all x1, starting transfers between devices, shards(): parts = lax.all_to_all(part, YZ, split_axis=0, concat_axis=0, tiled=True)  11.5 us
    all_gather x1, blocking collectives, shards(): line_grads = lax.all_gather(grad_latent, 'x', axis=0, tiled=True)  11.5 us
    all_to_all x1, starting transfers between devices, shards(): lax.all_to_all(jnp.broadcast_to(w_in[None], (64,) + w_in.shape), YZ, spli...  10.9 us
    all_to_all x1, starting transfers between devices, shards(): recv = lax.all_to_all(out_send, ZX, split_axis=0, concat_axis=0, tiled=True)  9.55 us
    pallas_call x1, Pallas kernels, expert_rows(): pl.pallas_call(expert_kernel, in_specs=[pl.BlockSpec(memory_space=pl.ANY)...  9.44 us
  transfers between devices with their start and end apart: 24, of which 12 were waited for; matrix products, arithmetic and copies ran while one was open for 8% of the time, Pallas kernels for 4%

profile of v7, /device:TPU:1, one launch (start us, length us, event | category | flops | bytes accessed | tf_op | source)
XLA Modules:
  0.0 232.1 jit_solution(17614734440009768176)
XLA Ops:
  7.3 2.6 %shard_map.95 = (bf16[4,128,512]{2,1,0:T(8,128)(2,1)S(1)}, bf16[4,128,512]{2,1,0:T(8,128)(2,1)S(1)}) custom-call(s32[1,1024]{1,0:T(1,128)S(1)} %fusion.63.to_ref, bf16[128,4096]{1,0:T(8,128)(2,1)} %tokens_ref.1), custom_call_target="tpu_custom_call" | custom-call | flops 1100000000 | bytes 2100000 | tf_op jit(solution)/shard_map/pallas_call | solution.py:60
  9.9 8.8 %collective-permute-start = (bf16[4,128,512]{2,1,0:T(8,128)(2,1)S(1)}, bf16[4,128,512]{2,1,0:T(8,128)(2,1)S(1)}, u32[]{:S(2)}, u32[]{:S(2)}) collective-permute-start(bf16[4,128,512]{2,1,0:T(8,128)(2,1)S(1)} %get-tuple-element.23), channel_id=1, source_target_pairs={{0,1},{1,0},{2,3},{3,2},{4,5},{5,4},{6,7},{7,6},{8,9},{9,8},{10,11... | collective-permute-start | bytes 1572872 | tf_op jit(solution)/shard_map/ppermute | solution.py:27
  19.2 0.8 concatenate.6
  20.1 0.8 broadcast_in_dim.16
  20.9 10.9 %all-to-all-start = ((bf16[64,8,512]{2,1,0:T(8,128)(2,1)}), bf16[64,8,512]{2,1,0:T(8,128)(2,1)S(1)}, u32[]{:S(2)}, u32[]{:S(2)}) async-start(bf16[64,8,512]{2,1,0:T(8,128)(2,1)} %broadcast_in_dim.16), calls=%async_computation | async-start | bytes 1048576 | tf_op jit(solution)/shard_map/all_to_all | solution.py:299
  32.0 3.1 %collective-permute-start.1 = (bf16[2,128,512]{2,1,0:T(8,128)(2,1)S(1)}, bf16[2,128,512]{2,1,0:T(8,128)(2,1)S(1)}, u32[]{:S(2)}, u32[]{:S(2)}) collective-permute-start(bf16[2,128,512]{2,1,0:T(8,128)(2,1)S(1)} %get-tuple-element.58), channel_id=1, source_target_pairs={{0,2},{2,4},{4,6},{6,0},{1,3},{3,5},{5,7},{7,1},{8,10},{10,12},{12... | collective-permute-start | bytes 786440 | tf_op jit(solution)/shard_map/ppermute | solution.py:286
  35.2 3.4 %collective-permute-start.3 = (bf16[2,128,512]{2,1,0:T(8,128)(2,1)S(1)}, bf16[2,128,512]{2,1,0:T(8,128)(2,1)S(1)}, u32[]{:S(2)}, u32[]{:S(2)}) collective-permute-start(bf16[2,128,512]{2,1,0:T(8,128)(2,1)S(1)} %get-tuple-element.59), channel_id=1, source_target_pairs={{0,6},{2,0},{4,2},{6,4},{1,7},{3,1},{5,3},{7,5},{8,14},{10,8},{12,... | collective-permute-start | bytes 786440 | tf_op jit(solution)/shard_map/ppermute | solution.py:286
  38.6 3.4 %collective-permute-start.2 = (bf16[2,128,512]{2,1,0:T(8,128)(2,1)S(1)}, bf16[2,128,512]{2,1,0:T(8,128)(2,1)S(1)}, u32[]{:S(2)}, u32[]{:S(2)}) collective-permute-start(bf16[2,128,512]{2,1,0:T(8,128)(2,1)S(1)} %get-tuple-element.60), channel_id=1, source_target_pairs={{0,4},{2,6},{4,0},{6,2},{1,5},{3,7},{5,1},{7,3},{8,12},{10,14},{12... | collective-permute-start | bytes 786440 | tf_op jit(solution)/shard_map/ppermute | solution.py:286
  42.1 0.8 collective-permute-done.1
  42.9 1.6 collective-permute-done.3
  44.5 4.5 %collective-permute-done.2 = bf16[2,128,512]{2,1,0:T(8,128)(2,1)S(1)} collective-permute-done((bf16[2,128,512]{2,1,0:T(8,128)(2,1)S(1)}, bf16[2,128,512]{2,1,0:T(8,128)(2,1)S(1)}, u32[]{:S(2)}, u32[]{:S(2)}) %collective-permute-start.2) | collective-permute-done | bytes 262176 | tf_op jit(solution)/shard_map/ppermute | solution.py:286
  49.3 1.7 convolution_convert_fusion.2
  51.0 6.7 %all-to-all-start.1 = ((bf16[8,128,512]{2,1,0:T(8,128)(2,1)}), bf16[8,128,512]{2,1,0:T(8,128)(2,1)S(1)}, u32[]{:S(2)}, u32[]{:S(2)}) async-start(bf16[8,128,512]{2,1,0:T(8,128)(2,1)} %bitcast.101), calls=%async_computation.1 | async-start | bytes 2097152 | tf_op jit(solution)/shard_map/all_to_all | solution.py:321
  57.7 1.9 collective-permute-start.4
  59.7 2.4 %collective-permute-start.5 = (bf16[512,1024]{1,0:T(8,128)(2,1)}, bf16[512,1024]{1,0:T(8,128)(2,1)}, u32[]{:S(2)}, u32[]{:S(2)}) collective-permute-start(bf16[512,1024]{1,0:T(8,128)(2,1)} %bitcast.112), channel_id=1, source_target_pairs={{0,1},{1,0},{2,3},{3,2},{4,5},{5,4},{6,7},{7,6},{8,9},{9,8},{10,11... | collective-permute-start | bytes 3145736 | tf_op jit(solution)/shard_map/ppermute | solution.py:27
  62.9 1.9 collective-permute-start.6
  64.8 1.1 constant_dynamic-slice_fusion.1
  66.0 2.1 pad_maximum_fusion.5
  68.0 4.8 %shard_map.94 = (bf16[8,40,512]{2,1,0:T(8,128)(2,1)S(1)}, bf16[8,40,512]{2,1,0:T(8,128)(2,1)S(1)}, bf16[8,40,512]{2,1,0:T(8,128)(2,1)S(1)}, bf16[8,40,512]{2,1,0...) custom-call(s32[160,1]{1,0:T(8,128)S(1)} %get-tuple-element.68.expert_ref, ...), custom_call_target="tpu_custom_call" | custom-call | flops 1000000000 | bytes 3000000 | tf_op jit(solution)/shard_map/pallas_call | solution.py:136
  73.0 1.6 convolution_convert_fusion
  74.6 9.6 %all-to-all-start.2 = ((bf16[32,40,512]{2,1,0:T(8,128)(2,1)}), bf16[32,40,512]{2,1,0:T(8,128)(2,1)S(1)}, u32[]{:S(2)}, u32[]{:S(2)}) async-start(bf16[32,40,512]{2,1,0:T(8,128)(2,1)} %bitcast.91), calls=%async_computation.2 | async-start | bytes 2621440 | tf_op jit(solution)/shard_map/all_to_all | solution.py:341
  84.2 3.1 %collective-permute-start.7 = (bf16[8,40,512]{2,1,0:T(8,128)(2,1)S(1)}, bf16[8,40,512]{2,1,0:T(8,128)(2,1)S(1)}, u32[]{:S(2)}, u32[]{:S(2)}) collective-permute-start(bf16[8,40,512]{2,1,0:T(8,128)(2,1)S(1)} %get-tuple-element.25), channel_id=1, source_target_pairs={{0,2},{2,4},{4,6},{6,0},{1,3},{3,5},{5,7},{7,1},{8,10},{10,12},{12... | collective-permute-start | bytes 983048 | tf_op jit(solution)/shard_map/ppermute | solution.py:286
  87.3 4.3 %collective-permute-start.8 = (bf16[8,40,512]{2,1,0:T(8,128)(2,1)S(1)}, bf16[8,40,512]{2,1,0:T(8,128)(2,1)S(1)}, u32[]{:S(2)}, u32[]{:S(2)}) collective-permute-start(bf16[8,40,512]{2,1,0:T(8,128)(2,1)S(1)} %get-tuple-element.26), channel_id=1, source_target_pairs={{0,4},{2,6},{4,0},{6,2},{1,5},{3,7},{5,1},{7,3},{8,12},{10,14},{12... | collective-permute-start | bytes 983048 | tf_op jit(solution)/shard_map/ppermute | solution.py:286
  91.6 3.3 %collective-permute-start.9 = (bf16[8,40,512]{2,1,0:T(8,128)(2,1)S(1)}, bf16[8,40,512]{2,1,0:T(8,128)(2,1)S(1)}, u32[]{:S(2)}, u32[]{:S(2)}) collective-permute-start(bf16[8,40,512]{2,1,0:T(8,128)(2,1)S(1)} %get-tuple-element.27), channel_id=1, source_target_pairs={{0,6},{2,0},{4,2},{6,4},{1,7},{3,1},{5,3},{7,5},{8,14},{10,8},{12,... | collective-permute-start | bytes 983048 | tf_op jit(solution)/shard_map/ppermute | solution.py:286
  94.9 9.6 %collective-permute-done.7 = bf16[8,40,512]{2,1,0:T(8,128)(2,1)S(1)} collective-permute-done((bf16[8,40,512]{2,1,0:T(8,128)(2,1)S(1)}, bf16[8,40,512]{2,1,0:T(8,128)(2,1)S(1)}, u32[]{:S(2)}, u32[]{:S(2)}) %collective-permute-start.7) | collective-permute-done | bytes 327712 | tf_op jit(solution)/shard_map/ppermute | solution.py:286
  104.5 11.5 %collective-permute-done.8 = bf16[8,40,512]{2,1,0:T(8,128)(2,1)S(1)} collective-permute-done((bf16[8,40,512]{2,1,0:T(8,128)(2,1)S(1)}, bf16[8,40,512]{2,1,0:T(8,128)(2,1)S(1)}, u32[]{:S(2)}, u32[]{:S(2)}) %collective-permute-start.8) | collective-permute-done | bytes 327712 | tf_op jit(solution)/shard_map/ppermute | solution.py:286
  116.0 1.5 collective-permute-done.9
  117.8 1.2 pad_maximum_fusion.1
  119.0 9.4 %shard_map.96 = (bf16[16,80,512]{2,1,0:T(8,128)(2,1)}, bf16[16,80,512]{2,1,0:T(8,128)(2,1)}) custom-call(bf16[16,80,512]{2,1,0:T(8,128)(2,1)S(1)} %bitcast.85, bf16[16,80,512]{2,1,0:T(8,128)(2,1)} %bitcast.98, bf16[512,1024]{1,0:T(8,128)(2,1)} %bitcast.113, bf16[512,512]{1,0:T(8,128)(2,1)} %bitcast.115, bf16[512,1024]{1,0:T(8,128)(2,1)} %collective-permute-done.5.up2, ...), custom_call_target="tpu_custom_call" | custom-call | flops 4800000000 | bytes 8500000 | tf_op jit(solution)/shard_map/pallas_call | solution.py:234
  128.5 7.1 %all-to-all-start.3 = ((bf16[32,40,512]{2,1,0:T(8,128)(2,1)}), bf16[32,40,512]{2,1,0:T(8,128)(2,1)S(1)}, u32[]{:S(2)}, u32[]{:S(2)}) async-start(bf16[32,40,512]{2,1,0:T(8,128)(2,1)} %bitcast.97), calls=%async_computation.4 | async-start | bytes 2621440 | tf_op jit(solution)/shard_map/all_to_all | solution.py:347
  135.8 3.1 %collective-permute-start.12 = (bf16[8,40,512]{2,1,0:T(8,128)(2,1)S(1)}, bf16[8,40,512]{2,1,0:T(8,128)(2,1)S(1)}, u32[]{:S(2)}, u32[]{:S(2)}) collective-permute-start(bf16[8,40,512]{2,1,0:T(8,128)(2,1)S(1)} %get-tuple-element.40), channel_id=1, source_target_pairs={{0,2},{2,4},{4,6},{6,0},{1,3},{3,5},{5,7},{7,1},{8,10},{10,12},{12... | collective-permute-start | bytes 983048 | tf_op jit(solution)/shard_map/ppermute | solution.py:286
  138.9 4.3 %collective-permute-start.11 = (bf16[8,40,512]{2,1,0:T(8,128)(2,1)S(1)}, bf16[8,40,512]{2,1,0:T(8,128)(2,1)S(1)}, u32[]{:S(2)}, u32[]{:S(2)}) collective-permute-start(bf16[8,40,512]{2,1,0:T(8,128)(2,1)S(1)} %get-tuple-element.41), channel_id=1, source_target_pairs={{0,4},{2,6},{4,0},{6,2},{1,5},{3,7},{5,1},{7,3},{8,12},{10,14},{12... | collective-permute-start | bytes 983048 | tf_op jit(solution)/shard_map/ppermute | solution.py:286
  143.2 3.1 %collective-permute-start.10 = (bf16[8,40,512]{2,1,0:T(8,128)(2,1)S(1)}, bf16[8,40,512]{2,1,0:T(8,128)(2,1)S(1)}, u32[]{:S(2)}, u32[]{:S(2)}) collective-permute-start(bf16[8,40,512]{2,1,0:T(8,128)(2,1)S(1)} %get-tuple-element.42), channel_id=1, source_target_pairs={{0,6},{2,0},{4,2},{6,4},{1,7},{3,1},{5,3},{7,5},{8,14},{10,8},{12,... | collective-permute-start | bytes 983048 | tf_op jit(solution)/shard_map/ppermute | solution.py:286
  146.3 6.5 %collective-permute-done.12 = bf16[8,40,512]{2,1,0:T(8,128)(2,1)S(1)} collective-permute-done((bf16[8,40,512]{2,1,0:T(8,128)(2,1)S(1)}, bf16[8,40,512]{2,1,0:T(8,128)(2,1)S(1)}, u32[]{:S(2)}, u32[]{:S(2)}) %collective-permute-start.12) | collective-permute-done | bytes 327712 | tf_op jit(solution)/shard_map/ppermute | solution.py:286
  152.8 13.3 %collective-permute-done.11 = bf16[8,40,512]{2,1,0:T(8,128)(2,1)S(1)} collective-permute-done((bf16[8,40,512]{2,1,0:T(8,128)(2,1)S(1)}, bf16[8,40,512]{2,1,0:T(8,128)(2,1)S(1)}, u32[]{:S(2)}, u32[]{:S(2)}) %collective-permute-start.11) | collective-permute-done | bytes 327712 | tf_op jit(solution)/shard_map/ppermute | solution.py:286
  166.1 2.2 collective-permute-done.10
  169.0 1.9 convolution_add_fusion
  171.3 11.5 %all_gather.7 = bf16[512,512]{1,0:T(8,128)(2,1)S(1)} all-gather(bf16[128,512]{1,0:T(8,128)(2,1)S(1)} %convolution_convert_fusion.3), channel_id=1, replica_groups=mesh['dp'=8,'z'=8,'x'=4,'c'=2] {'x'}, dimensions={0}, use_global_device_ids=true | all-gather | bytes 655360 | tf_op jit(solution)/shard_map/all_gather | solution.py:361
  182.8 4.5 %collective-permute-start.13 = (bf16[512,512]{1,0:T(8,128)(2,1)S(1)}, bf16[512,512]{1,0:T(8,128)(2,1)S(1)}, u32[]{:S(2)}, u32[]{:S(2)}) collective-permute-start(bf16[512,512]{1,0:T(8,128)(2,1)S(1)} %all_gather.7), channel_id=1, source_target_pairs={{0,1},{1,0},{2,3},{3,2},{4,5},{5,4},{6,7},{7,6},{8,9},{9,8},{10,11... | collective-permute-start | bytes 1572872 | tf_op jit(solution)/shard_map/ppermute | solution.py:27
  188.9 1.3 fusion.1
  190.1 11.5 %all-to-all-start.4 = ((bf16[64,8,512]{2,1,0:T(8,128)(2,1)}), bf16[64,8,512]{2,1,0:T(8,128)(2,1)S(1)}, u32[]{:S(2)}, u32[]{:S(2)}) async-start(bf16[64,8,512]{2,1,0:T(8,128)(2,1)} %fusion.1), calls=%async_computation.5 | async-start | bytes 1048576 | tf_op jit(solution)/shard_map/all_to_all | solution.py:369
  201.7 2.4 %collective-permute-start.16 = (bf16[128,1024]{1,0:T(8,128)(2,1)S(1)}, bf16[128,1024]{1,0:T(8,128)(2,1)S(1)}, u32[]{:S(2)}, u32[]{:S(2)}) collective-permute-start(bf16[128,1024]{1,0:T(8,128)(2,1)S(1)} %get-tuple-element.47), channel_id=1, source_target_pairs={{0,2},{2,4},{4,6},{6,0},{1,3},{3,5},{5,7},{7,1},{8,10},{10,12},{12... | collective-permute-start | bytes 786440 | tf_op jit(solution)/shard_map/ppermute | solution.py:286
  204.1 4.3 %collective-permute-start.15 = (bf16[128,1024]{1,0:T(8,128)(2,1)S(1)}, bf16[128,1024]{1,0:T(8,128)(2,1)S(1)}, u32[]{:S(2)}, u32[]{:S(2)}) collective-permute-start(bf16[128,1024]{1,0:T(8,128)(2,1)S(1)} %get-tuple-element.48), channel_id=1, source_target_pairs={{0,4},{2,6},{4,0},{6,2},{1,5},{3,7},{5,1},{7,3},{8,12},{10,14},{12... | collective-permute-start | bytes 786440 | tf_op jit(solution)/shard_map/ppermute | solution.py:286
  208.4 2.3 collective-permute-start.14
  210.7 7.8 %all-to-all-done.4 = bf16[64,8,512]{2,1,0:T(8,128)(2,1)S(1)} async-done(((bf16[64,8,512]{2,1,0:T(8,128)(2,1)}), bf16[64,8,512]{2,1,0:T(8,128)(2,1)S(1)}, u32[]{:S(2)}, u32[]{:S(2)}) %all-to-all-start.4) | async-done | bytes 524320 | tf_op jit(solution)/shard_map/all_to_all | solution.py:369
  219.2 1.0 collective-permute-done.14.refs_2_.refs_3_
  220.1 3.5 %shard_map.97 = bf16[128,4096]{1,0:T(8,128)(2,1)} custom-call(s32[1,1024]{1,0:T(1,128)S(1)} %fusion.63.to_ref, bf16[128,1024]{1,0:T(8,128)(2,1)S(1)} %get-tuple-element.38.refs_0_.refs_1_, bf16[128,1024]{1,0:T(8,128)(2,1)S(1)} %get-tuple-element.38.refs_0_.refs_1_, bf16[128,1024]{1,0:T(8,128)(2,1)S(1)} %collective-permute-done.14.refs_2_.refs_3_, ...), custom_call_target="tpu_custom_call" | custom-call | flops 8999999488 | bytes 28000000 | tf_op jit(solution)/shard_map/pallas_call | solution.py:82
  223.6 1.6 convert_element_type.67
  (62 shorter events, 6.0 us)
Async XLA Ops:
  7.2 60.9 %all-gather.2.cloned.1.call-start = ((), (), s32[]{:S(2)}) async-start(), calls=%async_computation.6 | async-start | bytes 1474560 | tf_op jit(solution)/shard_map/all_gather | solution.py:306
  7.3 11.4 %copy-start.5 = (s32[128,8]{0,1:T(8,128)S(1)}, s32[128,8]{0,1:T(8,128)}, u32[]{:S(2)}) copy-start(s32[128,8]{0,1:T(8,128)} %param.8) | copy-start | bytes 12292
  7.3 11.4 %copy-start.7 = (f32[128,8]{0,1:T(8,128)S(1)}, f32[128,8]{0,1:T(8,128)}, u32[]{:S(2)}) copy-start(f32[128,8]{0,1:T(8,128)} %param.9) | copy-start | bytes 12292
  7.3 11.9 %copy-start.4 = (bf16[128,512]{1,0:T(8,128)(2,1)S(1)}, bf16[128,512]{1,0:T(8,128)(2,1)}, u32[]{:S(2)}) copy-start(bf16[128,512]{1,0:T(8,128)(2,1)} %param.13) | copy-start | bytes 393220
  7.3 12.8 %copy-start.6 = (bf16[8,512]{1,0:T(8,128)(2,1)S(1)}, bf16[8,512]{1,0:T(8,128)(2,1)}, u32[]{:S(2)}) copy-start(bf16[8,512]{1,0:T(8,128)(2,1)} %param.12) | copy-start | bytes 24580
  9.9 22.0 %collective-permute-start = (bf16[4,128,512]{2,1,0:T(8,128)(2,1)S(1)}, bf16[4,128,512]{2,1,0:T(8,128)(2,1)S(1)}, u32[]{:S(2)}, u32[]{:S(2)}) collective-permute-start(bf16[4,128,512]{2,1,0:T(8,128)(2,1)S(1)} %get-tuple-element.23), channel_id=1, source_target_pairs={{0,1},{1,0},{2,3},{3,2},{4,5},{5,4},{6,7},{7,6},{8,9},{9,8},{10,11... | collective-permute-start | bytes 1572872 | tf_op jit(solution)/shard_map/ppermute | solution.py:27
  20.9 28.4 %all-to-all-start = ((bf16[64,8,512]{2,1,0:T(8,128)(2,1)}), bf16[64,8,512]{2,1,0:T(8,128)(2,1)S(1)}, u32[]{:S(2)}, u32[]{:S(2)}) async-start(bf16[64,8,512]{2,1,0:T(8,128)(2,1)} %broadcast_in_dim.16), calls=%async_computation | async-start | bytes 1048576 | tf_op jit(solution)/shard_map/all_to_all | solution.py:299
  32.0 10.8 %collective-permute-start.1 = (bf16[2,128,512]{2,1,0:T(8,128)(2,1)S(1)}, bf16[2,128,512]{2,1,0:T(8,128)(2,1)S(1)}, u32[]{:S(2)}, u32[]{:S(2)}) collective-permute-start(bf16[2,128,512]{2,1,0:T(8,128)(2,1)S(1)} %get-tuple-element.58), channel_id=1, source_target_pairs={{0,2},{2,4},{4,6},{6,0},{1,3},{3,5},{5,7},{7,1},{8,10},{10,12},{12... | collective-permute-start | bytes 786440 | tf_op jit(solution)/shard_map/ppermute | solution.py:286
  35.2 9.3 %collective-permute-start.3 = (bf16[2,128,512]{2,1,0:T(8,128)(2,1)S(1)}, bf16[2,128,512]{2,1,0:T(8,128)(2,1)S(1)}, u32[]{:S(2)}, u32[]{:S(2)}) collective-permute-start(bf16[2,128,512]{2,1,0:T(8,128)(2,1)S(1)} %get-tuple-element.59), channel_id=1, source_target_pairs={{0,6},{2,0},{4,2},{6,4},{1,7},{3,1},{5,3},{7,5},{8,14},{10,8},{12,... | collective-permute-start | bytes 786440 | tf_op jit(solution)/shard_map/ppermute | solution.py:286
  38.6 10.4 %collective-permute-start.2 = (bf16[2,128,512]{2,1,0:T(8,128)(2,1)S(1)}, bf16[2,128,512]{2,1,0:T(8,128)(2,1)S(1)}, u32[]{:S(2)}, u32[]{:S(2)}) collective-permute-start(bf16[2,128,512]{2,1,0:T(8,128)(2,1)S(1)} %get-tuple-element.60), channel_id=1, source_target_pairs={{0,4},{2,6},{4,0},{6,2},{1,5},{3,7},{5,1},{7,3},{8,12},{10,14},{12... | collective-permute-start | bytes 786440 | tf_op jit(solution)/shard_map/ppermute | solution.py:286
  51.0 21.8 %all-to-all-start.1 = ((bf16[8,128,512]{2,1,0:T(8,128)(2,1)}), bf16[8,128,512]{2,1,0:T(8,128)(2,1)S(1)}, u32[]{:S(2)}, u32[]{:S(2)}) async-start(bf16[8,128,512]{2,1,0:T(8,128)(2,1)} %bitcast.101), calls=%async_computation.1 | async-start | bytes 2097152 | tf_op jit(solution)/shard_map/all_to_all | solution.py:321
  57.7 8.2 %collective-permute-start.4 = (bf16[512,512]{1,0:T(8,128)(2,1)S(1)}, bf16[512,512]{1,0:T(8,128)(2,1)}, u32[]{:S(2)}, u32[]{:S(2)}) collective-permute-start(bf16[512,512]{1,0:T(8,128)(2,1)S(1)} %bitcast.94), channel_id=1, source_target_pairs={{0,1},{1,0},{2,3},{3,2},{4,5},{5,4},{6,7},{7,6},{8,9},{9,8},{10,11... | collective-permute-start | bytes 1572872 | tf_op jit(solution)/shard_map/ppermute | solution.py:27
  59.7 15.0 %collective-permute-start.5 = (bf16[512,1024]{1,0:T(8,128)(2,1)}, bf16[512,1024]{1,0:T(8,128)(2,1)}, u32[]{:S(2)}, u32[]{:S(2)}) collective-permute-start(bf16[512,1024]{1,0:T(8,128)(2,1)} %bitcast.112), channel_id=1, source_target_pairs={{0,1},{1,0},{2,3},{3,2},{4,5},{5,4},{6,7},{7,6},{8,9},{9,8},{10,11... | collective-permute-start | bytes 3145736 | tf_op jit(solution)/shard_map/ppermute | solution.py:27
  62.9 11.7 %collective-permute-start.6 = (bf16[512,512]{1,0:T(8,128)(2,1)}, bf16[512,512]{1,0:T(8,128)(2,1)}, u32[]{:S(2)}, u32[]{:S(2)}) collective-permute-start(bf16[512,512]{1,0:T(8,128)(2,1)} %bitcast.114), channel_id=1, source_target_pairs={{0,1},{1,0},{2,3},{3,2},{4,5},{5,4},{6,7},{7,6},{8,9},{9,8},{10,11... | collective-permute-start | bytes 1572872 | tf_op jit(solution)/shard_map/ppermute | solution.py:27
  74.6 44.4 %all-to-all-start.2 = ((bf16[32,40,512]{2,1,0:T(8,128)(2,1)}), bf16[32,40,512]{2,1,0:T(8,128)(2,1)S(1)}, u32[]{:S(2)}, u32[]{:S(2)}) async-start(bf16[32,40,512]{2,1,0:T(8,128)(2,1)} %bitcast.91), calls=%async_computation.2 | async-start | bytes 2621440 | tf_op jit(solution)/shard_map/all_to_all | solution.py:341
  84.2 20.3 %collective-permute-start.7 = (bf16[8,40,512]{2,1,0:T(8,128)(2,1)S(1)}, bf16[8,40,512]{2,1,0:T(8,128)(2,1)S(1)}, u32[]{:S(2)}, u32[]{:S(2)}) collective-permute-start(bf16[8,40,512]{2,1,0:T(8,128)(2,1)S(1)} %get-tuple-element.25), channel_id=1, source_target_pairs={{0,2},{2,4},{4,6},{6,0},{1,3},{3,5},{5,7},{7,1},{8,10},{10,12},{12... | collective-permute-start | bytes 983048 | tf_op jit(solution)/shard_map/ppermute | solution.py:286
  87.3 28.7 %collective-permute-start.8 = (bf16[8,40,512]{2,1,0:T(8,128)(2,1)S(1)}, bf16[8,40,512]{2,1,0:T(8,128)(2,1)S(1)}, u32[]{:S(2)}, u32[]{:S(2)}) collective-permute-start(bf16[8,40,512]{2,1,0:T(8,128)(2,1)S(1)} %get-tuple-element.26), channel_id=1, source_target_pairs={{0,4},{2,6},{4,0},{6,2},{1,5},{3,7},{5,1},{7,3},{8,12},{10,14},{12... | collective-permute-start | bytes 983048 | tf_op jit(solution)/shard_map/ppermute | solution.py:286
  91.6 25.9 %collective-permute-start.9 = (bf16[8,40,512]{2,1,0:T(8,128)(2,1)S(1)}, bf16[8,40,512]{2,1,0:T(8,128)(2,1)S(1)}, u32[]{:S(2)}, u32[]{:S(2)}) collective-permute-start(bf16[8,40,512]{2,1,0:T(8,128)(2,1)S(1)} %get-tuple-element.27), channel_id=1, source_target_pairs={{0,6},{2,0},{4,2},{6,4},{1,7},{3,1},{5,3},{7,5},{8,14},{10,8},{12,... | collective-permute-start | bytes 983048 | tf_op jit(solution)/shard_map/ppermute | solution.py:286
  128.5 7.2 %copy-start.2 = (bf16[16,80,512]{2,1,0:T(8,128)(2,1)S(1)}, bf16[16,80,512]{2,1,0:T(8,128)(2,1)}, u32[]{:S(2)}) copy-start(bf16[16,80,512]{2,1,0:T(8,128)(2,1)} %get-tuple-element.32) | copy-start | bytes 3932164
  128.5 42.4 %all-to-all-start.3 = ((bf16[32,40,512]{2,1,0:T(8,128)(2,1)}), bf16[32,40,512]{2,1,0:T(8,128)(2,1)S(1)}, u32[]{:S(2)}, u32[]{:S(2)}) async-start(bf16[32,40,512]{2,1,0:T(8,128)(2,1)} %bitcast.97), calls=%async_computation.4 | async-start | bytes 2621440 | tf_op jit(solution)/shard_map/all_to_all | solution.py:347
  135.6 88.0 %reduce-scatter.2.cloned.1.call-start = ((), (), s32[]{:S(2)}) async-start(), calls=%async_computation.7 | async-start | bytes 2359296 | tf_op jit(solution)/shard_map/reduce_scatter | solution.py:356
  135.8 17.0 %collective-permute-start.12 = (bf16[8,40,512]{2,1,0:T(8,128)(2,1)S(1)}, bf16[8,40,512]{2,1,0:T(8,128)(2,1)S(1)}, u32[]{:S(2)}, u32[]{:S(2)}) collective-permute-start(bf16[8,40,512]{2,1,0:T(8,128)(2,1)S(1)} %get-tuple-element.40), channel_id=1, source_target_pairs={{0,2},{2,4},{4,6},{6,0},{1,3},{3,5},{5,7},{7,1},{8,10},{10,12},{12... | collective-permute-start | bytes 983048 | tf_op jit(solution)/shard_map/ppermute | solution.py:286
  138.9 27.1 %collective-permute-start.11 = (bf16[8,40,512]{2,1,0:T(8,128)(2,1)S(1)}, bf16[8,40,512]{2,1,0:T(8,128)(2,1)S(1)}, u32[]{:S(2)}, u32[]{:S(2)}) collective-permute-start(bf16[8,40,512]{2,1,0:T(8,128)(2,1)S(1)} %get-tuple-element.41), channel_id=1, source_target_pairs={{0,4},{2,6},{4,0},{6,2},{1,5},{3,7},{5,1},{7,3},{8,12},{10,14},{12... | collective-permute-start | bytes 983048 | tf_op jit(solution)/shard_map/ppermute | solution.py:286
  143.2 25.0 %collective-permute-start.10 = (bf16[8,40,512]{2,1,0:T(8,128)(2,1)S(1)}, bf16[8,40,512]{2,1,0:T(8,128)(2,1)S(1)}, u32[]{:S(2)}, u32[]{:S(2)}) collective-permute-start(bf16[8,40,512]{2,1,0:T(8,128)(2,1)S(1)} %get-tuple-element.42), channel_id=1, source_target_pairs={{0,6},{2,0},{4,2},{6,4},{1,7},{3,1},{5,3},{7,5},{8,14},{10,8},{12,... | collective-permute-start | bytes 983048 | tf_op jit(solution)/shard_map/ppermute | solution.py:286
  170.9 16.4 %copy-start.1 = (bf16[4,1,128,512]{3,2,1,0:T(8,128)(2,1)S(1)}, bf16[4,1,128,512]{3,2,1,0:T(8,128)(2,1)}, u32[]{:S(2)}) copy-start(bf16[4,1,128,512]{3,2,1,0:T(8,128)(2,1)} %get-tuple-element.52) | copy-start | bytes 1572868
  171.3 16.5 %copy-start.3 = (bf16[1024,512]{1,0:T(8,128)(2,1)S(1)}, bf16[1024,512]{1,0:T(8,128)(2,1)}, u32[]{:S(2)}) copy-start(bf16[1024,512]{1,0:T(8,128)(2,1)} %pad_maximum_fusion.5) | copy-start | bytes 3145732
  182.8 6.0 %collective-permute-start.13 = (bf16[512,512]{1,0:T(8,128)(2,1)S(1)}, bf16[512,512]{1,0:T(8,128)(2,1)S(1)}, u32[]{:S(2)}, u32[]{:S(2)}) collective-permute-start(bf16[512,512]{1,0:T(8,128)(2,1)S(1)} %all_gather.7), channel_id=1, source_target_pairs={{0,1},{1,0},{2,3},{3,2},{4,5},{5,4},{6,7},{7,6},{8,9},{9,8},{10,11... | collective-permute-start | bytes 1572872 | tf_op jit(solution)/shard_map/ppermute | solution.py:27
  187.8 1.0 copy-start
  190.1 28.4 %all-to-all-start.4 = ((bf16[64,8,512]{2,1,0:T(8,128)(2,1)}), bf16[64,8,512]{2,1,0:T(8,128)(2,1)S(1)}, u32[]{:S(2)}, u32[]{:S(2)}) async-start(bf16[64,8,512]{2,1,0:T(8,128)(2,1)} %fusion.1), calls=%async_computation.5 | async-start | bytes 1048576 | tf_op jit(solution)/shard_map/all_to_all | solution.py:369
  201.7 17.5 %collective-permute-start.16 = (bf16[128,1024]{1,0:T(8,128)(2,1)S(1)}, bf16[128,1024]{1,0:T(8,128)(2,1)S(1)}, u32[]{:S(2)}, u32[]{:S(2)}) collective-permute-start(bf16[128,1024]{1,0:T(8,128)(2,1)S(1)} %get-tuple-element.47), channel_id=1, source_target_pairs={{0,2},{2,4},{4,6},{6,0},{1,3},{3,5},{5,7},{7,1},{8,10},{10,12},{12... | collective-permute-start | bytes 786440 | tf_op jit(solution)/shard_map/ppermute | solution.py:286
  204.1 15.0 %collective-permute-start.15 = (bf16[128,1024]{1,0:T(8,128)(2,1)S(1)}, bf16[128,1024]{1,0:T(8,128)(2,1)S(1)}, u32[]{:S(2)}, u32[]{:S(2)}) collective-permute-start(bf16[128,1024]{1,0:T(8,128)(2,1)S(1)} %get-tuple-element.48), channel_id=1, source_target_pairs={{0,4},{2,6},{4,0},{6,2},{1,5},{3,7},{5,1},{7,3},{8,12},{10,14},{12... | collective-permute-start | bytes 786440 | tf_op jit(solution)/shard_map/ppermute | solution.py:286
  208.4 11.7 %collective-permute-start.14 = (bf16[128,1024]{1,0:T(8,128)(2,1)S(1)}, bf16[128,1024]{1,0:T(8,128)(2,1)S(1)}, u32[]{:S(2)}, u32[]{:S(2)}) collective-permute-start(bf16[128,1024]{1,0:T(8,128)(2,1)S(1)} %get-tuple-element.49), channel_id=1, source_target_pairs={{0,6},{2,0},{4,2},{6,4},{1,7},{3,1},{5,3},{7,5},{8,14},{10,8},{12,... | collective-permute-start | bytes 786440 | tf_op jit(solution)/shard_map/ppermute | solution.py:286
Sparse Core Ops, SparseCore 0:
  20.2 46.0 all-gather.1
  171.0 51.3 reduce-scatter.1

commit v8 on v7

--- a/solution.py
+++ b/solution.py
@@ -32,13 +32,6 @@
     y, z, x, c, i = a // 512, (a // 64) % 8, (a // 16) % 4, (a // 8) % 2, a % 8
     d, m = (x - at) % 4, (c - core) % 2
     return (d * 2 + m) * 128 + y * 64 + z * 8 + i
-
-
-def make_pick(to_ref, pick_ref):
-    @pl.when(pl.program_id(0) == 0)
-    def _():
-        at = lax.broadcasted_iota(jnp.int32, (1024, 1024), 0)
-        pick_ref[...] = jnp.where(to_ref[...] == at, 1.0, 0.0).astype(BF)
 
 
 def split_kernel(to_ref, tokens_ref, mine_ref, theirs_ref, pick_ref):
@@ -70,25 +63,31 @@
 
 
 def join_kernel(to_ref, *refs):
-    *parts, out_ref, pick_ref = refs
-    make_pick(to_ref, pick_ref)
-    out_ref[...] = mm(jnp.concatenate([ref[...] for ref in parts], axis=1), pick_ref[...]).astype(BF)
+    *slices, out_ref, pick_ref = refs
+    at = lax.broadcasted_iota(jnp.int32, (1024, 1024), 0)
+    pick_ref[...] = jnp.where(to_ref[...] == at, 1.0, 0.0).astype(BF)
+    rows = []
+    for p in range(4):
+        cols = [ref[:, k + 128 * p : k + 128 * (p + 1)] for ref in slices for k in (0, 512)]
+        rows.append(jnp.concatenate(cols, axis=1))
+    out = mm(jnp.concatenate(rows, axis=0), pick_ref[...]).astype(BF)
+    for p in range(4):
+        out_ref[:, 1024 * p : 1024 * (p + 1)] = out[128 * p : 128 * (p + 1)]
 
 
 def join_columns(to, *slices):
     rows = slices[0].shape[0]
-    near = pl.BlockSpec((rows, 128), lambda p: (0, p))
-    far = pl.BlockSpec((rows, 128), lambda p: (0, p + 4))
+    full = pl.BlockSpec((rows, 1024), lambda p: (0, 0))
     return pl.pallas_call(
         join_kernel,
-        grid=(4,),
-        in_specs=[pl.BlockSpec((1, 1024), lambda p: (0, 0))] + [near, far] * 4,
-        out_specs=pl.BlockSpec((rows, 1024), lambda p: (0, p)),
+        grid=(1,),
+        in_specs=[pl.BlockSpec((1, 1024), lambda p: (0, 0))] + [full] * 4,
+        out_specs=pl.BlockSpec((rows, 4096), lambda p: (0, 0)),
         out_shape=jax.ShapeDtypeStruct((rows, 4096), BF),
         scratch_shapes=[pltpu.VMEM((1024, 1024), BF)],
         compiler_params=pltpu.CompilerParams(vmem_limit_bytes=32 * 1024 * 1024),
         cost_estimate=pl.CostEstimate(flops=9_000_000_000, bytes_accessed=28_000_000, transcendentals=0),
-    )(to, *[x for pair in slices for x in (pair, pair)])
+    )(to, *slices)
 
 
 def cotangent_kernel(

time: 235 us -> 235 us (level)
  transfers between devices with their start and end apart: 24 -> 24, of which waited for: 12 -> 13; matrix products, arithmetic and copies ran while one was open for 8% -> 8% of each run, Pallas kernels for 4% -> 3%
where the time goes in v8:
time: 235 us; the launch traced here: 231 us
  starting transfers between devices  106 us (45%)
  waiting for transfers between devices  60.5 us (26%)
  Pallas kernels  19 us (8%)
  between operations  14.6 us (6%)
  blocking collectives  11.5 us (5%)
  matrix products  9.01 us (4%)
  other arithmetic  7.04 us (3%)
  local copies, waits for them, and re-layouts  3.66 us (2%)
    ppermute x12, waiting for transfers between devices, shift_x(): return lax.ppermute(x, 'x', [(i, (i + d) % 4) for i in range(4)])  52.4 us
    ppermute x12, starting transfers between devices, shift_x(): return lax.ppermute(x, 'x', [(i, (i + d) % 4) for i in range(4)])  40.1 us
    ppermute x5, starting transfers between devices, swap_core(): return lax.ppermute(x, 'c', [(0, 1), (1, 0)])  19.6 us
    all_to_all x1, starting transfers between devices, shards(): parts = lax.all_to_all(part, YZ, split_axis=0, concat_axis=0, tiled=True)  11.5 us
    all_gather x1, blocking collectives, shards(): line_grads = lax.all_gather(grad_latent, 'x', axis=0, tiled=True)  11.5 us
    all_to_all x1, starting transfers between devices, shards(): lax.all_to_all(jnp.broadcast_to(w_in[None], (64,) + w_in.shape), YZ, spli...  10.9 us
    all_to_all x1, starting transfers between devices, shards(): recv = lax.all_to_all(out_send, ZX, split_axis=0, concat_axis=0, tiled=True)  9.55 us
    pallas_call x1, Pallas kernels, expert_rows(): pl.pallas_call(expert_kernel, in_specs=[pl.BlockSpec(memory_space=pl.ANY)...  9.44 us
  transfers between devices with their start and end apart: 24, of which 13 were waited for; matrix products, arithmetic and copies ran while one was open for 8% of the time, Pallas kernels for 3%

profile of v8, /device:TPU:1, one launch (start us, length us, event | category | flops | bytes accessed | tf_op | source)
XLA Modules:
  0.0 230.9 jit_solution(4515711358713716288)
XLA Ops:
  7.3 2.6 %shard_map.95 = (bf16[4,128,512]{2,1,0:T(8,128)(2,1)S(1)}, bf16[4,128,512]{2,1,0:T(8,128)(2,1)S(1)}) custom-call(s32[1,1024]{1,0:T(1,128)S(1)} %fusion.63.to_ref, bf16[128,4096]{1,0:T(8,128)(2,1)} %tokens_ref.1), custom_call_target="tpu_custom_call" | custom-call | flops 1100000000 | bytes 2100000 | tf_op jit(solution)/shard_map/pallas_call | solution.py:53
  9.9 8.8 %collective-permute-start = (bf16[4,128,512]{2,1,0:T(8,128)(2,1)S(1)}, bf16[4,128,512]{2,1,0:T(8,128)(2,1)S(1)}, u32[]{:S(2)}, u32[]{:S(2)}) collective-permute-start(bf16[4,128,512]{2,1,0:T(8,128)(2,1)S(1)} %get-tuple-element.23), channel_id=1, source_target_pairs={{0,1},{1,0},{2,3},{3,2},{4,5},{5,4},{6,7},{7,6},{8,9},{9,8},{10,11... | collective-permute-start | bytes 1572872 | tf_op jit(solution)/shard_map/ppermute | solution.py:27
  19.2 0.8 concatenate.6
  20.1 0.8 broadcast_in_dim.16
  20.9 10.9 %all-to-all-start = ((bf16[64,8,512]{2,1,0:T(8,128)(2,1)}), bf16[64,8,512]{2,1,0:T(8,128)(2,1)S(1)}, u32[]{:S(2)}, u32[]{:S(2)}) async-start(bf16[64,8,512]{2,1,0:T(8,128)(2,1)} %broadcast_in_dim.16), calls=%async_computation | async-start | bytes 1048576 | tf_op jit(solution)/shard_map/all_to_all | solution.py:298
  32.0 3.1 %collective-permute-start.1 = (bf16[2,128,512]{2,1,0:T(8,128)(2,1)S(1)}, bf16[2,128,512]{2,1,0:T(8,128)(2,1)S(1)}, u32[]{:S(2)}, u32[]{:S(2)}) collective-permute-start(bf16[2,128,512]{2,1,0:T(8,128)(2,1)S(1)} %get-tuple-element.58), channel_id=1, source_target_pairs={{0,2},{2,4},{4,6},{6,0},{1,3},{3,5},{5,7},{7,1},{8,10},{10,12},{12... | collective-permute-start | bytes 786440 | tf_op jit(solution)/shard_map/ppermute | solution.py:285
  35.2 3.4 %collective-permute-start.3 = (bf16[2,128,512]{2,1,0:T(8,128)(2,1)S(1)}, bf16[2,128,512]{2,1,0:T(8,128)(2,1)S(1)}, u32[]{:S(2)}, u32[]{:S(2)}) collective-permute-start(bf16[2,128,512]{2,1,0:T(8,128)(2,1)S(1)} %get-tuple-element.59), channel_id=1, source_target_pairs={{0,6},{2,0},{4,2},{6,4},{1,7},{3,1},{5,3},{7,5},{8,14},{10,8},{12,... | collective-permute-start | bytes 786440 | tf_op jit(solution)/shard_map/ppermute | solution.py:285
  38.6 3.4 %collective-permute-start.2 = (bf16[2,128,512]{2,1,0:T(8,128)(2,1)S(1)}, bf16[2,128,512]{2,1,0:T(8,128)(2,1)S(1)}, u32[]{:S(2)}, u32[]{:S(2)}) collective-permute-start(bf16[2,128,512]{2,1,0:T(8,128)(2,1)S(1)} %get-tuple-element.60), channel_id=1, source_target_pairs={{0,4},{2,6},{4,0},{6,2},{1,5},{3,7},{5,1},{7,3},{8,12},{10,14},{12... | collective-permute-start | bytes 786440 | tf_op jit(solution)/shard_map/ppermute | solution.py:285
  42.1 0.8 collective-permute-done.1
  42.9 1.6 collective-permute-done.3
  44.5 4.5 %collective-permute-done.2 = bf16[2,128,512]{2,1,0:T(8,128)(2,1)S(1)} collective-permute-done((bf16[2,128,512]{2,1,0:T(8,128)(2,1)S(1)}, bf16[2,128,512]{2,1,0:T(8,128)(2,1)S(1)}, u32[]{:S(2)}, u32[]{:S(2)}) %collective-permute-start.2) | collective-permute-done | bytes 262176 | tf_op jit(solution)/shard_map/ppermute | solution.py:285
  49.3 1.7 convolution_convert_fusion.2
  51.0 6.7 %all-to-all-start.1 = ((bf16[8,128,512]{2,1,0:T(8,128)(2,1)}), bf16[8,128,512]{2,1,0:T(8,128)(2,1)S(1)}, u32[]{:S(2)}, u32[]{:S(2)}) async-start(bf16[8,128,512]{2,1,0:T(8,128)(2,1)} %bitcast.101), calls=%async_computation.1 | async-start | bytes 2097152 | tf_op jit(solution)/shard_map/all_to_all | solution.py:320
  57.7 1.9 collective-permute-start.4
  59.7 2.4 %collective-permute-start.5 = (bf16[512,1024]{1,0:T(8,128)(2,1)}, bf16[512,1024]{1,0:T(8,128)(2,1)}, u32[]{:S(2)}, u32[]{:S(2)}) collective-permute-start(bf16[512,1024]{1,0:T(8,128)(2,1)} %bitcast.112), channel_id=1, source_target_pairs={{0,1},{1,0},{2,3},{3,2},{4,5},{5,4},{6,7},{7,6},{8,9},{9,8},{10,11... | collective-permute-start | bytes 3145736 | tf_op jit(solution)/shard_map/ppermute | solution.py:27
  62.9 1.9 collective-permute-start.6
  64.8 1.1 constant_dynamic-slice_fusion.1
  66.0 2.1 pad_maximum_fusion.5
  68.0 4.8 %shard_map.94 = (bf16[8,40,512]{2,1,0:T(8,128)(2,1)S(1)}, bf16[8,40,512]{2,1,0:T(8,128)(2,1)S(1)}, bf16[8,40,512]{2,1,0:T(8,128)(2,1)S(1)}, bf16[8,40,512]{2,1,0...) custom-call(s32[160,1]{1,0:T(8,128)S(1)} %get-tuple-element.68.expert_ref, ...), custom_call_target="tpu_custom_call" | custom-call | flops 1000000000 | bytes 3000000 | tf_op jit(solution)/shard_map/pallas_call | solution.py:135
  73.0 1.6 convolution_convert_fusion
  74.6 9.6 %all-to-all-start.2 = ((bf16[32,40,512]{2,1,0:T(8,128)(2,1)}), bf16[32,40,512]{2,1,0:T(8,128)(2,1)S(1)}, u32[]{:S(2)}, u32[]{:S(2)}) async-start(bf16[32,40,512]{2,1,0:T(8,128)(2,1)} %bitcast.91), calls=%async_computation.2 | async-start | bytes 2621440 | tf_op jit(solution)/shard_map/all_to_all | solution.py:340
  84.2 3.1 %collective-permute-start.7 = (bf16[8,40,512]{2,1,0:T(8,128)(2,1)S(1)}, bf16[8,40,512]{2,1,0:T(8,128)(2,1)S(1)}, u32[]{:S(2)}, u32[]{:S(2)}) collective-permute-start(bf16[8,40,512]{2,1,0:T(8,128)(2,1)S(1)} %get-tuple-element.25), channel_id=1, source_target_pairs={{0,2},{2,4},{4,6},{6,0},{1,3},{3,5},{5,7},{7,1},{8,10},{10,12},{12... | collective-permute-start | bytes 983048 | tf_op jit(solution)/shard_map/ppermute | solution.py:285
  87.3 4.3 %collective-permute-start.8 = (bf16[8,40,512]{2,1,0:T(8,128)(2,1)S(1)}, bf16[8,40,512]{2,1,0:T(8,128)(2,1)S(1)}, u32[]{:S(2)}, u32[]{:S(2)}) collective-permute-start(bf16[8,40,512]{2,1,0:T(8,128)(2,1)S(1)} %get-tuple-element.26), channel_id=1, source_target_pairs={{0,4},{2,6},{4,0},{6,2},{1,5},{3,7},{5,1},{7,3},{8,12},{10,14},{12... | collective-permute-start | bytes 983048 | tf_op jit(solution)/shard_map/ppermute | solution.py:285
  91.6 3.3 %collective-permute-start.9 = (bf16[8,40,512]{2,1,0:T(8,128)(2,1)S(1)}, bf16[8,40,512]{2,1,0:T(8,128)(2,1)S(1)}, u32[]{:S(2)}, u32[]{:S(2)}) collective-permute-start(bf16[8,40,512]{2,1,0:T(8,128)(2,1)S(1)} %get-tuple-element.27), channel_id=1, source_target_pairs={{0,6},{2,0},{4,2},{6,4},{1,7},{3,1},{5,3},{7,5},{8,14},{10,8},{12,... | collective-permute-start | bytes 983048 | tf_op jit(solution)/shard_map/ppermute | solution.py:285
  94.9 9.6 %collective-permute-done.7 = bf16[8,40,512]{2,1,0:T(8,128)(2,1)S(1)} collective-permute-done((bf16[8,40,512]{2,1,0:T(8,128)(2,1)S(1)}, bf16[8,40,512]{2,1,0:T(8,128)(2,1)S(1)}, u32[]{:S(2)}, u32[]{:S(2)}) %collective-permute-start.7) | collective-permute-done | bytes 327712 | tf_op jit(solution)/shard_map/ppermute | solution.py:285
  104.5 11.5 %collective-permute-done.8 = bf16[8,40,512]{2,1,0:T(8,128)(2,1)S(1)} collective-permute-done((bf16[8,40,512]{2,1,0:T(8,128)(2,1)S(1)}, bf16[8,40,512]{2,1,0:T(8,128)(2,1)S(1)}, u32[]{:S(2)}, u32[]{:S(2)}) %collective-permute-start.8) | collective-permute-done | bytes 327712 | tf_op jit(solution)/shard_map/ppermute | solution.py:285
  116.0 1.5 collective-permute-done.9
  117.8 1.2 pad_maximum_fusion.1
  119.0 9.4 %shard_map.96 = (bf16[16,80,512]{2,1,0:T(8,128)(2,1)}, bf16[16,80,512]{2,1,0:T(8,128)(2,1)}) custom-call(bf16[16,80,512]{2,1,0:T(8,128)(2,1)S(1)} %bitcast.85, bf16[16,80,512]{2,1,0:T(8,128)(2,1)} %bitcast.98, bf16[512,1024]{1,0:T(8,128)(2,1)} %bitcast.113, bf16[512,512]{1,0:T(8,128)(2,1)} %bitcast.115, bf16[512,1024]{1,0:T(8,128)(2,1)} %collective-permute-done.5.up2, ...), custom_call_target="tpu_custom_call" | custom-call | flops 4800000000 | bytes 8500000 | tf_op jit(solution)/shard_map/pallas_call | solution.py:233
  128.5 7.1 %all-to-all-start.3 = ((bf16[32,40,512]{2,1,0:T(8,128)(2,1)}), bf16[32,40,512]{2,1,0:T(8,128)(2,1)S(1)}, u32[]{:S(2)}, u32[]{:S(2)}) async-start(bf16[32,40,512]{2,1,0:T(8,128)(2,1)} %bitcast.97), calls=%async_computation.4 | async-start | bytes 2621440 | tf_op jit(solution)/shard_map/all_to_all | solution.py:346
  135.8 3.1 %collective-permute-start.12 = (bf16[8,40,512]{2,1,0:T(8,128)(2,1)S(1)}, bf16[8,40,512]{2,1,0:T(8,128)(2,1)S(1)}, u32[]{:S(2)}, u32[]{:S(2)}) collective-permute-start(bf16[8,40,512]{2,1,0:T(8,128)(2,1)S(1)} %get-tuple-element.40), channel_id=1, source_target_pairs={{0,2},{2,4},{4,6},{6,0},{1,3},{3,5},{5,7},{7,1},{8,10},{10,12},{12... | collective-permute-start | bytes 983048 | tf_op jit(solution)/shard_map/ppermute | solution.py:285
  138.9 4.3 %collective-permute-start.11 = (bf16[8,40,512]{2,1,0:T(8,128)(2,1)S(1)}, bf16[8,40,512]{2,1,0:T(8,128)(2,1)S(1)}, u32[]{:S(2)}, u32[]{:S(2)}) collective-permute-start(bf16[8,40,512]{2,1,0:T(8,128)(2,1)S(1)} %get-tuple-element.41), channel_id=1, source_target_pairs={{0,4},{2,6},{4,0},{6,2},{1,5},{3,7},{5,1},{7,3},{8,12},{10,14},{12... | collective-permute-start | bytes 983048 | tf_op jit(solution)/shard_map/ppermute | solution.py:285
  143.2 3.1 %collective-permute-start.10 = (bf16[8,40,512]{2,1,0:T(8,128)(2,1)S(1)}, bf16[8,40,512]{2,1,0:T(8,128)(2,1)S(1)}, u32[]{:S(2)}, u32[]{:S(2)}) collective-permute-start(bf16[8,40,512]{2,1,0:T(8,128)(2,1)S(1)} %get-tuple-element.42), channel_id=1, source_target_pairs={{0,6},{2,0},{4,2},{6,4},{1,7},{3,1},{5,3},{7,5},{8,14},{10,8},{12,... | collective-permute-start | bytes 983048 | tf_op jit(solution)/shard_map/ppermute | solution.py:285
  146.3 6.5 %collective-permute-done.12 = bf16[8,40,512]{2,1,0:T(8,128)(2,1)S(1)} collective-permute-done((bf16[8,40,512]{2,1,0:T(8,128)(2,1)S(1)}, bf16[8,40,512]{2,1,0:T(8,128)(2,1)S(1)}, u32[]{:S(2)}, u32[]{:S(2)}) %collective-permute-start.12) | collective-permute-done | bytes 327712 | tf_op jit(solution)/shard_map/ppermute | solution.py:285
  152.8 13.3 %collective-permute-done.11 = bf16[8,40,512]{2,1,0:T(8,128)(2,1)S(1)} collective-permute-done((bf16[8,40,512]{2,1,0:T(8,128)(2,1)S(1)}, bf16[8,40,512]{2,1,0:T(8,128)(2,1)S(1)}, u32[]{:S(2)}, u32[]{:S(2)}) %collective-permute-start.11) | collective-permute-done | bytes 327712 | tf_op jit(solution)/shard_map/ppermute | solution.py:285
  166.1 2.2 collective-permute-done.10
  169.0 1.9 convolution_add_fusion
  171.3 11.5 %all_gather.7 = bf16[512,512]{1,0:T(8,128)(2,1)S(1)} all-gather(bf16[128,512]{1,0:T(8,128)(2,1)S(1)} %convolution_convert_fusion.3), channel_id=1, replica_groups=mesh['dp'=8,'z'=8,'x'=4,'c'=2] {'x'}, dimensions={0}, use_global_device_ids=true | all-gather | bytes 655360 | tf_op jit(solution)/shard_map/all_gather | solution.py:360
  182.8 4.5 %collective-permute-start.13 = (bf16[512,512]{1,0:T(8,128)(2,1)S(1)}, bf16[512,512]{1,0:T(8,128)(2,1)S(1)}, u32[]{:S(2)}, u32[]{:S(2)}) collective-permute-start(bf16[512,512]{1,0:T(8,128)(2,1)S(1)} %all_gather.7), channel_id=1, source_target_pairs={{0,1},{1,0},{2,3},{3,2},{4,5},{5,4},{6,7},{7,6},{8,9},{9,8},{10,11... | collective-permute-start | bytes 1572872 | tf_op jit(solution)/shard_map/ppermute | solution.py:27
  188.9 1.3 fusion.1
  190.1 11.5 %all-to-all-start.4 = ((bf16[64,8,512]{2,1,0:T(8,128)(2,1)}), bf16[64,8,512]{2,1,0:T(8,128)(2,1)S(1)}, u32[]{:S(2)}, u32[]{:S(2)}) async-start(bf16[64,8,512]{2,1,0:T(8,128)(2,1)} %fusion.1), calls=%async_computation.5 | async-start | bytes 1048576 | tf_op jit(solution)/shard_map/all_to_all | solution.py:368
  201.7 2.4 %collective-permute-start.16 = (bf16[128,1024]{1,0:T(8,128)(2,1)S(1)}, bf16[128,1024]{1,0:T(8,128)(2,1)S(1)}, u32[]{:S(2)}, u32[]{:S(2)}) collective-permute-start(bf16[128,1024]{1,0:T(8,128)(2,1)S(1)} %get-tuple-element.47), channel_id=1, source_target_pairs={{0,2},{2,4},{4,6},{6,0},{1,3},{3,5},{5,7},{7,1},{8,10},{10,12},{12... | collective-permute-start | bytes 786440 | tf_op jit(solution)/shard_map/ppermute | solution.py:285
  204.1 4.3 %collective-permute-start.15 = (bf16[128,1024]{1,0:T(8,128)(2,1)S(1)}, bf16[128,1024]{1,0:T(8,128)(2,1)S(1)}, u32[]{:S(2)}, u32[]{:S(2)}) collective-permute-start(bf16[128,1024]{1,0:T(8,128)(2,1)S(1)} %get-tuple-element.48), channel_id=1, source_target_pairs={{0,4},{2,6},{4,0},{6,2},{1,5},{3,7},{5,1},{7,3},{8,12},{10,14},{12... | collective-permute-start | bytes 786440 | tf_op jit(solution)/shard_map/ppermute | solution.py:285
  208.4 2.3 collective-permute-start.14
  210.7 7.8 %all-to-all-done.4 = bf16[64,8,512]{2,1,0:T(8,128)(2,1)S(1)} async-done(((bf16[64,8,512]{2,1,0:T(8,128)(2,1)}), bf16[64,8,512]{2,1,0:T(8,128)(2,1)S(1)}, u32[]{:S(2)}, u32[]{:S(2)}) %all-to-all-start.4) | async-done | bytes 524320 | tf_op jit(solution)/shard_map/all_to_all | solution.py:368
  219.2 1.0 collective-permute-done.14.refs_1_
  220.1 2.2 shard_map.97
  222.4 1.6 convert_element_type.67
  (62 shorter events, 6.0 us)
Async XLA Ops:
  7.2 60.9 %all-gather.2.cloned.1.call-start = ((), (), s32[]{:S(2)}) async-start(), calls=%async_computation.6 | async-start | bytes 1474560 | tf_op jit(solution)/shard_map/all_gather | solution.py:305
  7.3 11.4 %copy-start.5 = (s32[128,8]{0,1:T(8,128)S(1)}, s32[128,8]{0,1:T(8,128)}, u32[]{:S(2)}) copy-start(s32[128,8]{0,1:T(8,128)} %param.8) | copy-start | bytes 12292
  7.3 11.4 %copy-start.7 = (f32[128,8]{0,1:T(8,128)S(1)}, f32[128,8]{0,1:T(8,128)}, u32[]{:S(2)}) copy-start(f32[128,8]{0,1:T(8,128)} %param.9) | copy-start | bytes 12292
  7.3 11.9 %copy-start.4 = (bf16[128,512]{1,0:T(8,128)(2,1)S(1)}, bf16[128,512]{1,0:T(8,128)(2,1)}, u32[]{:S(2)}) copy-start(bf16[128,512]{1,0:T(8,128)(2,1)} %param.13) | copy-start | bytes 393220
  7.3 12.8 %copy-start.6 = (bf16[8,512]{1,0:T(8,128)(2,1)S(1)}, bf16[8,512]{1,0:T(8,128)(2,1)}, u32[]{:S(2)}) copy-start(bf16[8,512]{1,0:T(8,128)(2,1)} %param.12) | copy-start | bytes 24580
  9.9 22.0 %collective-permute-start = (bf16[4,128,512]{2,1,0:T(8,128)(2,1)S(1)}, bf16[4,128,512]{2,1,0:T(8,128)(2,1)S(1)}, u32[]{:S(2)}, u32[]{:S(2)}) collective-permute-start(bf16[4,128,512]{2,1,0:T(8,128)(2,1)S(1)} %get-tuple-element.23), channel_id=1, source_target_pairs={{0,1},{1,0},{2,3},{3,2},{4,5},{5,4},{6,7},{7,6},{8,9},{9,8},{10,11... | collective-permute-start | bytes 1572872 | tf_op jit(solution)/shard_map/ppermute | solution.py:27
  20.9 28.4 %all-to-all-start = ((bf16[64,8,512]{2,1,0:T(8,128)(2,1)}), bf16[64,8,512]{2,1,0:T(8,128)(2,1)S(1)}, u32[]{:S(2)}, u32[]{:S(2)}) async-start(bf16[64,8,512]{2,1,0:T(8,128)(2,1)} %broadcast_in_dim.16), calls=%async_computation | async-start | bytes 1048576 | tf_op jit(solution)/shard_map/all_to_all | solution.py:298
  32.0 10.8 %collective-permute-start.1 = (bf16[2,128,512]{2,1,0:T(8,128)(2,1)S(1)}, bf16[2,128,512]{2,1,0:T(8,128)(2,1)S(1)}, u32[]{:S(2)}, u32[]{:S(2)}) collective-permute-start(bf16[2,128,512]{2,1,0:T(8,128)(2,1)S(1)} %get-tuple-element.58), channel_id=1, source_target_pairs={{0,2},{2,4},{4,6},{6,0},{1,3},{3,5},{5,7},{7,1},{8,10},{10,12},{12... | collective-permute-start | bytes 786440 | tf_op jit(solution)/shard_map/ppermute | solution.py:285
  35.2 9.3 %collective-permute-start.3 = (bf16[2,128,512]{2,1,0:T(8,128)(2,1)S(1)}, bf16[2,128,512]{2,1,0:T(8,128)(2,1)S(1)}, u32[]{:S(2)}, u32[]{:S(2)}) collective-permute-start(bf16[2,128,512]{2,1,0:T(8,128)(2,1)S(1)} %get-tuple-element.59), channel_id=1, source_target_pairs={{0,6},{2,0},{4,2},{6,4},{1,7},{3,1},{5,3},{7,5},{8,14},{10,8},{12,... | collective-permute-start | bytes 786440 | tf_op jit(solution)/shard_map/ppermute | solution.py:285
  38.6 10.4 %collective-permute-start.2 = (bf16[2,128,512]{2,1,0:T(8,128)(2,1)S(1)}, bf16[2,128,512]{2,1,0:T(8,128)(2,1)S(1)}, u32[]{:S(2)}, u32[]{:S(2)}) collective-permute-start(bf16[2,128,512]{2,1,0:T(8,128)(2,1)S(1)} %get-tuple-element.60), channel_id=1, source_target_pairs={{0,4},{2,6},{4,0},{6,2},{1,5},{3,7},{5,1},{7,3},{8,12},{10,14},{12... | collective-permute-start | bytes 786440 | tf_op jit(solution)/shard_map/ppermute | solution.py:285
  51.0 21.8 %all-to-all-start.1 = ((bf16[8,128,512]{2,1,0:T(8,128)(2,1)}), bf16[8,128,512]{2,1,0:T(8,128)(2,1)S(1)}, u32[]{:S(2)}, u32[]{:S(2)}) async-start(bf16[8,128,512]{2,1,0:T(8,128)(2,1)} %bitcast.101), calls=%async_computation.1 | async-start | bytes 2097152 | tf_op jit(solution)/shard_map/all_to_all | solution.py:320
  57.7 8.2 %collective-permute-start.4 = (bf16[512,512]{1,0:T(8,128)(2,1)S(1)}, bf16[512,512]{1,0:T(8,128)(2,1)}, u32[]{:S(2)}, u32[]{:S(2)}) collective-permute-start(bf16[512,512]{1,0:T(8,128)(2,1)S(1)} %bitcast.94), channel_id=1, source_target_pairs={{0,1},{1,0},{2,3},{3,2},{4,5},{5,4},{6,7},{7,6},{8,9},{9,8},{10,11... | collective-permute-start | bytes 1572872 | tf_op jit(solution)/shard_map/ppermute | solution.py:27
  59.7 15.0 %collective-permute-start.5 = (bf16[512,1024]{1,0:T(8,128)(2,1)}, bf16[512,1024]{1,0:T(8,128)(2,1)}, u32[]{:S(2)}, u32[]{:S(2)}) collective-permute-start(bf16[512,1024]{1,0:T(8,128)(2,1)} %bitcast.112), channel_id=1, source_target_pairs={{0,1},{1,0},{2,3},{3,2},{4,5},{5,4},{6,7},{7,6},{8,9},{9,8},{10,11... | collective-permute-start | bytes 3145736 | tf_op jit(solution)/shard_map/ppermute | solution.py:27
  62.9 11.7 %collective-permute-start.6 = (bf16[512,512]{1,0:T(8,128)(2,1)}, bf16[512,512]{1,0:T(8,128)(2,1)}, u32[]{:S(2)}, u32[]{:S(2)}) collective-permute-start(bf16[512,512]{1,0:T(8,128)(2,1)} %bitcast.114), channel_id=1, source_target_pairs={{0,1},{1,0},{2,3},{3,2},{4,5},{5,4},{6,7},{7,6},{8,9},{9,8},{10,11... | collective-permute-start | bytes 1572872 | tf_op jit(solution)/shard_map/ppermute | solution.py:27
  74.6 44.4 %all-to-all-start.2 = ((bf16[32,40,512]{2,1,0:T(8,128)(2,1)}), bf16[32,40,512]{2,1,0:T(8,128)(2,1)S(1)}, u32[]{:S(2)}, u32[]{:S(2)}) async-start(bf16[32,40,512]{2,1,0:T(8,128)(2,1)} %bitcast.91), calls=%async_computation.2 | async-start | bytes 2621440 | tf_op jit(solution)/shard_map/all_to_all | solution.py:340
  84.2 20.3 %collective-permute-start.7 = (bf16[8,40,512]{2,1,0:T(8,128)(2,1)S(1)}, bf16[8,40,512]{2,1,0:T(8,128)(2,1)S(1)}, u32[]{:S(2)}, u32[]{:S(2)}) collective-permute-start(bf16[8,40,512]{2,1,0:T(8,128)(2,1)S(1)} %get-tuple-element.25), channel_id=1, source_target_pairs={{0,2},{2,4},{4,6},{6,0},{1,3},{3,5},{5,7},{7,1},{8,10},{10,12},{12... | collective-permute-start | bytes 983048 | tf_op jit(solution)/shard_map/ppermute | solution.py:285
  87.3 28.7 %collective-permute-start.8 = (bf16[8,40,512]{2,1,0:T(8,128)(2,1)S(1)}, bf16[8,40,512]{2,1,0:T(8,128)(2,1)S(1)}, u32[]{:S(2)}, u32[]{:S(2)}) collective-permute-start(bf16[8,40,512]{2,1,0:T(8,128)(2,1)S(1)} %get-tuple-element.26), channel_id=1, source_target_pairs={{0,4},{2,6},{4,0},{6,2},{1,5},{3,7},{5,1},{7,3},{8,12},{10,14},{12... | collective-permute-start | bytes 983048 | tf_op jit(solution)/shard_map/ppermute | solution.py:285
  91.6 25.9 %collective-permute-start.9 = (bf16[8,40,512]{2,1,0:T(8,128)(2,1)S(1)}, bf16[8,40,512]{2,1,0:T(8,128)(2,1)S(1)}, u32[]{:S(2)}, u32[]{:S(2)}) collective-permute-start(bf16[8,40,512]{2,1,0:T(8,128)(2,1)S(1)} %get-tuple-element.27), channel_id=1, source_target_pairs={{0,6},{2,0},{4,2},{6,4},{1,7},{3,1},{5,3},{7,5},{8,14},{10,8},{12,... | collective-permute-start | bytes 983048 | tf_op jit(solution)/shard_map/ppermute | solution.py:285
  128.5 7.2 %copy-start.2 = (bf16[16,80,512]{2,1,0:T(8,128)(2,1)S(1)}, bf16[16,80,512]{2,1,0:T(8,128)(2,1)}, u32[]{:S(2)}) copy-start(bf16[16,80,512]{2,1,0:T(8,128)(2,1)} %get-tuple-element.32) | copy-start | bytes 3932164
  128.5 42.4 %all-to-all-start.3 = ((bf16[32,40,512]{2,1,0:T(8,128)(2,1)}), bf16[32,40,512]{2,1,0:T(8,128)(2,1)S(1)}, u32[]{:S(2)}, u32[]{:S(2)}) async-start(bf16[32,40,512]{2,1,0:T(8,128)(2,1)} %bitcast.97), calls=%async_computation.4 | async-start | bytes 2621440 | tf_op jit(solution)/shard_map/all_to_all | solution.py:346
  135.6 86.8 %reduce-scatter.2.cloned.1.call-start = ((), (), s32[]{:S(2)}) async-start(), calls=%async_computation.7 | async-start | bytes 2359296 | tf_op jit(solution)/shard_map/reduce_scatter | solution.py:355
  135.8 17.0 %collective-permute-start.12 = (bf16[8,40,512]{2,1,0:T(8,128)(2,1)S(1)}, bf16[8,40,512]{2,1,0:T(8,128)(2,1)S(1)}, u32[]{:S(2)}, u32[]{:S(2)}) collective-permute-start(bf16[8,40,512]{2,1,0:T(8,128)(2,1)S(1)} %get-tuple-element.40), channel_id=1, source_target_pairs={{0,2},{2,4},{4,6},{6,0},{1,3},{3,5},{5,7},{7,1},{8,10},{10,12},{12... | collective-permute-start | bytes 983048 | tf_op jit(solution)/shard_map/ppermute | solution.py:285
  138.9 27.1 %collective-permute-start.11 = (bf16[8,40,512]{2,1,0:T(8,128)(2,1)S(1)}, bf16[8,40,512]{2,1,0:T(8,128)(2,1)S(1)}, u32[]{:S(2)}, u32[]{:S(2)}) collective-permute-start(bf16[8,40,512]{2,1,0:T(8,128)(2,1)S(1)} %get-tuple-element.41), channel_id=1, source_target_pairs={{0,4},{2,6},{4,0},{6,2},{1,5},{3,7},{5,1},{7,3},{8,12},{10,14},{12... | collective-permute-start | bytes 983048 | tf_op jit(solution)/shard_map/ppermute | solution.py:285
  143.2 25.0 %collective-permute-start.10 = (bf16[8,40,512]{2,1,0:T(8,128)(2,1)S(1)}, bf16[8,40,512]{2,1,0:T(8,128)(2,1)S(1)}, u32[]{:S(2)}, u32[]{:S(2)}) collective-permute-start(bf16[8,40,512]{2,1,0:T(8,128)(2,1)S(1)} %get-tuple-element.42), channel_id=1, source_target_pairs={{0,6},{2,0},{4,2},{6,4},{1,7},{3,1},{5,3},{7,5},{8,14},{10,8},{12,... | collective-permute-start | bytes 983048 | tf_op jit(solution)/shard_map/ppermute | solution.py:285
  170.9 16.4 %copy-start.1 = (bf16[4,1,128,512]{3,2,1,0:T(8,128)(2,1)S(1)}, bf16[4,1,128,512]{3,2,1,0:T(8,128)(2,1)}, u32[]{:S(2)}) copy-start(bf16[4,1,128,512]{3,2,1,0:T(8,128)(2,1)} %get-tuple-element.52) | copy-start | bytes 1572868
  171.3 16.5 %copy-start.3 = (bf16[1024,512]{1,0:T(8,128)(2,1)S(1)}, bf16[1024,512]{1,0:T(8,128)(2,1)}, u32[]{:S(2)}) copy-start(bf16[1024,512]{1,0:T(8,128)(2,1)} %pad_maximum_fusion.5) | copy-start | bytes 3145732
  182.8 6.0 %collective-permute-start.13 = (bf16[512,512]{1,0:T(8,128)(2,1)S(1)}, bf16[512,512]{1,0:T(8,128)(2,1)S(1)}, u32[]{:S(2)}, u32[]{:S(2)}) collective-permute-start(bf16[512,512]{1,0:T(8,128)(2,1)S(1)} %all_gather.7), channel_id=1, source_target_pairs={{0,1},{1,0},{2,3},{3,2},{4,5},{5,4},{6,7},{7,6},{8,9},{9,8},{10,11... | collective-permute-start | bytes 1572872 | tf_op jit(solution)/shard_map/ppermute | solution.py:27
  187.8 1.0 copy-start
  190.1 28.4 %all-to-all-start.4 = ((bf16[64,8,512]{2,1,0:T(8,128)(2,1)}), bf16[64,8,512]{2,1,0:T(8,128)(2,1)S(1)}, u32[]{:S(2)}, u32[]{:S(2)}) async-start(bf16[64,8,512]{2,1,0:T(8,128)(2,1)} %fusion.1), calls=%async_computation.5 | async-start | bytes 1048576 | tf_op jit(solution)/shard_map/all_to_all | solution.py:368
  201.7 17.5 %collective-permute-start.16 = (bf16[128,1024]{1,0:T(8,128)(2,1)S(1)}, bf16[128,1024]{1,0:T(8,128)(2,1)S(1)}, u32[]{:S(2)}, u32[]{:S(2)}) collective-permute-start(bf16[128,1024]{1,0:T(8,128)(2,1)S(1)} %get-tuple-element.47), channel_id=1, source_target_pairs={{0,2},{2,4},{4,6},{6,0},{1,3},{3,5},{5,7},{7,1},{8,10},{10,12},{12... | collective-permute-start | bytes 786440 | tf_op jit(solution)/shard_map/ppermute | solution.py:285
  204.1 15.0 %collective-permute-start.15 = (bf16[128,1024]{1,0:T(8,128)(2,1)S(1)}, bf16[128,1024]{1,0:T(8,128)(2,1)S(1)}, u32[]{:S(2)}, u32[]{:S(2)}) collective-permute-start(bf16[128,1024]{1,0:T(8,128)(2,1)S(1)} %get-tuple-element.48), channel_id=1, source_target_pairs={{0,4},{2,6},{4,0},{6,2},{1,5},{3,7},{5,1},{7,3},{8,12},{10,14},{12... | collective-permute-start | bytes 786440 | tf_op jit(solution)/shard_map/ppermute | solution.py:285
  208.4 11.7 %collective-permute-start.14 = (bf16[128,1024]{1,0:T(8,128)(2,1)S(1)}, bf16[128,1024]{1,0:T(8,128)(2,1)S(1)}, u32[]{:S(2)}, u32[]{:S(2)}) collective-permute-start(bf16[128,1024]{1,0:T(8,128)(2,1)S(1)} %get-tuple-element.49), channel_id=1, source_target_pairs={{0,6},{2,0},{4,2},{6,4},{1,7},{3,1},{5,3},{7,5},{8,14},{10,8},{12,... | collective-permute-start | bytes 786440 | tf_op jit(solution)/shard_map/ppermute | solution.py:285
Sparse Core Ops, SparseCore 0:
  20.2 46.0 all-gather.1
  171.0 51.3 reduce-scatter.1
